TPU v7x, 1024 devices: a whole 8x8x8 slice. The times are simulated.
1024 devices in a mesh: dp: 8 (over z_hi, core), mx: 8 (over y), my: 16 (over x, z_lo).
Axes of the slice: x: 8, y: 8, z: 8 (z_hi: 4, z_lo: 2; z = z_hi * 2 + z_lo), core: 2. Of those that a mesh axis runs over, the one named last changes fastest.
Arguments:
- tokens: bfloat16 [1024, 6144], P('dp', 'my'), may hold values from -31 to 31
- ln_gain: float32 [6144], P('my'), may hold values from 0.5 to 1.5
- query_gain: float32 [128], replicated, may hold values from 0.5 to 1.5
- key_gain: float32 [128], replicated, may hold values from 0.5 to 1.5
- w_qkv: bfloat16 [3, 6144, 3072], P(None, 'my', 'mx'), may hold values from -0.078125 to 0.078125
- w_hidden: bfloat16 [6144, 12288], P('my', 'mx'), may hold values from -0.078125 to 0.078125
- w_attn_out: bfloat16 [3072, 6144], P('mx', 'my'), may hold values from -0.046875 to 0.046875
- w_mlp_out: bfloat16 [12288, 6144], P('mx', 'my'), may hold values from -0.046875 to 0.046875
- cotangent: bfloat16 [1024, 6144], P('dp', 'my'), may hold values from -6 to 6
Outputs:
- mixed: bfloat16 [1024, 6144], P(('dp', 'mx'), 'my')
- grad_tokens: bfloat16 [1024, 6144], P(('dp', 'mx'), 'my')
- grad_qkv: float32 [3, 16, 384, 3072], P(None, 'my', 'dp', 'mx')
- grad_hidden: float32 [16, 384, 12288], P('my', 'dp', 'mx')
- grad_attn_out: float32 [8, 384, 6144], P('mx', 'dp', 'my')
- grad_mlp_out: float32 [8, 1536, 6144], P('mx', 'dp', 'my')
All inputs are finite; a program needn't handle non-finite values.
Results may differ from a plain program's by a relative error of at most 0.04.
Values may be sent and summed in bfloat16 or wider, within the bound.
No kernel may reach another device: no remote copies, remote signals or barrier semaphores. Data moves between devices by JAX's collectives and lax.ppermute only.
A program may use at most 32 MiB of HBM per device.

v0:
```python
import jax
import jax.numpy as jnp
from jax import lax
from jax.sharding import PartitionSpec as P

PATCHES = 128


EPSILON = 1e-06


def dot_first(matrix_a, matrix_b):
    return lax.dot_general(
        matrix_a, matrix_b, (((0,), (0,)), ((), ())), preferred_element_type=jnp.float32
    )


def dot_last(matrix_a, matrix_b):
    return lax.dot_general(
        matrix_a, matrix_b, (((1,), (1,)), ((), ())), preferred_element_type=jnp.float32
    )


def rows_of(matrix_a, first_row, length):
    return lax.dynamic_slice_in_dim(matrix_a, first_row, length, 0)


def feature_sums(first_sum, second_sum):
    return lax.psum((first_sum, second_sum), "my")


def rows_over_my(term_fn, share_rows):
    return lax.psum_scatter(
        term_fn(jnp.int32(0), share_rows * lax.axis_size("my")).astype(jnp.bfloat16),
        "my",
        scatter_dimension=0,
        tiled=True,
    ).astype(jnp.float32)


def rows_over_mx(term_fn, out_rows):
    return lax.psum_scatter(
        term_fn(jnp.int32(0), out_rows * lax.axis_size("mx")).astype(jnp.bfloat16),
        "mx",
        scatter_dimension=0,
        tiled=True,
    ).astype(jnp.float32)


def gather_my(share_values):
    return lax.all_gather(share_values, "my", axis=0, tiled=True)


def gelu_tanh(values):
    return jax.nn.gelu(values, approximate=True)


def gelu_back(hidden_pre, grad_act):
    _, pullback = jax.vjp(gelu_tanh, hidden_pre)
    return pullback(grad_act.astype(jnp.float32))[0].astype(jnp.bfloat16)


def head_norm(values, head_size):
    shaped = values.reshape(values.shape[0], -1, head_size)
    centred = shaped - jnp.mean(shaped, axis=2, keepdims=True)
    inverse = lax.rsqrt(jnp.mean(centred * centred, axis=2, keepdims=True) + EPSILON)
    return (centred * inverse, inverse)


def norm_back(grad_norm, hat_values, inverse, gain):
    grad_hat = grad_norm * gain
    centred = (
        grad_hat
        - jnp.mean(grad_hat, axis=2, keepdims=True)
        - hat_values * jnp.mean(grad_hat * hat_values, axis=2, keepdims=True)
    )
    return (inverse * centred).reshape(grad_norm.shape[0], -1).astype(jnp.bfloat16)


def activate(pre, query_gain, key_gain, head_width):
    head_size = query_gain.shape[0]
    values = pre.astype(jnp.float32)
    row_count = values.shape[0]
    query_hat, query_inv = head_norm(values[:, :head_width], head_size)
    key_hat, key_inv = head_norm(values[:, head_width : 2 * head_width], head_size)
    query_norm = (query_hat * query_gain).reshape(row_count, head_width).astype(jnp.bfloat16)
    key_norm = (key_hat * key_gain).reshape(row_count, head_width).astype(jnp.bfloat16)
    value_rows = pre[:, 2 * head_width : 3 * head_width]
    hidden_pre = values[:, 3 * head_width :]
    hidden_act = gelu_tanh(hidden_pre).astype(jnp.bfloat16)
    return (
        (query_norm, key_norm, value_rows, hidden_act),
        (query_hat, query_inv, key_hat, key_inv, hidden_pre),
    )


def attend(query_norm, key_norm, value_rows, head_size):
    total_rows = query_norm.shape[0]
    four_dims = (total_rows // PATCHES, PATCHES, -1, head_size)
    scale_factor = head_size ** (-0.5)
    scores = (
        jnp.einsum(
            "bqhc,bkhc->bhqk",
            query_norm.reshape(four_dims),
            key_norm.reshape(four_dims),
            preferred_element_type=jnp.float32,
        )
        * scale_factor
    )
    probs = jax.nn.softmax(scores, axis=-1)
    probs_low = probs.astype(jnp.bfloat16)
    attn_mix = jnp.einsum(
        "bhqk,bkhc->bqhc",
        probs_low,
        value_rows.reshape(four_dims),
        preferred_element_type=jnp.float32,
    )
    return (probs, probs_low, attn_mix.reshape(total_rows, -1).astype(jnp.bfloat16))


def attend_back(grad_mix, probs, probs_low, query_norm, key_norm, value_rows, head_size):
    total_rows = query_norm.shape[0]
    four_dims = (total_rows // PATCHES, PATCHES, -1, head_size)
    scale_factor = head_size ** (-0.5)
    grad_four = grad_mix.reshape(four_dims)
    grad_probs = jnp.einsum(
        "bqhc,bkhc->bhqk",
        grad_four,
        value_rows.reshape(four_dims),
        preferred_element_type=jnp.float32,
    )
    grad_value = jnp.einsum(
        "bhqk,bqhc->bkhc", probs_low, grad_four, preferred_element_type=jnp.float32
    )
    grad_value = grad_value.reshape(total_rows, -1).astype(jnp.bfloat16)
    grad_scores = (
        probs * (grad_probs - jnp.sum(grad_probs * probs, axis=-1, keepdims=True))
    ).astype(jnp.bfloat16)
    grad_qn = (
        jnp.einsum(
            "bhqk,bkhc->bqhc",
            grad_scores,
            key_norm.reshape(four_dims),
            preferred_element_type=jnp.float32,
        )
        * scale_factor
    )
    grad_kn = (
        jnp.einsum(
            "bhqk,bqhc->bkhc",
            grad_scores,
            query_norm.reshape(four_dims),
            preferred_element_type=jnp.float32,
        )
        * scale_factor
    )
    return (
        grad_qn.reshape(total_rows, -1, head_size),
        grad_kn.reshape(total_rows, -1, head_size),
        grad_value,
    )


def per_device(
    tokens, ln_gain, query_gain, key_gain, w_qkv, w_hidden, w_attn_out, w_mlp_out, cotangent
):
    head_size = query_gain.shape[0]
    row_count = tokens.shape[0]
    width = tokens.shape[1] * lax.axis_size("my")
    head_width = w_qkv.shape[2]
    share_rows = row_count // lax.axis_size("my")
    out_rows = row_count // lax.axis_size("mx")
    values = tokens.astype(jnp.float32)
    total_one, total_two = feature_sums(jnp.sum(values, axis=1), jnp.sum(values * values, axis=1))
    mean_row = total_one / width
    inverse_row = lax.rsqrt(total_two / width - mean_row * mean_row + EPSILON)
    normal_hat = (values - mean_row[:, None]) * inverse_row[:, None]
    normed = (normal_hat * ln_gain).astype(jnp.bfloat16)

    def in_term(first_row, length):
        rows_in = rows_of(normed, first_row, length)
        return jnp.concatenate(
            [
                jnp.dot(rows_in, w_qkv[0], preferred_element_type=jnp.float32),
                jnp.dot(rows_in, w_qkv[1], preferred_element_type=jnp.float32),
                jnp.dot(rows_in, w_qkv[2], preferred_element_type=jnp.float32),
                jnp.dot(rows_in, w_hidden, preferred_element_type=jnp.float32),
            ],
            1,
        )

    share_pre = rows_over_my(in_term, share_rows).astype(jnp.bfloat16)
    full_pre = gather_my(share_pre)
    full_acts, saved = activate(full_pre, query_gain, key_gain, head_width)
    query_norm, key_norm, value_rows, hidden_act = full_acts
    query_hat, query_inv, key_hat, key_inv, hidden_pre = saved
    probs, probs_low, attn_mix = attend(query_norm, key_norm, value_rows, head_size)

    def out_term(first_row, length):
        return jnp.dot(
            rows_of(attn_mix, first_row, length), w_attn_out, preferred_element_type=jnp.float32
        ) + jnp.dot(
            rows_of(hidden_act, first_row, length), w_mlp_out, preferred_element_type=jnp.float32
        )

    out_sum = rows_over_mx(out_term, out_rows)
    out_start = lax.axis_index("mx") * out_rows
    own_values = rows_of(values, out_start, out_rows)
    mixed = (own_values + out_sum).astype(jnp.bfloat16)
    attn_grad_w = dot_first(attn_mix, cotangent)
    mlp_grad_w = dot_first(hidden_act, cotangent)

    def back_term(first_row, length):
        rows_back = rows_of(cotangent, first_row, length)
        return jnp.concatenate([dot_last(rows_back, w_attn_out), dot_last(rows_back, w_mlp_out)], 1)

    share_back = rows_over_my(back_term, share_rows).astype(jnp.bfloat16)
    full_back = gather_my(share_back)
    grad_hpre = gelu_back(hidden_pre, full_back[:, head_width:])
    grad_qn, grad_kn, grad_value = attend_back(
        full_back[:, :head_width], probs, probs_low, query_norm, key_norm, value_rows, head_size
    )
    grad_query = norm_back(grad_qn, query_hat, query_inv, query_gain)
    grad_key = norm_back(grad_kn, key_hat, key_inv, key_gain)

    def input_term(first_row, length):
        total_term = dot_last(rows_of(grad_query, first_row, length), w_qkv[0])
        total_term = total_term + dot_last(rows_of(grad_key, first_row, length), w_qkv[1])
        total_term = total_term + dot_last(rows_of(grad_value, first_row, length), w_qkv[2])
        return total_term + dot_last(rows_of(grad_hpre, first_row, length), w_hidden)

    grad_normed = rows_over_mx(input_term, out_rows)
    own_hat = rows_of(normal_hat, out_start, out_rows)
    own_inverse = rows_of(inverse_row, out_start, out_rows)
    grad_hat = grad_normed * ln_gain
    mean_one, mean_two = feature_sums(
        jnp.sum(grad_hat, axis=1), jnp.sum(grad_hat * own_hat, axis=1)
    )
    grad_values = own_inverse[:, None] * (
        grad_hat - (mean_one / width)[:, None] - own_hat * (mean_two / width)[:, None]
    )
    own_cotangent = rows_of(cotangent, out_start, out_rows).astype(jnp.float32)
    grad_tokens = (own_cotangent + grad_values).astype(jnp.bfloat16)
    qkv_grad_w = jnp.stack(
        [dot_first(normed, grad_query), dot_first(normed, grad_key), dot_first(normed, grad_value)]
    )
    hidden_grad_w = dot_first(normed, grad_hpre)
    qkv_part, hidden_part, attn_part, mlp_part = (
        lax.psum_scatter(
            qkv_grad_w[:, None].astype(jnp.bfloat16), "dp", scatter_dimension=2, tiled=True
        ).astype(jnp.float32),
        lax.psum_scatter(
            hidden_grad_w[None].astype(jnp.bfloat16), "dp", scatter_dimension=1, tiled=True
        ).astype(jnp.float32),
        lax.psum_scatter(
            attn_grad_w[None].astype(jnp.bfloat16), "dp", scatter_dimension=1, tiled=True
        ).astype(jnp.float32),
        lax.psum_scatter(
            mlp_grad_w[None].astype(jnp.bfloat16), "dp", scatter_dimension=1, tiled=True
        ).astype(jnp.float32),
    )
    return (mixed, grad_tokens, qkv_part, hidden_part, attn_part, mlp_part)


def solution(mesh):
    placed = (
        P("dp", "my"),
        P("my"),
        P(),
        P(),
        P(None, "my", "mx"),
        P("my", "mx"),
        P("mx", "my"),
        P("mx", "my"),
        P("dp", "my"),
    )
    return jax.shard_map(
        per_device,
        mesh=mesh,
        in_specs=placed,
        out_specs=(
            P(("dp", "mx"), "my"),
            P(("dp", "mx"), "my"),
            P(None, "my", "dp", "mx"),
            P("my", "dp", "mx"),
            P("mx", "dp", "my"),
            P("mx", "dp", "my"),
        ),
        check_vma=False,
    )
```

profile of v0, /device:TPU:1, one launch (start us, length us, event | category | flops | bytes accessed | tf_op | source)
XLA Modules:
  0.0 596.5 jit_solution(10645963558544845343)
XLA Ops:
  8.3 29.8 %all-reduce.3 = (f32[128]{0:T(128)S(1)}, f32[128]{0:T(128)S(1)}) all-reduce(f32[128]{0:T(128)S(1)} %get-tuple-element.11, f32[128]{0:T(128)S(1)} %get-tuple-element.10), channel_id=1, replica_groups=mesh['dp'=8,'mx'=8,'my'=16] {'my'}, use_global_device_ids=true, to_apply=%region_3.0 | all-reduce | flops 256 | bytes 2048 | tf_op jit(solution)/shard_map/psum | solution.py:29
  38.2 1.3 convolution_convert_fusion.9
  39.5 1.3 convolution_convert_fusion.10
  40.8 1.3 convolution_convert_fusion.11
  45.7 1.3 dynamic-slice
  48.2 153.1 %all-reduce.7.cloned.1.call-done = (bf16[128,2688]{1,0:T(8,128)(2,1)}, bf16[128,1920]{1,0:T(8,128)(2,1)}) async-done(((bf16[128,2688]{1,0:T(8,128)(2,1)}, bf16[128,1920]{1,0:T(8,128)(2,1)}), (bf16[128,2688]{1,0:T(8,128)(2,1)}, bf16[128,1920]{1,0:T(8,128)(2,1)})) %all-reduce.7.cloned.1.call-update) | async-done | bytes 1179664
  202.1 30.4 %all_gather.6 = bf16[128,2688]{1,0:T(8,128)(2,1)S(1)} all-gather(bf16[8,2688]{1,0:T(8,128)(2,1)S(1)} %constant_dynamic-slice_fusion.1), channel_id=1, replica_groups=mesh['dp'=8,'mx'=8,'my'=16] {'my'}, dimensions={0}, use_global_device_ids=true | all-gather | bytes 731136 | tf_op jit(solution)/shard_map/all_gather | solution.py:51
  235.4 26.3 %all_gather.7 = bf16[128,1920]{1,0:T(8,128)(2,1)S(1)} all-gather(bf16[8,1920]{1,0:T(8,128)(2,1)S(1)} %constant_dynamic-slice_fusion), channel_id=1, replica_groups=mesh['dp'=8,'mx'=8,'my'=16] {'my'}, dimensions={0}, use_global_device_ids=true | all-gather | bytes 522240 | tf_op jit(solution)/shard_map/all_gather | solution.py:51
  265.4 1.5 fusion.46
  266.9 2.1 convolution_convert_fusion.13
  269.0 1.3 multiply_reduce_fusion.2
  271.4 1.5 fusion.39
  272.9 1.5 fusion.38
  274.5 2.1 convolution_convert_fusion.12
  284.7 1.5 fusion.35
  286.2 1.9 fusion.25
  291.4 2.5 fusion.9
  297.2 1.6 fusion.1
  298.9 1.5 fusion.2
  300.7 49.8 %reduce-scatter.9.cloned.1.call-done = bf16[16,384]{1,0:T(8,128)(2,1)} async-done(((bf16[128,384]{1,0:T(8,128)(2,1)}), bf16[16,384]{1,0:T(8,128)(2,1)}) %reduce-scatter.9.cloned.1.call-update) | async-done | bytes 12304 | tf_op jit(solution)/shard_map/reduce_scatter | solution.py:42
  351.3 27.5 %all-reduce.2 = (f32[16]{0:T(128)S(1)}, f32[16]{0:T(128)S(1)}) all-reduce(f32[16]{0:T(128)S(1)} %get-tuple-element.13, f32[16]{0:T(128)S(1)} %get-tuple-element.12), channel_id=1, replica_groups=mesh['dp'=8,'mx'=8,'my'=16] {'my'}, use_global_device_ids=true, to_apply=%region_22.0 | all-reduce | flops 32 | bytes 256 | tf_op jit(solution)/shard_map/psum | solution.py:29
  378.8 17.5 %reduce-scatter.7.cloned.1.call-done = bf16[16,384]{1,0:T(8,128)(2,1)} async-done(((bf16[128,384]{1,0:T(8,128)(2,1)}), bf16[16,384]{1,0:T(8,128)(2,1)}) %reduce-scatter.7.cloned.1.call-update) | async-done | bytes 12304 | tf_op jit(solution)/shard_map/reduce_scatter | solution.py:42
  396.3 1.3 add_convert_fusion.1
  397.6 1.4 add_convert_fusion
  399.0 48.1 %reduce-scatter.15.cloned.1.call-done = bf16[1,48,384]{2,1,0:T(8,128)(2,1)} async-done(((bf16[1,384,384]{2,1,0:T(8,128)(2,1)}), bf16[1,48,384]{2,1,0:T(8,128)(2,1)}) %reduce-scatter.15.cloned.1.call-update) | async-done | bytes 36880 | tf_op jit(solution)/shard_map/reduce_scatter | solution.py:255
  447.1 1.4 convert_element_type.164
  448.5 44.8 %reduce-scatter.11.cloned.1.call-done = bf16[3,1,48,384]{3,2,1,0:T(8,128)(2,1)} async-done(((bf16[3,1,384,384]{3,2,1,0:T(8,128)(2,1)}), bf16[3,1,48,384]{3,2,1,0:T(8,128)(2,1)}) %reduce-scatter.11.cloned.1.call-update) | async-done | bytes 110608 | tf_op jit(solution)/shard_map/reduce_scatter | solution.py:249
  493.3 1.6 convert_element_type.158
  494.9 45.7 %reduce-scatter.13.cloned.1.call-done = bf16[1,48,1536]{2,1,0:T(8,128)(2,1)} async-done(((bf16[1,384,1536]{2,1,0:T(8,128)(2,1)}), bf16[1,48,1536]{2,1,0:T(8,128)(2,1)}) %reduce-scatter.13.cloned.1.call-update) | async-done | bytes 147472 | tf_op jit(solution)/shard_map/reduce_scatter | solution.py:252
  540.6 1.6 convert_element_type.161
  542.3 45.7 %reduce-scatter.17.cloned.1.call-done = bf16[1,192,384]{2,1,0:T(8,128)(2,1)} async-done(((bf16[1,1536,384]{2,1,0:T(8,128)(2,1)}), bf16[1,192,384]{2,1,0:T(8,128)(2,1)}) %reduce-scatter.17.cloned.1.call-update) | async-done | bytes 147472 | tf_op jit(solution)/shard_map/reduce_scatter | solution.py:258
  588.0 1.6 convert_element_type.167
  (130 shorter events, 29.1 us)
Async XLA Ops:
  7.2 35.0 %copy-start = (bf16[384,1536]{1,0:T(8,128)(2,1)S(1)}, bf16[384,1536]{1,0:T(8,128)(2,1)}, u32[]{:S(2)}) copy-start(bf16[384,1536]{1,0:T(8,128)(2,1)} %param.14) | copy-start | bytes 3538948
  7.2 33.6 %copy-start.1 = (bf16[128,384]{1,0:T(8,128)(2,1)S(1)}, bf16[128,384]{1,0:T(8,128)(2,1)}, u32[]{:S(2)}) copy-start(bf16[128,384]{1,0:T(8,128)(2,1)} %param.9) | copy-start | bytes 294916
  7.2 33.6 %copy-start.21 = (f32[384]{0:T(512)S(1)}, f32[384]{0:T(512)}, u32[]{:S(2)}) copy-start(f32[384]{0:T(512)} %param.10) | copy-start | bytes 4612
  7.2 194.1 %all-reduce.7.cloned.1.call-start = ((), (), s32[]{:S(2)}) async-start(), calls=%async_computation.12 | async-start | bytes 2359296
  38.2 4.4 copy-start.24
  38.2 4.4 copy-start.26
  40.8 1.8 copy-start.4
  40.8 1.8 copy-start.7
  44.7 2.9 copy-start.28
  44.7 2.9 copy-start.30
  45.6 304.9 %reduce-scatter.9.cloned.1.call-start = ((), (), s32[]{:S(2)}) async-start(), calls=%async_computation.7 | async-start | bytes 110592 | tf_op jit(solution)/shard_map/reduce_scatter | solution.py:42
  261.7 14.9 %copy-start.2 = (bf16[128,1920]{1,0:T(8,128)(2,1)}, bf16[128,1920]{1,0:T(8,128)(2,1)S(1)}, u32[]{:S(2)}) copy-start(bf16[128,1920]{1,0:T(8,128)(2,1)S(1)} %all_gather.7) | copy-start | bytes 1474564
  265.4 1.6 copy-start.10
  266.9 4.4 copy-start.3
  269.0 2.3 copy-start.13
  269.0 2.4 copy-start.29
  269.0 3.9 copy-start.11
  269.0 3.9 copy-start.23
  269.0 3.9 copy-start.31
  274.5 2.1 copy-start.6
  274.5 2.1 copy-start.17
  277.5 10.6 %slice-start = ((bf16[128,1920]{1,0:T(8,128)(2,1)}), bf16[128,1536]{1,0:T(8,128)(2,1)S(1)}, s32[]{:S(2)}) async-start(bf16[128,1920]{1,0:T(8,128)(2,1)} %copy-done.2), calls=%async_computation.13 | async-start | bytes 786432 | tf_op jit(solution)/shard_map/slice | solution.py:219
  291.3 2.6 copy-start.8
  291.3 2.6 copy-start.18
  291.3 3.7 copy-start.20
  291.3 3.7 copy-start.25
  291.3 3.7 copy-start.27
  291.3 105.0 %reduce-scatter.7.cloned.1.call-start = ((), (), s32[]{:S(2)}) async-start(), calls=%async_computation.6 | async-start | bytes 110592 | tf_op jit(solution)/shard_map/reduce_scatter | solution.py:42
  293.9 153.2 %reduce-scatter.15.cloned.1.call-start = ((), (), s32[]{:S(2)}) async-start(), calls=%async_computation.10 | async-start | bytes 331776 | tf_op jit(solution)/shard_map/reduce_scatter | solution.py:255
  294.9 198.4 %reduce-scatter.11.cloned.1.call-start = ((), (), s32[]{:S(2)}) async-start(), calls=%async_computation.8 | async-start | bytes 995328 | tf_op jit(solution)/shard_map/reduce_scatter | solution.py:249
  297.2 243.4 %reduce-scatter.13.cloned.1.call-start = ((), (), s32[]{:S(2)}) async-start(), calls=%async_computation.9 | async-start | bytes 1327104 | tf_op jit(solution)/shard_map/reduce_scatter | solution.py:252
  298.8 289.1 %reduce-scatter.17.cloned.1.call-start = ((), (), s32[]{:S(2)}) async-start(), calls=%async_computation.11 | async-start | bytes 1327104 | tf_op jit(solution)/shard_map/reduce_scatter | solution.py:258
  (8 other events, 9.6 us)
Sparse Core Ops, SparseCore 0:
  45.7 155.5 all-reduce.6
  291.4 59.0 reduce-scatter.8
  354.8 41.4 reduce-scatter.6
  400.1 46.9 reduce-scatter.14
  450.8 42.5 reduce-scatter.10
  496.6 43.9 reduce-scatter.12
  544.0 43.9 reduce-scatter.16
where the time goes:
time: 600 us; the launch traced here: 596 us
  waiting for transfers between devices  405 us (68%)
  blocking collectives  114 us (19%)
  matrix products  27.3 us (5%)
  other arithmetic  24.3 us (4%)
  between operations  15.3 us (3%)
  local copies, waits for them, and re-layouts  10.4 us (2%)
    unnamed x8, waiting for transfers between devices  153 us
    reduce_scatter x2, waiting for transfers between devices, rows_over_mx(): lax.psum_scatter(term_fn(jnp.int32(0), out_rows * lax.axis_size('mx')).as...  67.3 us
    psum x2, blocking collectives, feature_sums(): return lax.psum((first_sum, second_sum), 'my')  57.3 us
    all_gather x2, blocking collectives, gather_my(): return lax.all_gather(share_values, 'my', axis=0, tiled=True)  56.7 us
    reduce_scatter x1, waiting for transfers between devices, per_device(): lax.psum_scatter(attn_grad_w[None].astype(jnp.bfloat16), 'dp', scatter_di...  48.1 us
    reduce_scatter x1, waiting for transfers between devices, per_device(): lax.psum_scatter(mlp_grad_w[None].astype(jnp.bfloat16), 'dp', scatter_dim...  45.7 us
    reduce_scatter x1, waiting for transfers between devices, per_device(): lax.psum_scatter(hidden_grad_w[None].astype(jnp.bfloat16), 'dp', scatter_...  45.7 us
    reduce_scatter x1, waiting for transfers between devices, per_device(): lax.psum_scatter(qkv_grad_w[:, None].astype(jnp.bfloat16), 'dp', scatter_...  44.8 us
  transfers between devices with their start and end apart: 7, of which 7 were waited for; matrix products, arithmetic and copies ran while one was open for 3% of the time, Pallas kernels for 0%

commit v1 on v0

v1 whole, which is shorter than its diff:
```python
import jax
import jax.numpy as jnp
from jax import lax
from jax.experimental import pallas as pl
from jax.experimental.pallas import tpu as pltpu
from jax.sharding import PartitionSpec as P

EPSILON = 1e-06
LANES = 128
BF16 = jnp.bfloat16
F32 = jnp.float32


def dot_plain(matrix_a, matrix_b):
    return jnp.dot(matrix_a, matrix_b, preferred_element_type=F32)


def dot_first(matrix_a, matrix_b):
    return lax.dot_general(matrix_a, matrix_b, (((0,), (0,)), ((), ())), preferred_element_type=F32)


def dot_last(matrix_a, matrix_b):
    return lax.dot_general(matrix_a, matrix_b, (((1,), (1,)), ((), ())), preferred_element_type=F32)


def pieces(value, count):
    out = []
    for _ in range(count):
        part = value.astype(BF16).astype(F32)
        out.append(part)
        value = value - part
    return out


def to_lanes(columns):
    rows = columns[0].shape[0]
    lane = lax.broadcasted_iota(jnp.int32, (rows, LANES), 1)
    block = jnp.zeros((rows, LANES), F32)
    for index, column in enumerate(columns):
        block = jnp.where(lane == index, column, block)
    return block


def from_lanes(block, first, count):
    lane = lax.broadcasted_iota(jnp.int32, block.shape, block.ndim - 1)
    keep = (lane >= first) & (lane < first + count)
    return jnp.sum(jnp.where(keep, block, 0.0), axis=-1, keepdims=True)


def whole(count):
    return [pl.BlockSpec(memory_space=pltpu.VMEM)] * count


def run(kernel, operands, out_shape, scratch=(), scalar=False):
    n_out = len(out_shape)
    in_specs = whole(len(operands))
    if scalar:
        in_specs[0] = pl.BlockSpec(memory_space=pltpu.SMEM)
    return pl.pallas_call(
        kernel,
        in_specs=in_specs,
        out_specs=whole(n_out),
        out_shape=out_shape,
        scratch_shapes=list(scratch),
        compiler_params=pltpu.CompilerParams(vmem_limit_bytes=56 * 1024 * 1024),
    )(*operands)


def project_kernel(share, tokens, ln_gain, w_qkv, w_hidden, w_attn, w_mlp, cotangent, out):
    rows, width = tokens.shape
    head_width = w_qkv.shape[2]
    blocks = w_hidden.shape[1] // head_width
    values = tokens[...].astype(F32)
    mean = jnp.sum(values, axis=1, keepdims=True) / width
    centred = values - mean
    squares = jnp.sum(centred * centred, axis=1, keepdims=True)
    gain = ln_gain[...]
    scaled = (centred * gain).astype(BF16)
    high, low = pieces(gain, 2)
    row_id = lax.broadcasted_iota(jnp.int32, (16, width), 0)
    gain_rows = jnp.where(row_id == 0, high, jnp.where(row_id == 1, low, 0.0)).astype(BF16)
    share_id = lax.broadcasted_iota(jnp.int32, (share, head_width), 0)
    gain_sums = jnp.zeros((share, head_width), F32)
    for block in range(3 + blocks):
        if block < 3:
            weight = w_qkv[block]
        else:
            weight = w_hidden[:, (block - 3) * head_width : (block - 2) * head_width]
        start = block * head_width
        out[:, start : start + head_width] = dot_plain(scaled, weight).astype(BF16)
        both = dot_plain(gain_rows, weight)
        gain_sums = jnp.where(share_id == block, both[0:1] + both[1:2], gain_sums)
    start = (3 + blocks) * head_width
    back = cotangent[...]
    out[:, start : start + head_width] = dot_last(back, w_attn[...]).astype(BF16)
    start += head_width
    for block in range(blocks):
        weight = w_mlp[block * head_width : (block + 1) * head_width, :]
        out[:, start : start + head_width] = dot_last(back, weight).astype(BF16)
        start += head_width
    spread = jnp.broadcast_to(gain_sums[None], (rows // share, share, head_width))
    out[:, start : start + head_width] = spread.reshape(rows, head_width).astype(BF16)
    start += head_width
    out[:, start : start + LANES] = to_lanes(pieces(mean, 3) + pieces(squares, 3)).astype(BF16)


def share_kernel(head_width, local_width, got, out, sums_out):
    rows, columns = got.shape
    share = sums_out.shape[0]
    parts = rows // share
    hidden_width = (columns - 5 * head_width - LANES) // 2
    blocks = hidden_width // head_width
    width = parts * local_width

    def take(start, length):
        return got[:, start : start + length].astype(F32).reshape(parts, share, length)

    stats_at = columns - LANES
    stats = take(stats_at, LANES)
    local_mean = from_lanes(stats, 0, 3)
    mean = jnp.sum(local_mean, axis=0, keepdims=True) / parts
    shift = local_mean - mean
    square_sum = jnp.sum(from_lanes(stats, 3, 3) + local_width * shift * shift, axis=0)
    inverse = lax.rsqrt(square_sum / width + EPSILON)
    gain_parts = take(stats_at - head_width, head_width)
    gain_sums = jnp.sum(gain_parts, axis=0)
    sums_out[...] = gain_sums

    def spread(value):
        length = value.shape[1]
        tiled = jnp.broadcast_to(value[None], (parts, share, length))
        return tiled.reshape(rows, length).astype(BF16)

    def projected(block):
        total = jnp.sum(take(block * head_width, head_width), axis=0)
        total = total + jnp.sum(shift * gain_parts[:, block : block + 1, :], axis=0)
        return (inverse * total).astype(BF16).astype(F32)

    back_at = (3 + blocks) * head_width
    for block in range(3):
        out[:, block * head_width : (block + 1) * head_width] = spread(projected(block))
    out[:, 3 * head_width : 4 * head_width] = spread(jnp.sum(take(back_at, head_width), axis=0))
    plain_sum = jnp.zeros((share, 1), F32)
    hat_sum = jnp.zeros((share, 1), F32)
    inner_scale = 0.7978845608028654
    for block in range(blocks):
        pre = projected(3 + block)
        grad_act = jnp.sum(take(back_at + (1 + block) * head_width, head_width), axis=0)
        grad_act = grad_act.astype(BF16).astype(F32)
        squared = pre * pre
        bent = jnp.tanh(inner_scale * (pre + 0.044715 * squared * pre))
        active = 0.5 * pre * (1.0 + bent)
        slope = 0.5 * (1.0 + bent) + 0.5 * pre * (1.0 - bent * bent) * inner_scale * (
            1.0 + 3.0 * 0.044715 * squared
        )
        grad_pre = (grad_act * slope).astype(BF16).astype(F32)
        plain_sum += jnp.sum(grad_pre * gain_sums[3 + block : 4 + block], axis=1, keepdims=True)
        hat_sum += jnp.sum(grad_pre * pre, axis=1, keepdims=True)
        start = (4 + block) * head_width
        out[:, start : start + head_width] = spread(active)
        start += hidden_width
        out[:, start : start + head_width] = spread(grad_pre)
    scalars = pieces(mean[0], 3) + pieces(inverse, 3) + pieces(plain_sum, 2) + pieces(hat_sum, 2)
    out[:, 4 * head_width + 2 * hidden_width :] = spread(to_lanes(scalars))


def attend_kernel(
    full, gain_sums, tokens, ln_gain, query_gain, key_gain, w_qkv, w_hidden, w_attn, w_mlp,
    cotangent, terms, acts,
):
    head_size = query_gain.shape[1]
    head_width = w_qkv.shape[2]
    hidden_width = w_hidden.shape[1]
    local_width = tokens.shape[1]
    stats = full[:, 4 * head_width + 2 * hidden_width :].astype(F32)
    mean, inverse = from_lanes(stats, 0, 3), from_lanes(stats, 3, 3)
    plain_sum, hat_sum = from_lanes(stats, 6, 2), from_lanes(stats, 8, 2)
    normal_hat = (tokens[...].astype(F32) - mean) * inverse
    acts[:, :local_width] = (normal_hat * ln_gain[...]).astype(BF16)
    acts[:, local_width : 2 * local_width] = cotangent[...]
    hidden_at = 4 * head_width
    acts_hidden = 2 * local_width
    acts[:, acts_hidden : acts_hidden + 2 * hidden_width] = full[:, hidden_at : hidden_at + 2 * hidden_width]
    acts_heads = acts_hidden + 2 * hidden_width
    scale = head_size ** (-0.5)

    def normalise(values):
        centred = values - jnp.mean(values, axis=1, keepdims=True)
        root = lax.rsqrt(jnp.mean(centred * centred, axis=1, keepdims=True) + EPSILON)
        return centred * root, root

    def back(grad, hat, root, gain):
        grad = grad * gain
        centred = grad - jnp.mean(grad, axis=1, keepdims=True)
        centred = centred - hat * jnp.mean(grad * hat, axis=1, keepdims=True)
        return (root * centred).astype(BF16)

    for head in range(head_width // head_size):
        low, high = head * head_size, (head + 1) * head_size
        query = full[:, low:high].astype(F32)
        key = full[:, head_width + low : head_width + high].astype(F32)
        value_low = full[:, 2 * head_width + low : 2 * head_width + high]
        grad_mix = full[:, 3 * head_width + low : 3 * head_width + high]
        query_hat, query_root = normalise(query)
        key_hat, key_root = normalise(key)
        query_norm = (query_hat * query_gain[...]).astype(BF16)
        key_norm = (key_hat * key_gain[...]).astype(BF16)
        scores = dot_last(query_norm, key_norm) * scale
        weights = jnp.exp(scores - jnp.max(scores, axis=1, keepdims=True))
        probs = weights / jnp.sum(weights, axis=1, keepdims=True)
        probs_low = probs.astype(BF16)
        acts[:, acts_heads + low : acts_heads + high] = dot_plain(probs_low, value_low).astype(BF16)
        grad_probs = dot_last(grad_mix, value_low)
        grad_value = dot_first(probs_low, grad_mix).astype(BF16)
        grad_scores = probs * (grad_probs - jnp.sum(grad_probs * probs, axis=1, keepdims=True))
        grad_scores = grad_scores.astype(BF16)
        grad_query = back(
            dot_plain(grad_scores, key_norm) * scale, query_hat, query_root, query_gain[...]
        )
        grad_key = back(
            dot_first(grad_scores, query_norm) * scale, key_hat, key_root, key_gain[...]
        )
        plain = jnp.zeros_like(query)
        with_hat = jnp.zeros_like(query)
        for part, (grad, pre) in enumerate(
            ((grad_query, query), (grad_key, key), (grad_value, value_low.astype(F32)))
        ):
            start = acts_heads + (1 + part) * head_width
            acts[:, start + low : start + high] = grad
            grad = grad.astype(F32)
            plain = plain + grad * gain_sums[part : part + 1, low:high]
            with_hat = with_hat + grad * pre
        plain_sum = plain_sum + jnp.sum(plain, axis=1, keepdims=True)
        hat_sum = hat_sum + jnp.sum(with_hat, axis=1, keepdims=True)

    mixed = dot_plain(acts[:, acts_heads : acts_heads + head_width], w_attn[...])
    mixed = mixed + dot_plain(full[:, hidden_at : hidden_at + hidden_width], w_mlp[...])
    terms[:, :local_width] = mixed.astype(BF16)
    grad_normed = dot_last(full[:, hidden_at + hidden_width : hidden_at + 2 * hidden_width], w_hidden[...])
    for part in range(3):
        start = acts_heads + (1 + part) * head_width
        grad_normed = grad_normed + dot_last(acts[:, start : start + head_width], w_qkv[part])
    terms[:, local_width : 2 * local_width] = grad_normed.astype(BF16)
    terms[:, 2 * local_width :] = to_lanes(pieces(plain_sum, 2) + pieces(hat_sum, 2)).astype(BF16)


def weight_kernel(
    head_width, hidden_width, n_dp, place, own, peer, first, *rest
):
    others, (norm_t, mix_t, act_t) = rest[:-3], rest[-3:]
    local_width = norm_t.shape[0]
    hidden_at = 2 * local_width
    heads_at = hidden_at + 2 * hidden_width

    def both(start, length):
        return jnp.concatenate([own[:, start : start + length], peer[:, start : start + length]], axis=0)

    norm_t[...] = both(0, local_width).T
    mix_t[...] = both(heads_at, head_width).T
    act_t[...] = both(hidden_at, hidden_width).T
    outs = (first,) + tuple(others)
    chips = n_dp // 2
    core, chip = place[0] % 2, place[0] // 2
    owners = [2 * ((chip + step) % chips) + core for step in range(chips)]

    def rows(ref, length):
        return jnp.concatenate(
            [ref[pl.ds(pl.multiple_of(owner * length, 16), length), :] for owner in owners], axis=0
        )

    row = 0

    def emit(left, right):
        nonlocal row
        length = left.shape[0] // chips
        product = dot_plain(left, right)
        for step, out in enumerate(outs):
            out[row : row + length, :] = product[step * length : (step + 1) * length].astype(out.dtype)
        row += length

    norm_rows = rows(norm_t, local_width // n_dp)
    for part in range(3):
        emit(norm_rows, both(heads_at + (1 + part) * head_width, head_width))
    for block in range(hidden_width // head_width):
        emit(norm_rows, both(hidden_at + hidden_width + block * head_width, head_width))
    cotangent = both(local_width, local_width)
    emit(rows(mix_t, head_width // n_dp), cotangent)
    emit(rows(act_t, hidden_width // n_dp), cotangent)


def token_kernel(place, got, full, tokens, ln_gain, cotangent, mixed, grad_tokens):
    out_rows, local_width = mixed.shape
    parts = got.shape[0] // out_rows
    width = place[1]
    first = pl.multiple_of(place[0] * out_rows, 16)

    def total(start, length):
        values = got[:, start : start + length].astype(F32)
        return jnp.sum(values.reshape(parts, out_rows, length), axis=0)

    values = tokens[pl.ds(first, out_rows), :].astype(F32)
    mixed[...] = (values + total(0, local_width)).astype(BF16)
    stats = full[pl.ds(first, out_rows), full.shape[1] - LANES :].astype(F32)
    mean, inverse = from_lanes(stats, 0, 3), from_lanes(stats, 3, 3)
    normal_hat = (values - mean) * inverse
    sums = total(2 * local_width, LANES)
    share = 1.0 / width.astype(F32)
    mean_one, mean_two = from_lanes(sums, 0, 2) * share, from_lanes(sums, 2, 2) * share
    grad_hat = total(local_width, local_width) * ln_gain[...]
    grad = inverse * (grad_hat - mean_one - normal_hat * mean_two)
    back = cotangent[pl.ds(first, out_rows), :].astype(F32)
    grad_tokens[...] = (back + grad).astype(BF16)


def sum_kernel(*refs):
    parts, (qkv, hidden, attn, mlp) = refs[:-4], refs[-4:]

    def total(start, length):
        value = parts[0][start : start + length, :].astype(F32)
        for part in parts[1:]:
            value = value + part[start : start + length, :].astype(F32)
        return value

    row = 0
    length, head_width = qkv.shape[2], qkv.shape[3]
    for part in range(3):
        qkv[part, 0] = total(row, length)
        row += length
    for block in range(hidden.shape[2] // head_width):
        hidden[0, :, block * head_width : (block + 1) * head_width] = total(row, length)
        row += length
    attn[0] = total(row, attn.shape[1])
    row += attn.shape[1]
    mlp[0] = total(row, mlp.shape[1])


def exchange(values, axis):
    return lax.all_to_all(values, axis, 0, 0, tiled=True)


def per_device(
    tokens, ln_gain, query_gain, key_gain, w_qkv, w_hidden, w_attn_out, w_mlp_out, cotangent
):
    n_dp, n_mx, n_my = lax.axis_size("dp"), lax.axis_size("mx"), lax.axis_size("my")
    row_count, local_width = tokens.shape
    head_width, hidden_width = w_qkv.shape[2], w_hidden.shape[1]
    width = local_width * n_my
    share, out_rows = row_count // n_my, row_count // n_mx
    ln_row, query_row, key_row = ln_gain[None], query_gain[None], key_gain[None]

    def shape(*dims, dtype=BF16):
        return jax.ShapeDtypeStruct(dims, dtype)

    (terms,) = run(
        lambda *refs: project_kernel(share, *refs),
        (tokens, ln_row, w_qkv, w_hidden, w_attn_out, w_mlp_out, cotangent),
        (shape(row_count, 5 * head_width + 2 * hidden_width + LANES),),
    )
    got = exchange(terms, "my")
    spread, gain_sums = run(
        lambda *refs: share_kernel(head_width, local_width, *refs),
        (got,),
        (
            shape(row_count, 4 * head_width + 2 * hidden_width + LANES),
            shape(share, head_width, dtype=F32),
        ),
    )
    full = exchange(spread, "my")
    act_width = 2 * local_width + 2 * hidden_width + 4 * head_width
    out_terms, acts = run(
        attend_kernel,
        (
            full, gain_sums, tokens, ln_row, query_row, key_row,
            w_qkv, w_hidden, w_attn_out, w_mlp_out, cotangent,
        ),
        (shape(row_count, 2 * local_width + LANES), shape(row_count, act_width)),
    )
    peer_acts = lax.ppermute(acts, "dp", [(source, source ^ 1) for source in range(n_dp)])
    out_got = exchange(out_terms, "mx")
    chips = n_dp // 2
    block_rows = (3 * local_width + local_width * hidden_width // head_width + head_width + hidden_width) // n_dp
    place = lax.axis_index("dp").reshape(1)
    sums = run(
        lambda *refs: weight_kernel(head_width, hidden_width, n_dp, *refs),
        (place, acts, peer_acts),
        tuple(shape(block_rows, local_width, dtype=BF16 if step else F32) for step in range(chips)),
        scratch=(
            pltpu.VMEM((local_width, 2 * row_count), BF16),
            pltpu.VMEM((head_width, 2 * row_count), BF16),
            pltpu.VMEM((hidden_width, 2 * row_count), BF16),
        ),
        scalar=True,
    )
    parts = [sums[0]]
    for step in range(1, chips):
        pairs = [(s, 2 * ((s // 2 + step) % chips) + s % 2) for s in range(n_dp)]
        parts.append(lax.ppermute(sums[step], "dp", pairs))
    place = jnp.stack([lax.axis_index("mx"), jnp.int32(width)])
    mixed, grad_tokens = run(
        token_kernel,
        (place, out_got, full, tokens, ln_row, cotangent),
        (shape(out_rows, local_width), shape(out_rows, local_width)),
        scalar=True,
    )
    grads = run(
        sum_kernel,
        tuple(parts),
        (
            shape(3, 1, local_width // n_dp, head_width, dtype=F32),
            shape(1, local_width // n_dp, hidden_width, dtype=F32),
            shape(1, head_width // n_dp, local_width, dtype=F32),
            shape(1, hidden_width // n_dp, local_width, dtype=F32),
        ),
    )
    return (mixed, grad_tokens, *grads)


def solution(mesh):
    placed = (
        P("dp", "my"),
        P("my"),
        P(),
        P(),
        P(None, "my", "mx"),
        P("my", "mx"),
        P("mx", "my"),
        P("mx", "my"),
        P("dp", "my"),
    )
    return jax.shard_map(
        per_device,
        mesh=mesh,
        in_specs=placed,
        out_specs=(
            P(("dp", "mx"), "my"),
            P(("dp", "mx"), "my"),
            P(None, "my", "dp", "mx"),
            P("my", "dp", "mx"),
            P("mx", "dp", "my"),
            P("mx", "dp", "my"),
        ),
        check_vma=False,
    )
```

time: 600 us -> 170 us (0.28)
  waiting for transfers between devices: 405 us -> 29.8 us
  blocking collectives: 114 us -> 64.2 us
  starting transfers between devices: 0.29 us -> 47.6 us
  matrix products: 27.3 us -> 0 us
  other arithmetic: 24.3 us -> 0.58 us
  Pallas kernels: 0 us -> 22.3 us
  between operations: 15.3 us -> 0.68 us
  local copies, waits for them, and re-layouts: 10.4 us -> 3.79 us
    reduce_scatter x6 -> x0, waiting for transfers between devices: 252 us -> none  [the longest x2 67.3 us: rows_over_mx(): lax.psum_scatter(term_fn(jnp.int32(0), out_rows * lax.axis_size('mx')).as...]
    unnamed x8 -> x0, waiting for transfers between devices: 153 us -> none
    all_to_all x0 -> x2, blocking collectives: none -> 64.2 us  [exchange(): return lax.all_to_all(values, axis, 0, 0, tiled=True)]
    psum x2 -> x0, blocking collectives: 57.3 us -> none  [feature_sums(): return lax.psum((first_sum, second_sum), 'my')]
    all_gather x2 -> x0, blocking collectives: 56.7 us -> none  [gather_my(): return lax.all_gather(share_values, 'my', axis=0, tiled=True)]
    ppermute x0 -> x4, starting transfers between devices: none -> 40.3 us  [the longest x3 27.9 us: per_device(): parts.append(lax.ppermute(sums[step], 'dp', pairs))]
    dot_general x23 -> x0, matrix products: 25.8 us -> none  [the longest x6 5.15 us: dot_first(): lax.dot_general(matrix_a, matrix_b, (((0,), (0,)), ((), ())), preferred_e...]
    pallas_call x0 -> x6, Pallas kernels: none -> 22.3 us  [run(): pl.pallas_call(kernel, in_specs=in_specs, out_specs=whole(n_out), out_sha...]
  transfers between devices with their start and end apart: 7 -> 5, of which waited for: 7 -> 4; matrix products, arithmetic and copies ran while one was open for 3% -> 0% of each run, Pallas kernels for 0% -> 1%
where the time goes in v1:
time: 170 us; the launch traced here: 169 us
  blocking collectives  64.2 us (38%)
  starting transfers between devices  47.6 us (28%)
  waiting for transfers between devices  29.8 us (18%)
  Pallas kernels  22.3 us (13%)
  local copies, waits for them, and re-layouts  3.79 us (2%)
    all_to_all x2, blocking collectives, exchange(): return lax.all_to_all(values, axis, 0, 0, tiled=True)  64.2 us
    ppermute x3, starting transfers between devices, per_device(): parts.append(lax.ppermute(sums[step], 'dp', pairs))  27.9 us
    pallas_call x6, Pallas kernels, run(): pl.pallas_call(kernel, in_specs=in_specs, out_specs=whole(n_out), out_sha...  22.3 us
    ppermute x3, waiting for transfers between devices, per_device(): parts.append(lax.ppermute(sums[step], 'dp', pairs))  17.7 us
    ppermute x1, starting transfers between devices, per_device(): lax.ppermute(acts, 'dp', [(source, source ^ 1) for source in range(n_dp)])  12.4 us
    all_to_all x1, waiting for transfers between devices, exchange(): return lax.all_to_all(values, axis, 0, 0, tiled=True)  9.1 us
    all_to_all x1, starting transfers between devices, exchange(): return lax.all_to_all(values, axis, 0, 0, tiled=True)  7.28 us
  transfers between devices with their start and end apart: 5, of which 4 were waited for; matrix products, arithmetic and copies ran while one was open for 0% of the time, Pallas kernels for 1%

profile of v1, /device:TPU:1, one launch (start us, length us, event | category | flops | bytes accessed | tf_op | source)
XLA Modules:
  0.0 169.0 jit_solution(6136469660418482303)
XLA Ops:
  0.6 1.2 broadcast_in_dim.9.refs_1_.ln_gain
  1.9 4.5 %shard_map.136 = bf16[128,5120]{1,0:T(8,128)(2,1)} custom-call(bf16[128,384]{1,0:T(8,128)(2,1)} %tokens.3, f32[1,384]{1,0:T(1,128)} %broadcast_in_dim.9.refs_1_.ln_gain, bf16[3,384,384]{2,1,0:T(8,128)(2,1)} %w_qkv.1, bf16[384,1536]{1,0:T(8,128)(2,1)} %w_hidden.1, bf16[384,384]{1,0:T(8,128)(2,1)} %w_attn.1, bf16[1536,384]{1,0:T(8,128)(2,1)} %w_mlp.1, ...), custom_call_target="tpu_custom_call" | custom-call | tf_op jit(solution)/shard_map/pallas_call | solution.py:59
  6.4 36.7 %all_to_all.33 = bf16[16,8,5120]{2,1,0:T(8,128)(2,1)} all-to-all(bf16[16,8,5120]{2,1,0:T(8,128)(2,1)} %bitcast.13), channel_id=1, replica_groups=mesh['dp'=8,'mx'=8,'my'=16] {'my'}, dimensions={0} | all-to-all | bytes 2621440 | tf_op jit(solution)/shard_map/all_to_all | solution.py:338
  43.1 2.9 %shard_map.137 = (bf16[128,4736]{1,0:T(8,128)(2,1)}, f32[8,384]{1,0:T(8,128)}) custom-call(bf16[128,5120]{1,0:T(8,128)(2,1)} %bitcast.12), custom_call_target="tpu_custom_call" | custom-call | tf_op jit(solution)/shard_map/pallas_call | solution.py:59
  46.0 27.6 %all_to_all.34 = bf16[16,8,4736]{2,1,0:T(8,128)(2,1)} all-to-all(bf16[16,8,4736]{2,1,0:T(8,128)(2,1)} %bitcast.14), channel_id=1, replica_groups=mesh['dp'=8,'mx'=8,'my'=16] {'my'}, dimensions={0} | all-to-all | bytes 2424832 | tf_op jit(solution)/shard_map/all_to_all | solution.py:338
  73.5 6.5 %shard_map.138 = (bf16[128,896]{1,0:T(8,128)(2,1)}, bf16[128,5376]{1,0:T(8,128)(2,1)}) custom-call(bf16[128,4736]{1,0:T(8,128)(2,1)} %bitcast.10, f32[8,384]{1,0:T(8,128)} %get-tuple-element.21.gain_sums, bf16[128,384]{1,0:T(8,128)(2,1)} %tokens.3, f32[1,384]{1,0:T(1,128)} %broadcast_in_dim.9.refs_1_.ln_gain, f32[1,128]{1,0:T(1,128)} %bitcast.16, ...), custom_call_target="tpu_custom_call" | custom-call | tf_op jit(solution)/shard_map/pallas_call | solution.py:59
  80.0 12.4 %collective-permute-start = (bf16[128,5376]{1,0:T(8,128)(2,1)}, bf16[128,5376]{1,0:T(8,128)(2,1)S(1)}, u32[]{:S(2)}, u32[]{:S(2)}) collective-permute-start(bf16[128,5376]{1,0:T(8,128)(2,1)} %get-tuple-element.25.refs_1_), channel_id=1, source_target_pairs={{0,128},{128,0},{256,384},{384,256},{512,640},{640,512},{768,896},... | collective-permute-start | bytes 4128776 | tf_op jit(solution)/shard_map/ppermute | solution.py:378
  92.5 2.9 %collective-permute-done.refs_2_ = bf16[128,5376]{1,0:T(8,128)(2,1)S(1)} collective-permute-done((bf16[128,5376]{1,0:T(8,128)(2,1)}, bf16[128,5376]{1,0:T(8,128)(2,1)S(1)}, u32[]{:S(2)}, u32[]{:S(2)}) %collective-permute-start) | collective-permute-done | bytes 1376288 | tf_op jit(solution)/shard_map/ppermute | solution.py:378
  95.4 0.0 copy-start
  95.4 1.1 copy-done
  96.5 3.8 %shard_map.140 = (f32[576,384]{1,0:T(8,128)}, bf16[576,384]{1,0:T(8,128)(2,1)}, bf16[576,384]{1,0:T(8,128)(2,1)}, bf16[576,384]{1,0:T(8,128)(2,1)}) custom-call(s32[1]{0:T(128)} %bitcast.9.refs_0_, bf16[128,5376]{1,0:T(8,128)(2,1)} %get-tuple-element.25.refs_1_, bf16[128,5376]{1,0:T(8,128)(2,1)} %copy-done), custom_call_target="tpu_custom_call" | custom-call | tf_op jit(solution)/shard_map/pallas_call | solution.py:59
  100.3 14.4 %collective-permute-start.1 = (bf16[576,384]{1,0:T(8,128)(2,1)}, bf16[576,384]{1,0:T(8,128)(2,1)S(1)}, u32[]{:S(2)}, u32[]{:S(2)}) collective-permute-start(bf16[576,384]{1,0:T(8,128)(2,1)} %get-tuple-element.27), channel_id=1, source_target_pairs={{0,256},{128,384},{256,512},{384,640},{512,768},{640,896},{768,0},... | collective-permute-start | bytes 1327112 | tf_op jit(solution)/shard_map/ppermute | solution.py:397
  114.7 11.6 %collective-permute-start.2 = (bf16[576,384]{1,0:T(8,128)(2,1)}, bf16[576,384]{1,0:T(8,128)(2,1)S(1)}, u32[]{:S(2)}, u32[]{:S(2)}) collective-permute-start(bf16[576,384]{1,0:T(8,128)(2,1)} %get-tuple-element.28), channel_id=1, source_target_pairs={{0,512},{128,640},{256,768},{384,896},{512,0},{640,128},{768,256},... | collective-permute-start | bytes 1327112 | tf_op jit(solution)/shard_map/ppermute | solution.py:397
  126.3 1.9 %collective-permute-start.3 = (bf16[576,384]{1,0:T(8,128)(2,1)}, bf16[576,384]{1,0:T(8,128)(2,1)S(1)}, u32[]{:S(2)}, u32[]{:S(2)}) collective-permute-start(bf16[576,384]{1,0:T(8,128)(2,1)} %get-tuple-element.29), channel_id=1, source_target_pairs={{0,768},{128,896},{256,0},{384,128},{512,256},{640,384},{768,512},... | collective-permute-start | bytes 1327112 | tf_op jit(solution)/shard_map/ppermute | solution.py:397
  128.2 7.3 %all-to-all-start.2 = ((bf16[8,16,896]{2,1,0:T(8,128)(2,1)}), bf16[8,16,896]{2,1,0:T(8,128)(2,1)S(1)}, u32[]{:S(2)}, u32[]{:S(2)}) async-start(bf16[8,16,896]{2,1,0:T(8,128)(2,1)} %bitcast.7), calls=%async_computation.2 | async-start | bytes 458752 | tf_op jit(solution)/shard_map/all_to_all | solution.py:338
  135.5 0.6 pad_add_fusion.place
  136.1 9.1 %all-to-all-done.2 = bf16[8,16,896]{2,1,0:T(8,128)(2,1)S(1)} async-done(((bf16[8,16,896]{2,1,0:T(8,128)(2,1)}), bf16[8,16,896]{2,1,0:T(8,128)(2,1)S(1)}, u32[]{:S(2)}, u32[]{:S(2)}) %all-to-all-start.2) | async-done | bytes 229408 | tf_op jit(solution)/shard_map/all_to_all | solution.py:338
  145.2 0.0 copy-start.1
  145.2 0.7 copy-done.1
  145.9 2.1 %shard_map.139 = (bf16[16,384]{1,0:T(8,128)(2,1)}, bf16[16,384]{1,0:T(8,128)(2,1)}) custom-call(s32[2]{0:T(128)} %pad_add_fusion.place, bf16[128,896]{1,0:T(8,128)(2,1)} %bitcast.15, bf16[128,4736]{1,0:T(8,128)(2,1)} %bitcast.11, bf16[128,384]{1,0:T(8,128)(2,1)} %tokens.3, f32[1,384]{1,0:T(1,128)} %broadcast_in_dim.9.refs_1_.ln_gain, bf16[128,384]{1,0:T(8,128)(2,1)} %cotangent.3), custom_call_target="tpu_custom_call" | custom-call | tf_op jit(solution)/shard_map/pallas_call | solution.py:59
  148.0 0.0 collective-permute-done.1.refs_1_
  148.0 0.0 copy-start.2
  148.0 5.4 %collective-permute-done.2.refs_2_ = bf16[576,384]{1,0:T(8,128)(2,1)S(1)} collective-permute-done((bf16[576,384]{1,0:T(8,128)(2,1)}, bf16[576,384]{1,0:T(8,128)(2,1)S(1)}, u32[]{:S(2)}, u32[]{:S(2)}) %collective-permute-start.2) | collective-permute-done | bytes 442400 | tf_op jit(solution)/shard_map/ppermute | solution.py:397
  153.4 0.0 copy-start.3
  153.4 12.3 %collective-permute-done.3.refs_3_ = bf16[576,384]{1,0:T(8,128)(2,1)S(1)} collective-permute-done((bf16[576,384]{1,0:T(8,128)(2,1)}, bf16[576,384]{1,0:T(8,128)(2,1)S(1)}, u32[]{:S(2)}, u32[]{:S(2)}) %collective-permute-start.3) | collective-permute-done | bytes 442400 | tf_op jit(solution)/shard_map/ppermute | solution.py:397
  165.7 0.0 copy-start.4
  165.7 0.0 copy-done.2
  165.7 0.0 copy-done.3
  165.7 0.8 copy-done.4
  166.5 2.5 %shard_map.141 = (f32[3,1,48,384]{3,2,1,0:T(8,128)}, f32[1,48,1536]{2,1,0:T(8,128)}, f32[1,48,384]{2,1,0:T(8,128)}, f32[1,192,384]{2,1,0:T(8,128)}) custom-call(f32[576,384]{1,0:T(8,128)} %get-tuple-element.26.refs_0_, bf16[576,384]{1,0:T(8,128)(2,1)} %copy-done.2, bf16[576,384]{1,0:T(8,128)(2,1)} %copy-done.3, bf16[576,384]{1,0:T(8,128)(2,1)} %copy-done.4), custom_call_target="tpu_custom_call" | custom-call | tf_op jit(solution)/shard_map/pallas_call | solution.py:59
Async XLA Ops:
  80.0 15.4 %collective-permute-start = (bf16[128,5376]{1,0:T(8,128)(2,1)}, bf16[128,5376]{1,0:T(8,128)(2,1)S(1)}, u32[]{:S(2)}, u32[]{:S(2)}) collective-permute-start(bf16[128,5376]{1,0:T(8,128)(2,1)} %get-tuple-element.25.refs_1_), channel_id=1, source_target_pairs={{0,128},{128,0},{256,384},{384,256},{512,640},{640,512},{768,896},... | collective-permute-start | bytes 4128776 | tf_op jit(solution)/shard_map/ppermute | solution.py:378
  95.4 1.1 copy-start
  100.3 47.6 %collective-permute-start.1 = (bf16[576,384]{1,0:T(8,128)(2,1)}, bf16[576,384]{1,0:T(8,128)(2,1)S(1)}, u32[]{:S(2)}, u32[]{:S(2)}) collective-permute-start(bf16[576,384]{1,0:T(8,128)(2,1)} %get-tuple-element.27), channel_id=1, source_target_pairs={{0,256},{128,384},{256,512},{384,640},{512,768},{640,896},{768,0},... | collective-permute-start | bytes 1327112 | tf_op jit(solution)/shard_map/ppermute | solution.py:397
  114.7 38.7 %collective-permute-start.2 = (bf16[576,384]{1,0:T(8,128)(2,1)}, bf16[576,384]{1,0:T(8,128)(2,1)S(1)}, u32[]{:S(2)}, u32[]{:S(2)}) collective-permute-start(bf16[576,384]{1,0:T(8,128)(2,1)} %get-tuple-element.28), channel_id=1, source_target_pairs={{0,512},{128,640},{256,768},{384,896},{512,0},{640,128},{768,256},... | collective-permute-start | bytes 1327112 | tf_op jit(solution)/shard_map/ppermute | solution.py:397
  126.3 39.4 %collective-permute-start.3 = (bf16[576,384]{1,0:T(8,128)(2,1)}, bf16[576,384]{1,0:T(8,128)(2,1)S(1)}, u32[]{:S(2)}, u32[]{:S(2)}) collective-permute-start(bf16[576,384]{1,0:T(8,128)(2,1)} %get-tuple-element.29), channel_id=1, source_target_pairs={{0,768},{128,896},{256,0},{384,128},{512,256},{640,384},{768,512},... | collective-permute-start | bytes 1327112 | tf_op jit(solution)/shard_map/ppermute | solution.py:397
  128.2 17.0 %all-to-all-start.2 = ((bf16[8,16,896]{2,1,0:T(8,128)(2,1)}), bf16[8,16,896]{2,1,0:T(8,128)(2,1)S(1)}, u32[]{:S(2)}, u32[]{:S(2)}) async-start(bf16[8,16,896]{2,1,0:T(8,128)(2,1)} %bitcast.7), calls=%async_computation.2 | async-start | bytes 458752 | tf_op jit(solution)/shard_map/all_to_all | solution.py:338
  145.2 0.7 copy-start.1
  148.0 17.7 %copy-start.2 = (bf16[576,384]{1,0:T(8,128)(2,1)}, bf16[576,384]{1,0:T(8,128)(2,1)S(1)}, u32[]{:S(2)}) copy-start(bf16[576,384]{1,0:T(8,128)(2,1)S(1)} %collective-permute-done.1.refs_1_) | copy-start | bytes 1327108
  153.4 12.3 %copy-start.3 = (bf16[576,384]{1,0:T(8,128)(2,1)}, bf16[576,384]{1,0:T(8,128)(2,1)S(1)}, u32[]{:S(2)}) copy-start(bf16[576,384]{1,0:T(8,128)(2,1)S(1)} %collective-permute-done.2.refs_2_) | copy-start | bytes 1327108
  165.7 0.8 copy-start.4

commit v2 on v1

--- a/solution.py
+++ b/solution.py
@@ -47,34 +47,60 @@
     return jnp.sum(jnp.where(keep, block, 0.0), axis=-1, keepdims=True)
 
 
-def whole(count):
-    return [pl.BlockSpec(memory_space=pltpu.VMEM)] * count
-
-
-def run(kernel, operands, out_shape, scratch=(), scalar=False):
-    n_out = len(out_shape)
-    in_specs = whole(len(operands))
+def run(kernel, operands, out_shape, scratch=(), scalar=False, sent=(), fetched=(), mebibytes=16):
+    n_in, n_out, n_own = len(operands), len(out_shape), len(scratch)
+    in_specs = [pl.BlockSpec(memory_space=pltpu.VMEM)] * n_in
+    out_specs = [pl.BlockSpec(memory_space=pltpu.VMEM)] * n_out
     if scalar:
         in_specs[0] = pl.BlockSpec(memory_space=pltpu.SMEM)
+    for index in fetched:
+        in_specs[index] = pl.BlockSpec(memory_space=pltpu.HBM)
+    for index in sent:
+        out_specs[index] = pl.BlockSpec(memory_space=pltpu.HBM)
+    staging = [pltpu.VMEM(out_shape[index].shape, out_shape[index].dtype) for index in sent]
+    if sent:
+        staging.append(pltpu.SemaphoreType.DMA((len(sent),)))
+
+    def body(*refs):
+        outs = list(refs[n_in : n_in + n_out])
+        own = refs[n_in + n_out : n_in + n_out + n_own]
+        stage = refs[n_in + n_out + n_own :]
+        copies = []
+        for place, index in enumerate(sent):
+            copies.append(pltpu.make_async_copy(stage[place], outs[index], stage[-1].at[place]))
+            outs[index] = stage[place]
+        kernel(*refs[:n_in], *outs, *own)
+        for copy in copies:
+            copy.start()
+        for copy in copies:
+            copy.wait()
+
     return pl.pallas_call(
-        kernel,
+        body,
         in_specs=in_specs,
-        out_specs=whole(n_out),
+        out_specs=out_specs,
         out_shape=out_shape,
-        scratch_shapes=list(scratch),
-        compiler_params=pltpu.CompilerParams(vmem_limit_bytes=56 * 1024 * 1024),
+        scratch_shapes=list(scratch) + staging,
+        compiler_params=pltpu.CompilerParams(vmem_limit_bytes=mebibytes * 1024 * 1024),
     )(*operands)
 
 
-def project_kernel(share, tokens, ln_gain, w_qkv, w_hidden, w_attn, w_mlp, cotangent, out):
+def project_kernel(
+    share, tokens, ln_gain, w_qkv_far, w_hidden_far, w_attn_far, w_mlp_far, cotangent, out,
+    w_qkv, w_hidden, w_attn, w_mlp, arrived,
+):
     rows, width = tokens.shape
     head_width = w_qkv.shape[2]
     blocks = w_hidden.shape[1] // head_width
+    pairs = ((w_qkv_far, w_qkv), (w_hidden_far, w_hidden), (w_attn_far, w_attn), (w_mlp_far, w_mlp))
+    loads = [pltpu.make_async_copy(*pair, arrived.at[index]) for index, pair in enumerate(pairs)]
+    for load in loads:
+        load.start()
     values = tokens[...].astype(F32)
     mean = jnp.sum(values, axis=1, keepdims=True) / width
     centred = values - mean
     squares = jnp.sum(centred * centred, axis=1, keepdims=True)
-    gain = ln_gain[...]
+    gain = ln_gain[...][None]
     scaled = (centred * gain).astype(BF16)
     high, low = pieces(gain, 2)
     row_id = lax.broadcasted_iota(jnp.int32, (16, width), 0)
@@ -82,6 +108,8 @@
     share_id = lax.broadcasted_iota(jnp.int32, (share, head_width), 0)
     gain_sums = jnp.zeros((share, head_width), F32)
     for block in range(3 + blocks):
+        if block == 0 or block == 3:
+            loads[block // 3].wait()
         if block < 3:
             weight = w_qkv[block]
         else:
@@ -92,8 +120,10 @@
         gain_sums = jnp.where(share_id == block, both[0:1] + both[1:2], gain_sums)
     start = (3 + blocks) * head_width
     back = cotangent[...]
+    loads[2].wait()
     out[:, start : start + head_width] = dot_last(back, w_attn[...]).astype(BF16)
     start += head_width
+    loads[3].wait()
     for block in range(blocks):
         weight = w_mlp[block * head_width : (block + 1) * head_width, :]
         out[:, start : start + head_width] = dot_last(back, weight).astype(BF16)
@@ -168,7 +198,8 @@
     full, gain_sums, tokens, ln_gain, query_gain, key_gain, w_qkv, w_hidden, w_attn, w_mlp,
     cotangent, terms, acts,
 ):
-    head_size = query_gain.shape[1]
+    head_size = query_gain.shape[0]
+    query_row, key_row = query_gain[...][None], key_gain[...][None]
     head_width = w_qkv.shape[2]
     hidden_width = w_hidden.shape[1]
     local_width = tokens.shape[1]
@@ -176,7 +207,7 @@
     mean, inverse = from_lanes(stats, 0, 3), from_lanes(stats, 3, 3)
     plain_sum, hat_sum = from_lanes(stats, 6, 2), from_lanes(stats, 8, 2)
     normal_hat = (tokens[...].astype(F32) - mean) * inverse
-    acts[:, :local_width] = (normal_hat * ln_gain[...]).astype(BF16)
+    acts[:, :local_width] = (normal_hat * ln_gain[...][None]).astype(BF16)
     acts[:, local_width : 2 * local_width] = cotangent[...]
     hidden_at = 4 * head_width
     acts_hidden = 2 * local_width
@@ -203,8 +234,8 @@
         grad_mix = full[:, 3 * head_width + low : 3 * head_width + high]
         query_hat, query_root = normalise(query)
         key_hat, key_root = normalise(key)
-        query_norm = (query_hat * query_gain[...]).astype(BF16)
-        key_norm = (key_hat * key_gain[...]).astype(BF16)
+        query_norm = (query_hat * query_row).astype(BF16)
+        key_norm = (key_hat * key_row).astype(BF16)
         scores = dot_last(query_norm, key_norm) * scale
         weights = jnp.exp(scores - jnp.max(scores, axis=1, keepdims=True))
         probs = weights / jnp.sum(weights, axis=1, keepdims=True)
@@ -215,10 +246,10 @@
         grad_scores = probs * (grad_probs - jnp.sum(grad_probs * probs, axis=1, keepdims=True))
         grad_scores = grad_scores.astype(BF16)
         grad_query = back(
-            dot_plain(grad_scores, key_norm) * scale, query_hat, query_root, query_gain[...]
+            dot_plain(grad_scores, key_norm) * scale, query_hat, query_root, query_row
         )
         grad_key = back(
-            dot_first(grad_scores, query_norm) * scale, key_hat, key_root, key_gain[...]
+            dot_first(grad_scores, query_norm) * scale, key_hat, key_root, key_row
         )
         plain = jnp.zeros_like(query)
         with_hat = jnp.zeros_like(query)
@@ -245,9 +276,9 @@
 
 
 def weight_kernel(
-    head_width, hidden_width, n_dp, place, own, peer, first, *rest
+    head_width, hidden_width, n_dp, place, own, peer,
+    here, next_a, next_b, last_a, last_b, far_a, far_b, norm_t, mix_t, act_t,
 ):
-    others, (norm_t, mix_t, act_t) = rest[:-3], rest[-3:]
     local_width = norm_t.shape[0]
     hidden_at = 2 * local_width
     heads_at = hidden_at + 2 * hidden_width
@@ -258,10 +289,10 @@
     norm_t[...] = both(0, local_width).T
     mix_t[...] = both(heads_at, head_width).T
     act_t[...] = both(hidden_at, hidden_width).T
-    outs = (first,) + tuple(others)
-    chips = n_dp // 2
+    half = next_a.shape[0]
     core, chip = place[0] % 2, place[0] // 2
-    owners = [2 * ((chip + step) % chips) + core for step in range(chips)]
+    owners = [2 * ((chip + step) % (n_dp // 2)) + core for step in range(n_dp // 2)]
+    outs = ((next_a, next_b), (far_a, far_b), (last_a, last_b))
 
     def rows(ref, length):
         return jnp.concatenate(
@@ -272,10 +303,13 @@
 
     def emit(left, right):
         nonlocal row
-        length = left.shape[0] // chips
+        length = left.shape[0] // len(owners)
         product = dot_plain(left, right)
-        for step, out in enumerate(outs):
-            out[row : row + length, :] = product[step * length : (step + 1) * length].astype(out.dtype)
+        here[row : row + length, :] = product[:length]
+        for step, pair in enumerate(outs, 1):
+            start = row % half
+            out = pair[row // half]
+            out[start : start + length, :] = product[step * length : (step + 1) * length].astype(BF16)
         row += length
 
     norm_rows = rows(norm_t, local_width // n_dp)
@@ -288,6 +322,11 @@
     emit(rows(act_t, hidden_width // n_dp), cotangent)
 
 
+def relay_kernel(next_a, last_b, from_last, from_next, to_next, to_last):
+    to_next[...] = (next_a[...].astype(F32) + from_last[...].astype(F32)).astype(BF16)
+    to_last[...] = (last_b[...].astype(F32) + from_next[...].astype(F32)).astype(BF16)
+
+
 def token_kernel(place, got, full, tokens, ln_gain, cotangent, mixed, grad_tokens):
     out_rows, local_width = mixed.shape
     parts = got.shape[0] // out_rows
@@ -306,19 +345,20 @@
     sums = total(2 * local_width, LANES)
     share = 1.0 / width.astype(F32)
     mean_one, mean_two = from_lanes(sums, 0, 2) * share, from_lanes(sums, 2, 2) * share
-    grad_hat = total(local_width, local_width) * ln_gain[...]
+    grad_hat = total(local_width, local_width) * ln_gain[...][None]
     grad = inverse * (grad_hat - mean_one - normal_hat * mean_two)
     back = cotangent[pl.ds(first, out_rows), :].astype(F32)
     grad_tokens[...] = (back + grad).astype(BF16)
 
 
-def sum_kernel(*refs):
-    parts, (qkv, hidden, attn, mlp) = refs[:-4], refs[-4:]
+def sum_kernel(here, last_a, last_b, next_a, next_b, qkv, hidden, attn, mlp):
+    half = last_a.shape[0]
 
     def total(start, length):
-        value = parts[0][start : start + length, :].astype(F32)
-        for part in parts[1:]:
-            value = value + part[start : start + length, :].astype(F32)
+        pair = (last_a, next_a) if start < half else (last_b, next_b)
+        value = here[start : start + length, :]
+        for part in pair:
+            value = value + part[start % half : start % half + length, :].astype(F32)
         return value
 
     row = 0
@@ -346,15 +386,19 @@
     head_width, hidden_width = w_qkv.shape[2], w_hidden.shape[1]
     width = local_width * n_my
     share, out_rows = row_count // n_my, row_count // n_mx
-    ln_row, query_row, key_row = ln_gain[None], query_gain[None], key_gain[None]
+
+    weights = (w_qkv, w_hidden, w_attn_out, w_mlp_out)
 
     def shape(*dims, dtype=BF16):
         return jax.ShapeDtypeStruct(dims, dtype)
 
     (terms,) = run(
         lambda *refs: project_kernel(share, *refs),
-        (tokens, ln_row, w_qkv, w_hidden, w_attn_out, w_mlp_out, cotangent),
+        (tokens, ln_gain, *weights, cotangent),
         (shape(row_count, 5 * head_width + 2 * hidden_width + LANES),),
+        scratch=[pltpu.VMEM(array.shape, BF16) for array in weights] + [pltpu.SemaphoreType.DMA((4,))],
+        fetched=(2, 3, 4, 5),
+        mebibytes=56,
     )
     got = exchange(terms, "my")
     spread, gain_sums = run(
@@ -370,41 +414,47 @@
     out_terms, acts = run(
         attend_kernel,
         (
-            full, gain_sums, tokens, ln_row, query_row, key_row,
-            w_qkv, w_hidden, w_attn_out, w_mlp_out, cotangent,
+            full, gain_sums, tokens, ln_gain, query_gain, key_gain,
+            *weights, cotangent,
         ),
         (shape(row_count, 2 * local_width + LANES), shape(row_count, act_width)),
+        mebibytes=16,
     )
     peer_acts = lax.ppermute(acts, "dp", [(source, source ^ 1) for source in range(n_dp)])
     out_got = exchange(out_terms, "mx")
-    chips = n_dp // 2
     block_rows = (3 * local_width + local_width * hidden_width // head_width + head_width + hidden_width) // n_dp
+    halves = shape(block_rows // 2, local_width)
     place = lax.axis_index("dp").reshape(1)
-    sums = run(
+    here, next_a, next_b, last_a, last_b, far_a, far_b = run(
         lambda *refs: weight_kernel(head_width, hidden_width, n_dp, *refs),
         (place, acts, peer_acts),
-        tuple(shape(block_rows, local_width, dtype=BF16 if step else F32) for step in range(chips)),
+        (shape(block_rows, local_width, dtype=F32),) + (halves,) * 6,
         scratch=(
             pltpu.VMEM((local_width, 2 * row_count), BF16),
             pltpu.VMEM((head_width, 2 * row_count), BF16),
             pltpu.VMEM((hidden_width, 2 * row_count), BF16),
         ),
         scalar=True,
-    )
-    parts = [sums[0]]
-    for step in range(1, chips):
-        pairs = [(s, 2 * ((s // 2 + step) % chips) + s % 2) for s in range(n_dp)]
-        parts.append(lax.ppermute(sums[step], "dp", pairs))
+        mebibytes=60,
+    )
+
+    def pass_on(values, step):
+        return lax.ppermute(values, "dp", [(s, (s + 2 * step) % n_dp) for s in range(n_dp)])
+
+    from_last, from_next = pass_on(far_a, 1), pass_on(far_b, -1)
+    got_last_b, got_next_a = pass_on(next_b, 1), pass_on(last_a, -1)
+    to_next, to_last = run(relay_kernel, (next_a, last_b, from_last, from_next), (halves,) * 2)
+    got_last_a, got_next_b = pass_on(to_next, 1), pass_on(to_last, -1)
     place = jnp.stack([lax.axis_index("mx"), jnp.int32(width)])
     mixed, grad_tokens = run(
         token_kernel,
-        (place, out_got, full, tokens, ln_row, cotangent),
+        (place, out_got, full, tokens, ln_gain, cotangent),
         (shape(out_rows, local_width), shape(out_rows, local_width)),
         scalar=True,
     )
     grads = run(
         sum_kernel,
-        tuple(parts),
+        (here, got_last_a, got_last_b, got_next_a, got_next_b),
         (
             shape(3, 1, local_width // n_dp, head_width, dtype=F32),
             shape(1, local_width // n_dp, hidden_width, dtype=F32),

time: 170 us -> 153 us (0.900)
  the two profiles are of different devices: /device:TPU:1 before, /device:TPU:16 now
where the time goes in v2:
time: 153 us
  blocking collectives  79.5 us (52%)
  starting transfers between devices  43.2 us (28%)
  Pallas kernels  16.1 us (11%)
  waiting for transfers between devices  10.9 us (7%)
  local copies, waits for them, and re-layouts  1.92 us (1%)
    all_to_all x2, blocking collectives, exchange(): return lax.all_to_all(values, axis, 0, 0, tiled=True)  79.5 us
    ppermute x6, starting transfers between devices, pass_on(): lax.ppermute(values, 'dp', [(s, (s + 2 * step) % n_dp) for s in range(n_d...  33.4 us
    pallas_call x7, Pallas kernels, run(): pl.pallas_call(body, in_specs=in_specs, out_specs=out_specs, out_shape=ou...  16.1 us
    all_to_all x1, starting transfers between devices, exchange(): return lax.all_to_all(values, axis, 0, 0, tiled=True)  7.9 us
    ppermute x6, waiting for transfers between devices, pass_on(): lax.ppermute(values, 'dp', [(s, (s + 2 * step) % n_dp) for s in range(n_d...  7.72 us
    ppermute x1, waiting for transfers between devices, per_device(): lax.ppermute(acts, 'dp', [(source, source ^ 1) for source in range(n_dp)])  3.22 us
  transfers between devices with their start and end apart: 8, of which 3 were waited for; matrix products, arithmetic and copies ran while one was open for 0% of the time, Pallas kernels for 1%

profile of v2, /device:TPU:16, one launch (start us, length us, event | category | flops | bytes accessed | tf_op | source)
XLA Modules:
  0.0 152.6 jit_solution(9656752499014643688)
XLA Ops:
  0.6 5.1 %shard_map.136 = bf16[128,5120]{1,0:T(8,128)(2,1)} custom-call(bf16[128,384]{1,0:T(8,128)(2,1)} %refs_3_.5, f32[384]{0:T(512)} %refs_4_.5, bf16[3,384,384]{2,1,0:T(8,128)(2,1)} %refs_6_.3, bf16[384,1536]{1,0:T(8,128)(2,1)} %refs_7_.1, bf16[384,384]{1,0:T(8,128)(2,1)} %refs_8_.1, bf16[1536,384]{1,0:T(8,128)(2,1)} %refs_9_.1, bf16[128,384]{1,0:T(8,128)(2,1)} %refs_5_.5), custom_call_target="tpu_custom_call" | custom-call | tf_op jit(solution)/shard_map/pallas_call | solution.py:78
  5.8 44.2 %all_to_all.33 = bf16[16,8,5120]{2,1,0:T(8,128)(2,1)S(1)} all-to-all(bf16[16,8,5120]{2,1,0:T(8,128)(2,1)} %bitcast.13), channel_id=1, replica_groups=mesh['dp'=8,'mx'=8,'my'=16] {'my'}, dimensions={0} | all-to-all | bytes 2621440 | tf_op jit(solution)/shard_map/all_to_all | solution.py:378
  50.0 0.5 shard_map.137
  50.5 0.0 copy-start.1
  50.5 0.0 copy-start.10
  50.5 0.0 copy-start.11
  50.5 0.0 copy-start.12
  50.6 35.3 %all_to_all.34 = bf16[16,8,4736]{2,1,0:T(8,128)(2,1)S(1)} all-to-all(bf16[16,8,4736]{2,1,0:T(8,128)(2,1)S(1)} %bitcast.11), channel_id=1, replica_groups=mesh['dp'=8,'mx'=8,'my'=16] {'my'}, dimensions={0} | all-to-all | bytes 2424832 | tf_op jit(solution)/shard_map/all_to_all | solution.py:378
  86.0 3.8 %shard_map.138 = (bf16[128,896]{1,0:T(8,128)(2,1)}, bf16[128,5376]{1,0:T(8,128)(2,1)S(1)}) custom-call(bf16[128,4736]{1,0:T(8,128)(2,1)S(1)} %bitcast.8, f32[8,384]{1,0:T(8,128)S(1)} %get-tuple-element.26.refs_1_, bf16[128,384]{1,0:T(8,128)(2,1)S(1)} %copy-done.6, f32[384]{0:T(512)S(1)} %copy-done.10, f32[128]{0:T(128)S(1)} %copy-done.11, ...), custom_call_target="tpu_custom_call" | custom-call | tf_op jit(solution)/shard_map/pallas_call | solution.py:78
  89.7 1.9 %collective-permute-start = (bf16[128,5376]{1,0:T(8,128)(2,1)S(1)}, bf16[128,5376]{1,0:T(8,128)(2,1)}, u32[]{:S(2)}, u32[]{:S(2)}) collective-permute-start(bf16[128,5376]{1,0:T(8,128)(2,1)S(1)} %get-tuple-element.30.refs_1_), channel_id=1, source_target_pairs={{0,128},{128,0},{256,384},{384,256},{512,640},{640,512},{768,896},... | collective-permute-start | bytes 4128776 | tf_op jit(solution)/shard_map/ppermute | solution.py:423
  91.6 3.2 %collective-permute-done.refs_2_ = bf16[128,5376]{1,0:T(8,128)(2,1)} collective-permute-done((bf16[128,5376]{1,0:T(8,128)(2,1)S(1)}, bf16[128,5376]{1,0:T(8,128)(2,1)}, u32[]{:S(2)}, u32[]{:S(2)}) %collective-permute-start) | collective-permute-done | bytes 1376288 | tf_op jit(solution)/shard_map/ppermute | solution.py:423
  94.9 3.6 %shard_map.140 = (f32[576,384]{1,0:T(8,128)}, bf16[288,384]{1,0:T(8,128)(2,1)}, bf16[288,384]{1,0:T(8,128)(2,1)}, bf16[288,384]{1,0:T(8,128)(2,1)}, bf16[288,384...) custom-call(s32[1]{0:T(128)} %bitcast.7.refs_0_, bf16[128,5376]{1,0:T(8,128)(2,1)} %copy-done.3, ...), custom_call_target="tpu_custom_call" | custom-call | tf_op jit(solution)/shard_map/pallas_call | solution.py:78
  98.5 7.9 %collective-permute-start.1 = (bf16[288,384]{1,0:T(8,128)(2,1)}, bf16[288,384]{1,0:T(8,128)(2,1)S(1)}, u32[]{:S(2)}, u32[]{:S(2)}) collective-permute-start(bf16[288,384]{1,0:T(8,128)(2,1)} %get-tuple-element.34), channel_id=1, source_target_pairs={{0,256},{128,384},{256,512},{384,640},{512,768},{640,896},{768,0},... | collective-permute-start | bytes 663560 | tf_op jit(solution)/shard_map/ppermute | solution.py:442
  106.4 9.5 %collective-permute-start.2 = (bf16[288,384]{1,0:T(8,128)(2,1)}, bf16[288,384]{1,0:T(8,128)(2,1)S(1)}, u32[]{:S(2)}, u32[]{:S(2)}) collective-permute-start(bf16[288,384]{1,0:T(8,128)(2,1)} %get-tuple-element.35), channel_id=1, source_target_pairs={{0,768},{128,896},{256,0},{384,128},{512,256},{640,384},{768,512},... | collective-permute-start | bytes 663560 | tf_op jit(solution)/shard_map/ppermute | solution.py:442
  115.9 7.9 %all-to-all-start.2 = ((bf16[8,16,896]{2,1,0:T(8,128)(2,1)}), bf16[8,16,896]{2,1,0:T(8,128)(2,1)S(1)}, u32[]{:S(2)}, u32[]{:S(2)}) async-start(bf16[8,16,896]{2,1,0:T(8,128)(2,1)} %bitcast.5), calls=%async_computation.2 | async-start | bytes 458752 | tf_op jit(solution)/shard_map/all_to_all | solution.py:378
  123.8 2.0 %collective-permute-start.4 = (bf16[288,384]{1,0:T(8,128)(2,1)}, bf16[288,384]{1,0:T(8,128)(2,1)S(1)}, u32[]{:S(2)}, u32[]{:S(2)}) collective-permute-start(bf16[288,384]{1,0:T(8,128)(2,1)} %get-tuple-element.37), channel_id=1, source_target_pairs={{0,256},{128,384},{256,512},{384,640},{512,768},{640,896},{768,0},... | collective-permute-start | bytes 663560 | tf_op jit(solution)/shard_map/ppermute | solution.py:442
  125.9 6.0 %collective-permute-start.5 = (bf16[288,384]{1,0:T(8,128)(2,1)}, bf16[288,384]{1,0:T(8,128)(2,1)S(1)}, u32[]{:S(2)}, u32[]{:S(2)}) collective-permute-start(bf16[288,384]{1,0:T(8,128)(2,1)} %get-tuple-element.38), channel_id=1, source_target_pairs={{0,768},{128,896},{256,0},{384,128},{512,256},{640,384},{768,512},... | collective-permute-start | bytes 663560 | tf_op jit(solution)/shard_map/ppermute | solution.py:442
  131.9 0.0 collective-permute-done.1.refs_2_
  131.9 0.0 collective-permute-done.2.refs_3_
  131.9 0.0 copy-start.8
  132.0 0.9 copy-done.8
  132.9 0.9 copy-done.9
  133.8 0.8 shard_map.141
  134.6 1.9 %collective-permute-start.3 = (bf16[288,384]{1,0:T(8,128)(2,1)}, bf16[288,384]{1,0:T(8,128)(2,1)S(1)}, u32[]{:S(2)}, u32[]{:S(2)}) collective-permute-start(bf16[288,384]{1,0:T(8,128)(2,1)} %get-tuple-element.36), channel_id=1, source_target_pairs={{0,256},{128,384},{256,512},{384,640},{512,768},{640,896},{768,0},... | collective-permute-start | bytes 663560 | tf_op jit(solution)/shard_map/ppermute | solution.py:442
  136.6 6.0 %collective-permute-start.6 = (bf16[288,384]{1,0:T(8,128)(2,1)}, bf16[288,384]{1,0:T(8,128)(2,1)S(1)}, u32[]{:S(2)}, u32[]{:S(2)}) collective-permute-start(bf16[288,384]{1,0:T(8,128)(2,1)} %get-tuple-element.39), channel_id=1, source_target_pairs={{0,768},{128,896},{256,0},{384,128},{512,256},{640,384},{768,512},... | collective-permute-start | bytes 663560 | tf_op jit(solution)/shard_map/ppermute | solution.py:442
  142.6 0.1 pad_add_fusion.refs_0_
  142.7 1.2 shard_map.139
  143.9 0.0 collective-permute-done.4.refs_2_
  143.9 0.0 collective-permute-done.5.refs_3_
  143.9 4.6 %collective-permute-done.3.refs_1_ = bf16[288,384]{1,0:T(8,128)(2,1)S(1)} collective-permute-done((bf16[288,384]{1,0:T(8,128)(2,1)}, bf16[288,384]{1,0:T(8,128)(2,1)S(1)}, u32[]{:S(2)}, u32[]{:S(2)}) %collective-permute-start.3) | collective-permute-done | bytes 221216 | tf_op jit(solution)/shard_map/ppermute | solution.py:442
  148.5 3.1 %collective-permute-done.6.refs_4_ = bf16[288,384]{1,0:T(8,128)(2,1)S(1)} collective-permute-done((bf16[288,384]{1,0:T(8,128)(2,1)}, bf16[288,384]{1,0:T(8,128)(2,1)S(1)}, u32[]{:S(2)}, u32[]{:S(2)}) %collective-permute-start.6) | collective-permute-done | bytes 221216 | tf_op jit(solution)/shard_map/ppermute | solution.py:442
  151.6 1.0 shard_map.142
  (20 shorter events, 0.0 us)
Async XLA Ops:
  49.9 35.9 %copy-start.2 = (bf16[3,384,384]{2,1,0:T(8,128)(2,1)S(1)}, bf16[3,384,384]{2,1,0:T(8,128)(2,1)}, u32[]{:S(2)}) copy-start(bf16[3,384,384]{2,1,0:T(8,128)(2,1)} %refs_6_.3) | copy-start | bytes 2654212
  49.9 35.9 %copy-start.4 = (bf16[384,384]{1,0:T(8,128)(2,1)S(1)}, bf16[384,384]{1,0:T(8,128)(2,1)}, u32[]{:S(2)}) copy-start(bf16[384,384]{1,0:T(8,128)(2,1)} %refs_8_.1) | copy-start | bytes 884740
  49.9 35.9 %copy-start.6 = (bf16[128,384]{1,0:T(8,128)(2,1)S(1)}, bf16[128,384]{1,0:T(8,128)(2,1)}, u32[]{:S(2)}) copy-start(bf16[128,384]{1,0:T(8,128)(2,1)} %refs_3_.5) | copy-start | bytes 294916
  49.9 35.9 %copy-start.7 = (bf16[128,384]{1,0:T(8,128)(2,1)S(1)}, bf16[128,384]{1,0:T(8,128)(2,1)}, u32[]{:S(2)}) copy-start(bf16[128,384]{1,0:T(8,128)(2,1)} %refs_5_.5) | copy-start | bytes 294916
  50.5 35.4 %copy-start = (bf16[384,1536]{1,0:T(8,128)(2,1)S(1)}, bf16[384,1536]{1,0:T(8,128)(2,1)}, u32[]{:S(2)}) copy-start(bf16[384,1536]{1,0:T(8,128)(2,1)} %refs_7_.1) | copy-start | bytes 3538948
  50.5 35.4 %copy-start.1 = (bf16[1536,384]{1,0:T(8,128)(2,1)S(1)}, bf16[1536,384]{1,0:T(8,128)(2,1)}, u32[]{:S(2)}) copy-start(bf16[1536,384]{1,0:T(8,128)(2,1)} %refs_9_.1) | copy-start | bytes 3538948
  50.5 35.4 %copy-start.10 = (f32[384]{0:T(512)S(1)}, f32[384]{0:T(512)}, u32[]{:S(2)}) copy-start(f32[384]{0:T(512)} %refs_4_.5) | copy-start | bytes 4612
  50.5 35.4 %copy-start.11 = (f32[128]{0:T(128)S(1)}, f32[128]{0:T(128)}, u32[]{:S(2)}) copy-start(f32[128]{0:T(128)} %refs_4_.4) | copy-start | bytes 1540
  50.5 35.4 %copy-start.12 = (f32[128]{0:T(128)S(1)}, f32[128]{0:T(128)}, u32[]{:S(2)}) copy-start(f32[128]{0:T(128)} %refs_5_.4) | copy-start | bytes 1540
  89.7 5.1 %copy-start.3 = (bf16[128,5376]{1,0:T(8,128)(2,1)}, bf16[128,5376]{1,0:T(8,128)(2,1)S(1)}, u32[]{:S(2)}) copy-start(bf16[128,5376]{1,0:T(8,128)(2,1)S(1)} %get-tuple-element.30.refs_1_) | copy-start | bytes 4128772
  89.7 5.1 %collective-permute-start = (bf16[128,5376]{1,0:T(8,128)(2,1)S(1)}, bf16[128,5376]{1,0:T(8,128)(2,1)}, u32[]{:S(2)}, u32[]{:S(2)}) collective-permute-start(bf16[128,5376]{1,0:T(8,128)(2,1)S(1)} %get-tuple-element.30.refs_1_), channel_id=1, source_target_pairs={{0,128},{128,0},{256,384},{384,256},{512,640},{640,512},{768,896},... | collective-permute-start | bytes 4128776 | tf_op jit(solution)/shard_map/ppermute | solution.py:423
  98.5 33.4 %collective-permute-start.1 = (bf16[288,384]{1,0:T(8,128)(2,1)}, bf16[288,384]{1,0:T(8,128)(2,1)S(1)}, u32[]{:S(2)}, u32[]{:S(2)}) collective-permute-start(bf16[288,384]{1,0:T(8,128)(2,1)} %get-tuple-element.34), channel_id=1, source_target_pairs={{0,256},{128,384},{256,512},{384,640},{512,768},{640,896},{768,0},... | collective-permute-start | bytes 663560 | tf_op jit(solution)/shard_map/ppermute | solution.py:442
  106.4 25.5 %collective-permute-start.2 = (bf16[288,384]{1,0:T(8,128)(2,1)}, bf16[288,384]{1,0:T(8,128)(2,1)S(1)}, u32[]{:S(2)}, u32[]{:S(2)}) collective-permute-start(bf16[288,384]{1,0:T(8,128)(2,1)} %get-tuple-element.35), channel_id=1, source_target_pairs={{0,768},{128,896},{256,0},{384,128},{512,256},{640,384},{768,512},... | collective-permute-start | bytes 663560 | tf_op jit(solution)/shard_map/ppermute | solution.py:442
  115.9 26.7 %all-to-all-start.2 = ((bf16[8,16,896]{2,1,0:T(8,128)(2,1)}), bf16[8,16,896]{2,1,0:T(8,128)(2,1)S(1)}, u32[]{:S(2)}, u32[]{:S(2)}) async-start(bf16[8,16,896]{2,1,0:T(8,128)(2,1)} %bitcast.5), calls=%async_computation.2 | async-start | bytes 458752 | tf_op jit(solution)/shard_map/all_to_all | solution.py:378
  123.8 27.8 %copy-start.5 = (f32[576,384]{1,0:T(8,128)S(1)}, f32[576,384]{1,0:T(8,128)}, u32[]{:S(2)}) copy-start(f32[576,384]{1,0:T(8,128)} %get-tuple-element.31.refs_0_) | copy-start | bytes 2654212
  123.8 20.1 %collective-permute-start.4 = (bf16[288,384]{1,0:T(8,128)(2,1)}, bf16[288,384]{1,0:T(8,128)(2,1)S(1)}, u32[]{:S(2)}, u32[]{:S(2)}) collective-permute-start(bf16[288,384]{1,0:T(8,128)(2,1)} %get-tuple-element.37), channel_id=1, source_target_pairs={{0,256},{128,384},{256,512},{384,640},{512,768},{640,896},{768,0},... | collective-permute-start | bytes 663560 | tf_op jit(solution)/shard_map/ppermute | solution.py:442
  125.9 18.0 %collective-permute-start.5 = (bf16[288,384]{1,0:T(8,128)(2,1)}, bf16[288,384]{1,0:T(8,128)(2,1)S(1)}, u32[]{:S(2)}, u32[]{:S(2)}) collective-permute-start(bf16[288,384]{1,0:T(8,128)(2,1)} %get-tuple-element.38), channel_id=1, source_target_pairs={{0,768},{128,896},{256,0},{384,128},{512,256},{640,384},{768,512},... | collective-permute-start | bytes 663560 | tf_op jit(solution)/shard_map/ppermute | solution.py:442
  131.9 0.9 copy-start.8
  132.9 0.9 copy-start.9
  134.6 13.9 %collective-permute-start.3 = (bf16[288,384]{1,0:T(8,128)(2,1)}, bf16[288,384]{1,0:T(8,128)(2,1)S(1)}, u32[]{:S(2)}, u32[]{:S(2)}) collective-permute-start(bf16[288,384]{1,0:T(8,128)(2,1)} %get-tuple-element.36), channel_id=1, source_target_pairs={{0,256},{128,384},{256,512},{384,640},{512,768},{640,896},{768,0},... | collective-permute-start | bytes 663560 | tf_op jit(solution)/shard_map/ppermute | solution.py:442
  136.6 15.1 %collective-permute-start.6 = (bf16[288,384]{1,0:T(8,128)(2,1)}, bf16[288,384]{1,0:T(8,128)(2,1)S(1)}, u32[]{:S(2)}, u32[]{:S(2)}) collective-permute-start(bf16[288,384]{1,0:T(8,128)(2,1)} %get-tuple-element.39), channel_id=1, source_target_pairs={{0,768},{128,896},{256,0},{384,128},{512,256},{640,384},{768,512},... | collective-permute-start | bytes 663560 | tf_op jit(solution)/shard_map/ppermute | solution.py:442

commit v3 on v2

--- a/solution.py
+++ b/solution.py
@@ -47,7 +47,7 @@
     return jnp.sum(jnp.where(keep, block, 0.0), axis=-1, keepdims=True)
 
 
-def run(kernel, operands, out_shape, scratch=(), scalar=False, sent=(), fetched=(), mebibytes=16):
+def run(kernel, operands, out_shape, scratch=(), scalar=False, sent=(), fetched=(), mebibytes=16, work=None):
     n_in, n_out, n_own = len(operands), len(out_shape), len(scratch)
     in_specs = [pl.BlockSpec(memory_space=pltpu.VMEM)] * n_in
     out_specs = [pl.BlockSpec(memory_space=pltpu.VMEM)] * n_out
@@ -82,6 +82,7 @@
         out_shape=out_shape,
         scratch_shapes=list(scratch) + staging,
         compiler_params=pltpu.CompilerParams(vmem_limit_bytes=mebibytes * 1024 * 1024),
+        cost_estimate=work and pl.CostEstimate(flops=work, bytes_accessed=work, transcendentals=0),
     )(*operands)
 
 
@@ -105,6 +106,7 @@
     high, low = pieces(gain, 2)
     row_id = lax.broadcasted_iota(jnp.int32, (16, width), 0)
     gain_rows = jnp.where(row_id == 0, high, jnp.where(row_id == 1, low, 0.0)).astype(BF16)
+    left = jnp.concatenate([scaled, gain_rows], axis=0)
     share_id = lax.broadcasted_iota(jnp.int32, (share, head_width), 0)
     gain_sums = jnp.zeros((share, head_width), F32)
     for block in range(3 + blocks):
@@ -115,9 +117,10 @@
         else:
             weight = w_hidden[:, (block - 3) * head_width : (block - 2) * head_width]
         start = block * head_width
-        out[:, start : start + head_width] = dot_plain(scaled, weight).astype(BF16)
-        both = dot_plain(gain_rows, weight)
-        gain_sums = jnp.where(share_id == block, both[0:1] + both[1:2], gain_sums)
+        product = dot_plain(left, weight)
+        out[:, start : start + head_width] = product[:rows].astype(BF16)
+        both = product[rows : rows + 1] + product[rows + 1 : rows + 2]
+        gain_sums = jnp.where(share_id == block, both, gain_sums)
     start = (3 + blocks) * head_width
     back = cotangent[...]
     loads[2].wait()
@@ -322,7 +325,7 @@
     emit(rows(act_t, hidden_width // n_dp), cotangent)
 
 
-def relay_kernel(next_a, last_b, from_last, from_next, to_next, to_last):
+def relay_kernel(next_a, last_b, from_last, from_next, out_got, to_next, to_last):
     to_next[...] = (next_a[...].astype(F32) + from_last[...].astype(F32)).astype(BF16)
     to_last[...] = (last_b[...].astype(F32) + from_next[...].astype(F32)).astype(BF16)
 
@@ -443,7 +446,13 @@
 
     from_last, from_next = pass_on(far_a, 1), pass_on(far_b, -1)
     got_last_b, got_next_a = pass_on(next_b, 1), pass_on(last_a, -1)
-    to_next, to_last = run(relay_kernel, (next_a, last_b, from_last, from_next), (halves,) * 2)
+    to_next, to_last = run(
+        relay_kernel,
+        (next_a, last_b, from_last, from_next, out_got),
+        (halves,) * 2,
+        fetched=(4,),
+        mebibytes=16,
+    )
     got_last_a, got_next_b = pass_on(to_next, 1), pass_on(to_last, -1)
     place = jnp.stack([lax.axis_index("mx"), jnp.int32(width)])
     mixed, grad_tokens = run(

time: 153 us -> 153 us (level)
  the two profiles are of different devices: /device:TPU:16 before, /device:TPU:144 now
where the time goes in v3:
time: 153 us; the launch traced here: 152 us
  blocking collectives  76.8 us (50%)
  starting transfers between devices  43.7 us (29%)
  Pallas kernels  15.9 us (10%)
  waiting for transfers between devices  13.2 us (9%)
  local copies, waits for them, and re-layouts  1.92 us (1%)
    all_to_all x2, blocking collectives, exchange(): return lax.all_to_all(values, axis, 0, 0, tiled=True)  76.8 us
    ppermute x6, starting transfers between devices, pass_on(): lax.ppermute(values, 'dp', [(s, (s + 2 * step) % n_dp) for s in range(n_d...  33.9 us
    pallas_call x7, Pallas kernels, run(): pl.pallas_call(body, in_specs=in_specs, out_specs=out_specs, out_shape=ou...  15.9 us
    ppermute x6, waiting for transfers between devices, pass_on(): lax.ppermute(values, 'dp', [(s, (s + 2 * step) % n_dp) for s in range(n_d...  13.2 us
    all_to_all x1, starting transfers between devices, exchange(): return lax.all_to_all(values, axis, 0, 0, tiled=True)  7.9 us
  transfers between devices with their start and end apart: 8, of which 3 were waited for; matrix products, arithmetic and copies ran while one was open for 0% of the time, Pallas kernels for 4%

profile of v3, /device:TPU:144, one launch (start us, length us, event | category | flops | bytes accessed | tf_op | source)
XLA Modules:
  0.0 152.3 jit_solution(16180716154091413946)
XLA Ops:
  0.6 4.9 %shard_map.136 = bf16[128,5120]{1,0:T(8,128)(2,1)} custom-call(bf16[128,384]{1,0:T(8,128)(2,1)} %refs_3_.5, f32[384]{0:T(512)} %refs_4_.5, bf16[3,384,384]{2,1,0:T(8,128)(2,1)} %refs_6_.3, bf16[384,1536]{1,0:T(8,128)(2,1)} %refs_7_.1, bf16[384,384]{1,0:T(8,128)(2,1)} %refs_8_.1, bf16[1536,384]{1,0:T(8,128)(2,1)} %refs_9_.1, bf16[128,384]{1,0:T(8,128)(2,1)} %refs_5_.5), custom_call_target="tpu_custom_call" | custom-call | tf_op jit(solution)/shard_map/pallas_call | solution.py:78
  5.5 41.4 %all_to_all.33 = bf16[16,8,5120]{2,1,0:T(8,128)(2,1)S(1)} all-to-all(bf16[16,8,5120]{2,1,0:T(8,128)(2,1)} %bitcast.14), channel_id=1, replica_groups=mesh['dp'=8,'mx'=8,'my'=16] {'my'}, dimensions={0} | all-to-all | bytes 2621440 | tf_op jit(solution)/shard_map/all_to_all | solution.py:381
  46.9 0.5 shard_map.137
  47.5 0.0 copy-start.1
  47.5 0.0 copy-start.10
  47.5 0.0 copy-start.11
  47.5 0.0 copy-start.12
  47.5 35.4 %all_to_all.34 = bf16[16,8,4736]{2,1,0:T(8,128)(2,1)S(1)} all-to-all(bf16[16,8,4736]{2,1,0:T(8,128)(2,1)S(1)} %bitcast.13), channel_id=1, replica_groups=mesh['dp'=8,'mx'=8,'my'=16] {'my'}, dimensions={0} | all-to-all | bytes 2424832 | tf_op jit(solution)/shard_map/all_to_all | solution.py:381
  83.0 3.7 %shard_map.138 = (bf16[128,896]{1,0:T(8,128)(2,1)}, bf16[128,5376]{1,0:T(8,128)(2,1)S(1)}) custom-call(bf16[128,4736]{1,0:T(8,128)(2,1)S(1)} %bitcast.8, f32[8,384]{1,0:T(8,128)S(1)} %get-tuple-element.26.refs_1_, bf16[128,384]{1,0:T(8,128)(2,1)S(1)} %copy-done.6, f32[384]{0:T(512)S(1)} %copy-done.10, f32[128]{0:T(128)S(1)} %copy-done.11, ...), custom_call_target="tpu_custom_call" | custom-call | tf_op jit(solution)/shard_map/pallas_call | solution.py:78
  86.7 1.9 %collective-permute-start = (bf16[128,5376]{1,0:T(8,128)(2,1)S(1)}, bf16[128,5376]{1,0:T(8,128)(2,1)}, u32[]{:S(2)}, u32[]{:S(2)}) collective-permute-start(bf16[128,5376]{1,0:T(8,128)(2,1)S(1)} %get-tuple-element.30.refs_1_), channel_id=1, source_target_pairs={{0,128},{128,0},{256,384},{384,256},{512,640},{640,512},{768,896},... | collective-permute-start | bytes 4128776 | tf_op jit(solution)/shard_map/ppermute | solution.py:426
  88.7 7.9 %all-to-all-start.2 = ((bf16[8,16,896]{2,1,0:T(8,128)(2,1)}), bf16[8,16,896]{2,1,0:T(8,128)(2,1)S(1)}, u32[]{:S(2)}, u32[]{:S(2)}) async-start(bf16[8,16,896]{2,1,0:T(8,128)(2,1)} %bitcast.5), calls=%async_computation.2 | async-start | bytes 458752 | tf_op jit(solution)/shard_map/all_to_all | solution.py:381
  96.6 0.0 collective-permute-done.refs_2_
  96.6 3.6 %shard_map.140 = (f32[576,384]{1,0:T(8,128)}, bf16[288,384]{1,0:T(8,128)(2,1)}, bf16[288,384]{1,0:T(8,128)(2,1)}, bf16[288,384]{1,0:T(8,128)(2,1)}, bf16[288,384...) custom-call(s32[1]{0:T(128)} %bitcast.7.refs_0_, bf16[128,5376]{1,0:T(8,128)(2,1)} %copy-done.3, ...), custom_call_target="tpu_custom_call" | custom-call | tf_op jit(solution)/shard_map/pallas_call | solution.py:78
  100.2 7.9 %collective-permute-start.1 = (bf16[288,384]{1,0:T(8,128)(2,1)}, bf16[288,384]{1,0:T(8,128)(2,1)S(1)}, u32[]{:S(2)}, u32[]{:S(2)}) collective-permute-start(bf16[288,384]{1,0:T(8,128)(2,1)} %get-tuple-element.34), channel_id=1, source_target_pairs={{0,256},{128,384},{256,512},{384,640},{512,768},{640,896},{768,0},... | collective-permute-start | bytes 663560 | tf_op jit(solution)/shard_map/ppermute | solution.py:445
  108.1 9.5 %collective-permute-start.2 = (bf16[288,384]{1,0:T(8,128)(2,1)}, bf16[288,384]{1,0:T(8,128)(2,1)S(1)}, u32[]{:S(2)}, u32[]{:S(2)}) collective-permute-start(bf16[288,384]{1,0:T(8,128)(2,1)} %get-tuple-element.35), channel_id=1, source_target_pairs={{0,768},{128,896},{256,0},{384,128},{512,256},{640,384},{768,512},... | collective-permute-start | bytes 663560 | tf_op jit(solution)/shard_map/ppermute | solution.py:445
  117.6 1.9 %collective-permute-start.4 = (bf16[288,384]{1,0:T(8,128)(2,1)}, bf16[288,384]{1,0:T(8,128)(2,1)S(1)}, u32[]{:S(2)}, u32[]{:S(2)}) collective-permute-start(bf16[288,384]{1,0:T(8,128)(2,1)} %get-tuple-element.37), channel_id=1, source_target_pairs={{0,256},{128,384},{256,512},{384,640},{512,768},{640,896},{768,0},... | collective-permute-start | bytes 663560 | tf_op jit(solution)/shard_map/ppermute | solution.py:445
  119.6 6.0 %collective-permute-start.5 = (bf16[288,384]{1,0:T(8,128)(2,1)}, bf16[288,384]{1,0:T(8,128)(2,1)S(1)}, u32[]{:S(2)}, u32[]{:S(2)}) collective-permute-start(bf16[288,384]{1,0:T(8,128)(2,1)} %get-tuple-element.38), channel_id=1, source_target_pairs={{0,768},{128,896},{256,0},{384,128},{512,256},{640,384},{768,512},... | collective-permute-start | bytes 663560 | tf_op jit(solution)/shard_map/ppermute | solution.py:445
  125.6 0.0 all-to-all-done.2
  125.6 0.0 collective-permute-done.1.refs_2_
  125.6 7.1 %collective-permute-done.2.refs_3_ = bf16[288,384]{1,0:T(8,128)(2,1)S(1)} collective-permute-done((bf16[288,384]{1,0:T(8,128)(2,1)}, bf16[288,384]{1,0:T(8,128)(2,1)S(1)}, u32[]{:S(2)}, u32[]{:S(2)}) %collective-permute-start.2) | collective-permute-done | bytes 221216 | tf_op jit(solution)/shard_map/ppermute | solution.py:445
  132.7 0.9 copy-done.8
  133.7 0.9 copy-done.9
  134.6 0.8 shard_map.141
  135.4 1.9 %collective-permute-start.3 = (bf16[288,384]{1,0:T(8,128)(2,1)}, bf16[288,384]{1,0:T(8,128)(2,1)S(1)}, u32[]{:S(2)}, u32[]{:S(2)}) collective-permute-start(bf16[288,384]{1,0:T(8,128)(2,1)} %get-tuple-element.36), channel_id=1, source_target_pairs={{0,256},{128,384},{256,512},{384,640},{512,768},{640,896},{768,0},... | collective-permute-start | bytes 663560 | tf_op jit(solution)/shard_map/ppermute | solution.py:445
  137.3 6.6 %collective-permute-start.6 = (bf16[288,384]{1,0:T(8,128)(2,1)}, bf16[288,384]{1,0:T(8,128)(2,1)S(1)}, u32[]{:S(2)}, u32[]{:S(2)}) collective-permute-start(bf16[288,384]{1,0:T(8,128)(2,1)} %get-tuple-element.39), channel_id=1, source_target_pairs={{0,768},{128,896},{256,0},{384,128},{512,256},{640,384},{768,512},... | collective-permute-start | bytes 663560 | tf_op jit(solution)/shard_map/ppermute | solution.py:445
  143.9 0.1 pad_add_fusion.refs_0_
  144.0 1.2 shard_map.139
  145.3 0.0 collective-permute-done.4.refs_2_
  145.3 0.0 collective-permute-done.5.refs_3_
  145.3 0.9 collective-permute-done.3.refs_1_
  146.1 5.2 %collective-permute-done.6.refs_4_ = bf16[288,384]{1,0:T(8,128)(2,1)S(1)} collective-permute-done((bf16[288,384]{1,0:T(8,128)(2,1)}, bf16[288,384]{1,0:T(8,128)(2,1)S(1)}, u32[]{:S(2)}, u32[]{:S(2)}) %collective-permute-start.6) | collective-permute-done | bytes 221216 | tf_op jit(solution)/shard_map/ppermute | solution.py:445
  151.3 1.0 shard_map.142
  (20 shorter events, 0.0 us)
Async XLA Ops:
  46.9 36.0 %copy-start.2 = (bf16[3,384,384]{2,1,0:T(8,128)(2,1)S(1)}, bf16[3,384,384]{2,1,0:T(8,128)(2,1)}, u32[]{:S(2)}) copy-start(bf16[3,384,384]{2,1,0:T(8,128)(2,1)} %refs_6_.3) | copy-start | bytes 2654212
  46.9 36.0 %copy-start.4 = (bf16[384,384]{1,0:T(8,128)(2,1)S(1)}, bf16[384,384]{1,0:T(8,128)(2,1)}, u32[]{:S(2)}) copy-start(bf16[384,384]{1,0:T(8,128)(2,1)} %refs_8_.1) | copy-start | bytes 884740
  46.9 36.0 %copy-start.6 = (bf16[128,384]{1,0:T(8,128)(2,1)S(1)}, bf16[128,384]{1,0:T(8,128)(2,1)}, u32[]{:S(2)}) copy-start(bf16[128,384]{1,0:T(8,128)(2,1)} %refs_3_.5) | copy-start | bytes 294916
  46.9 36.0 %copy-start.7 = (bf16[128,384]{1,0:T(8,128)(2,1)S(1)}, bf16[128,384]{1,0:T(8,128)(2,1)}, u32[]{:S(2)}) copy-start(bf16[128,384]{1,0:T(8,128)(2,1)} %refs_5_.5) | copy-start | bytes 294916
  47.5 35.5 %copy-start = (bf16[384,1536]{1,0:T(8,128)(2,1)S(1)}, bf16[384,1536]{1,0:T(8,128)(2,1)}, u32[]{:S(2)}) copy-start(bf16[384,1536]{1,0:T(8,128)(2,1)} %refs_7_.1) | copy-start | bytes 3538948
  47.5 35.5 %copy-start.1 = (bf16[1536,384]{1,0:T(8,128)(2,1)S(1)}, bf16[1536,384]{1,0:T(8,128)(2,1)}, u32[]{:S(2)}) copy-start(bf16[1536,384]{1,0:T(8,128)(2,1)} %refs_9_.1) | copy-start | bytes 3538948
  47.5 35.5 %copy-start.10 = (f32[384]{0:T(512)S(1)}, f32[384]{0:T(512)}, u32[]{:S(2)}) copy-start(f32[384]{0:T(512)} %refs_4_.5) | copy-start | bytes 4612
  47.5 35.5 %copy-start.11 = (f32[128]{0:T(128)S(1)}, f32[128]{0:T(128)}, u32[]{:S(2)}) copy-start(f32[128]{0:T(128)} %refs_4_.4) | copy-start | bytes 1540
  47.5 35.5 %copy-start.12 = (f32[128]{0:T(128)S(1)}, f32[128]{0:T(128)}, u32[]{:S(2)}) copy-start(f32[128]{0:T(128)} %refs_5_.4) | copy-start | bytes 1540
  86.7 9.8 %copy-start.3 = (bf16[128,5376]{1,0:T(8,128)(2,1)}, bf16[128,5376]{1,0:T(8,128)(2,1)S(1)}, u32[]{:S(2)}) copy-start(bf16[128,5376]{1,0:T(8,128)(2,1)S(1)} %get-tuple-element.30.refs_1_) | copy-start | bytes 4128772
  86.7 9.8 %collective-permute-start = (bf16[128,5376]{1,0:T(8,128)(2,1)S(1)}, bf16[128,5376]{1,0:T(8,128)(2,1)}, u32[]{:S(2)}, u32[]{:S(2)}) collective-permute-start(bf16[128,5376]{1,0:T(8,128)(2,1)S(1)} %get-tuple-element.30.refs_1_), channel_id=1, source_target_pairs={{0,128},{128,0},{256,384},{384,256},{512,640},{640,512},{768,896},... | collective-permute-start | bytes 4128776 | tf_op jit(solution)/shard_map/ppermute | solution.py:426
  88.7 36.9 %all-to-all-start.2 = ((bf16[8,16,896]{2,1,0:T(8,128)(2,1)}), bf16[8,16,896]{2,1,0:T(8,128)(2,1)S(1)}, u32[]{:S(2)}, u32[]{:S(2)}) async-start(bf16[8,16,896]{2,1,0:T(8,128)(2,1)} %bitcast.5), calls=%async_computation.2 | async-start | bytes 458752 | tf_op jit(solution)/shard_map/all_to_all | solution.py:381
  100.2 25.4 %collective-permute-start.1 = (bf16[288,384]{1,0:T(8,128)(2,1)}, bf16[288,384]{1,0:T(8,128)(2,1)S(1)}, u32[]{:S(2)}, u32[]{:S(2)}) collective-permute-start(bf16[288,384]{1,0:T(8,128)(2,1)} %get-tuple-element.34), channel_id=1, source_target_pairs={{0,256},{128,384},{256,512},{384,640},{512,768},{640,896},{768,0},... | collective-permute-start | bytes 663560 | tf_op jit(solution)/shard_map/ppermute | solution.py:445
  108.1 24.6 %collective-permute-start.2 = (bf16[288,384]{1,0:T(8,128)(2,1)}, bf16[288,384]{1,0:T(8,128)(2,1)S(1)}, u32[]{:S(2)}, u32[]{:S(2)}) collective-permute-start(bf16[288,384]{1,0:T(8,128)(2,1)} %get-tuple-element.35), channel_id=1, source_target_pairs={{0,768},{128,896},{256,0},{384,128},{512,256},{640,384},{768,512},... | collective-permute-start | bytes 663560 | tf_op jit(solution)/shard_map/ppermute | solution.py:445
  117.6 27.6 %collective-permute-start.4 = (bf16[288,384]{1,0:T(8,128)(2,1)}, bf16[288,384]{1,0:T(8,128)(2,1)S(1)}, u32[]{:S(2)}, u32[]{:S(2)}) collective-permute-start(bf16[288,384]{1,0:T(8,128)(2,1)} %get-tuple-element.37), channel_id=1, source_target_pairs={{0,256},{128,384},{256,512},{384,640},{512,768},{640,896},{768,0},... | collective-permute-start | bytes 663560 | tf_op jit(solution)/shard_map/ppermute | solution.py:445
  119.6 25.7 %collective-permute-start.5 = (bf16[288,384]{1,0:T(8,128)(2,1)}, bf16[288,384]{1,0:T(8,128)(2,1)S(1)}, u32[]{:S(2)}, u32[]{:S(2)}) collective-permute-start(bf16[288,384]{1,0:T(8,128)(2,1)} %get-tuple-element.38), channel_id=1, source_target_pairs={{0,768},{128,896},{256,0},{384,128},{512,256},{640,384},{768,512},... | collective-permute-start | bytes 663560 | tf_op jit(solution)/shard_map/ppermute | solution.py:445
  132.7 0.9 copy-start.8
  133.7 0.9 copy-start.9
  134.6 16.7 %copy-start.5 = (f32[576,384]{1,0:T(8,128)S(1)}, f32[576,384]{1,0:T(8,128)}, u32[]{:S(2)}) copy-start(f32[576,384]{1,0:T(8,128)} %get-tuple-element.31.refs_0_) | copy-start | bytes 2654212
  135.4 10.7 %collective-permute-start.3 = (bf16[288,384]{1,0:T(8,128)(2,1)}, bf16[288,384]{1,0:T(8,128)(2,1)S(1)}, u32[]{:S(2)}, u32[]{:S(2)}) collective-permute-start(bf16[288,384]{1,0:T(8,128)(2,1)} %get-tuple-element.36), channel_id=1, source_target_pairs={{0,256},{128,384},{256,512},{384,640},{512,768},{640,896},{768,0},... | collective-permute-start | bytes 663560 | tf_op jit(solution)/shard_map/ppermute | solution.py:445
  137.3 14.0 %collective-permute-start.6 = (bf16[288,384]{1,0:T(8,128)(2,1)}, bf16[288,384]{1,0:T(8,128)(2,1)S(1)}, u32[]{:S(2)}, u32[]{:S(2)}) collective-permute-start(bf16[288,384]{1,0:T(8,128)(2,1)} %get-tuple-element.39), channel_id=1, source_target_pairs={{0,768},{128,896},{256,0},{384,128},{512,256},{640,384},{768,512},... | collective-permute-start | bytes 663560 | tf_op jit(solution)/shard_map/ppermute | solution.py:445

commit v4 on v1

--- a/solution.py
+++ b/solution.py
@@ -47,61 +47,83 @@
     return jnp.sum(jnp.where(keep, block, 0.0), axis=-1, keepdims=True)
 
 
-def whole(count):
-    return [pl.BlockSpec(memory_space=pltpu.VMEM)] * count
-
-
-def run(kernel, operands, out_shape, scratch=(), scalar=False):
-    n_out = len(out_shape)
-    in_specs = whole(len(operands))
+def run(kernel, operands, out_shape, scratch=(), scalar=False, fetched=(), written=(), mebibytes=16):
+    in_specs = [pl.BlockSpec(memory_space=pltpu.VMEM)] * len(operands)
+    out_specs = [pl.BlockSpec(memory_space=pltpu.VMEM)] * len(out_shape)
     if scalar:
         in_specs[0] = pl.BlockSpec(memory_space=pltpu.SMEM)
+    for index in fetched:
+        in_specs[index] = pl.BlockSpec(memory_space=pltpu.HBM)
+    for index in written:
+        out_specs[index] = pl.BlockSpec(memory_space=pltpu.HBM)
     return pl.pallas_call(
         kernel,
         in_specs=in_specs,
-        out_specs=whole(n_out),
+        out_specs=out_specs,
         out_shape=out_shape,
         scratch_shapes=list(scratch),
-        compiler_params=pltpu.CompilerParams(vmem_limit_bytes=56 * 1024 * 1024),
+        compiler_params=pltpu.CompilerParams(vmem_limit_bytes=mebibytes * 1024 * 1024),
     )(*operands)
 
 
-def project_kernel(share, tokens, ln_gain, w_qkv, w_hidden, w_attn, w_mlp, cotangent, out):
+def project_kernel(share, *refs):
+    far, out_far, near, out, arrived, left_for = refs[:7], refs[7], refs[8:15], refs[15], refs[16], refs[17]
+    tokens, ln_gain, w_qkv, w_hidden, cotangent, w_attn, w_mlp = near
     rows, width = tokens.shape
     head_width = w_qkv.shape[2]
     blocks = w_hidden.shape[1] // head_width
+    loads = [
+        pltpu.make_async_copy(source, target, arrived.at[index])
+        for index, (source, target) in enumerate(zip(far, near))
+    ]
+    for load in loads:
+        load.start()
+    sends = []
+
+    def emit(values):
+        columns = pl.ds(sum(send[1] for send in sends), values.shape[1])
+        out[:, columns] = values.astype(BF16)
+        copy = pltpu.make_async_copy(out.at[:, columns], out_far.at[:, columns], left_for.at[len(sends)])
+        copy.start()
+        sends.append((copy, values.shape[1]))
+
+    loads[0].wait()
+    loads[1].wait()
     values = tokens[...].astype(F32)
     mean = jnp.sum(values, axis=1, keepdims=True) / width
     centred = values - mean
     squares = jnp.sum(centred * centred, axis=1, keepdims=True)
-    gain = ln_gain[...]
+    gain = ln_gain[...][None]
     scaled = (centred * gain).astype(BF16)
     high, low = pieces(gain, 2)
     row_id = lax.broadcasted_iota(jnp.int32, (16, width), 0)
     gain_rows = jnp.where(row_id == 0, high, jnp.where(row_id == 1, low, 0.0)).astype(BF16)
+    left = jnp.concatenate([scaled, gain_rows], axis=0)
     share_id = lax.broadcasted_iota(jnp.int32, (share, head_width), 0)
     gain_sums = jnp.zeros((share, head_width), F32)
     for block in range(3 + blocks):
+        if block == 0 or block == 3:
+            loads[2 + block // 3].wait()
         if block < 3:
             weight = w_qkv[block]
         else:
             weight = w_hidden[:, (block - 3) * head_width : (block - 2) * head_width]
-        start = block * head_width
-        out[:, start : start + head_width] = dot_plain(scaled, weight).astype(BF16)
-        both = dot_plain(gain_rows, weight)
-        gain_sums = jnp.where(share_id == block, both[0:1] + both[1:2], gain_sums)
-    start = (3 + blocks) * head_width
+        product = dot_plain(left, weight)
+        emit(product[:rows])
+        both = product[rows : rows + 1] + product[rows + 1 : rows + 2]
+        gain_sums = jnp.where(share_id == block, both, gain_sums)
+    loads[4].wait()
+    loads[5].wait()
     back = cotangent[...]
-    out[:, start : start + head_width] = dot_last(back, w_attn[...]).astype(BF16)
-    start += head_width
+    emit(dot_last(back, w_attn[...]))
+    loads[6].wait()
     for block in range(blocks):
-        weight = w_mlp[block * head_width : (block + 1) * head_width, :]
-        out[:, start : start + head_width] = dot_last(back, weight).astype(BF16)
-        start += head_width
+        emit(dot_last(back, w_mlp[block * head_width : (block + 1) * head_width, :]))
     spread = jnp.broadcast_to(gain_sums[None], (rows // share, share, head_width))
-    out[:, start : start + head_width] = spread.reshape(rows, head_width).astype(BF16)
-    start += head_width
-    out[:, start : start + LANES] = to_lanes(pieces(mean, 3) + pieces(squares, 3)).astype(BF16)
+    emit(spread.reshape(rows, head_width))
+    emit(to_lanes(pieces(mean, 3) + pieces(squares, 3)))
+    for copy, _ in sends:
+        copy.wait()
 
 
 def share_kernel(head_width, local_width, got, out, sums_out):
@@ -168,7 +190,8 @@
     full, gain_sums, tokens, ln_gain, query_gain, key_gain, w_qkv, w_hidden, w_attn, w_mlp,
     cotangent, terms, acts,
 ):
-    head_size = query_gain.shape[1]
+    head_size = query_gain.shape[0]
+    query_row, key_row = query_gain[...][None], key_gain[...][None]
     head_width = w_qkv.shape[2]
     hidden_width = w_hidden.shape[1]
     local_width = tokens.shape[1]
@@ -176,7 +199,7 @@
     mean, inverse = from_lanes(stats, 0, 3), from_lanes(stats, 3, 3)
     plain_sum, hat_sum = from_lanes(stats, 6, 2), from_lanes(stats, 8, 2)
     normal_hat = (tokens[...].astype(F32) - mean) * inverse
-    acts[:, :local_width] = (normal_hat * ln_gain[...]).astype(BF16)
+    acts[:, :local_width] = (normal_hat * ln_gain[...][None]).astype(BF16)
     acts[:, local_width : 2 * local_width] = cotangent[...]
     hidden_at = 4 * head_width
     acts_hidden = 2 * local_width
@@ -203,8 +226,8 @@
         grad_mix = full[:, 3 * head_width + low : 3 * head_width + high]
         query_hat, query_root = normalise(query)
         key_hat, key_root = normalise(key)
-        query_norm = (query_hat * query_gain[...]).astype(BF16)
-        key_norm = (key_hat * key_gain[...]).astype(BF16)
+        query_norm = (query_hat * query_row).astype(BF16)
+        key_norm = (key_hat * key_row).astype(BF16)
         scores = dot_last(query_norm, key_norm) * scale
         weights = jnp.exp(scores - jnp.max(scores, axis=1, keepdims=True))
         probs = weights / jnp.sum(weights, axis=1, keepdims=True)
@@ -215,10 +238,10 @@
         grad_scores = probs * (grad_probs - jnp.sum(grad_probs * probs, axis=1, keepdims=True))
         grad_scores = grad_scores.astype(BF16)
         grad_query = back(
-            dot_plain(grad_scores, key_norm) * scale, query_hat, query_root, query_gain[...]
+            dot_plain(grad_scores, key_norm) * scale, query_hat, query_root, query_row
         )
         grad_key = back(
-            dot_first(grad_scores, query_norm) * scale, key_hat, key_root, key_gain[...]
+            dot_first(grad_scores, query_norm) * scale, key_hat, key_root, key_row
         )
         plain = jnp.zeros_like(query)
         with_hat = jnp.zeros_like(query)
@@ -245,12 +268,15 @@
 
 
 def weight_kernel(
-    head_width, hidden_width, n_dp, place, own, peer, first, *rest
+    head_width, hidden_width, n_dp, place, own, peer, here, far, relayed, direct, norm_t, mix_t, act_t,
 ):
-    others, (norm_t, mix_t, act_t) = rest[:-3], rest[-3:]
     local_width = norm_t.shape[0]
     hidden_at = 2 * local_width
     heads_at = hidden_at + 2 * hidden_width
+    core, chip, chips = place[0] % 2, place[0] // 2, n_dp // 2
+    toward = 1 - 2 * core
+    outs = (here, far, relayed, direct)
+    owners = [2 * ((chip + chips + step) % chips) + core for step in (0, 2, toward, -toward)]
 
     def both(start, length):
         return jnp.concatenate([own[:, start : start + length], peer[:, start : start + length]], axis=0)
@@ -258,11 +284,6 @@
     norm_t[...] = both(0, local_width).T
     mix_t[...] = both(heads_at, head_width).T
     act_t[...] = both(hidden_at, hidden_width).T
-    outs = (first,) + tuple(others)
-    chips = n_dp // 2
-    core, chip = place[0] % 2, place[0] // 2
-    owners = [2 * ((chip + step) % chips) + core for step in range(chips)]
-
     def rows(ref, length):
         return jnp.concatenate(
             [ref[pl.ds(pl.multiple_of(owner * length, 16), length), :] for owner in owners], axis=0
@@ -272,7 +293,7 @@
 
     def emit(left, right):
         nonlocal row
-        length = left.shape[0] // chips
+        length = left.shape[0] // len(owners)
         product = dot_plain(left, right)
         for step, out in enumerate(outs):
             out[row : row + length, :] = product[step * length : (step + 1) * length].astype(out.dtype)
@@ -306,18 +327,16 @@
     sums = total(2 * local_width, LANES)
     share = 1.0 / width.astype(F32)
     mean_one, mean_two = from_lanes(sums, 0, 2) * share, from_lanes(sums, 2, 2) * share
-    grad_hat = total(local_width, local_width) * ln_gain[...]
+    grad_hat = total(local_width, local_width) * ln_gain[...][None]
     grad = inverse * (grad_hat - mean_one - normal_hat * mean_two)
     back = cotangent[pl.ds(first, out_rows), :].astype(F32)
     grad_tokens[...] = (back + grad).astype(BF16)
 
 
-def sum_kernel(*refs):
-    parts, (qkv, hidden, attn, mlp) = refs[:-4], refs[-4:]
-
+def sum_kernel(here, relayed, direct, qkv, hidden, attn, mlp):
     def total(start, length):
-        value = parts[0][start : start + length, :].astype(F32)
-        for part in parts[1:]:
+        value = here[start : start + length, :]
+        for part in (relayed, direct):
             value = value + part[start : start + length, :].astype(F32)
         return value
 
@@ -346,15 +365,27 @@
     head_width, hidden_width = w_qkv.shape[2], w_hidden.shape[1]
     width = local_width * n_my
     share, out_rows = row_count // n_my, row_count // n_mx
-    ln_row, query_row, key_row = ln_gain[None], query_gain[None], key_gain[None]
+
+    weights = (w_qkv, w_hidden, w_attn_out, w_mlp_out)
 
     def shape(*dims, dtype=BF16):
         return jax.ShapeDtypeStruct(dims, dtype)
 
+    term_width = 5 * head_width + 2 * hidden_width + LANES
+    inputs = (tokens, ln_gain, w_qkv, w_hidden, cotangent, w_attn_out, w_mlp_out)
     (terms,) = run(
         lambda *refs: project_kernel(share, *refs),
-        (tokens, ln_row, w_qkv, w_hidden, w_attn_out, w_mlp_out, cotangent),
-        (shape(row_count, 5 * head_width + 2 * hidden_width + LANES),),
+        inputs,
+        (shape(row_count, term_width),),
+        scratch=[pltpu.VMEM(array.shape, array.dtype) for array in inputs]
+        + [
+            pltpu.VMEM((row_count, term_width), BF16),
+            pltpu.SemaphoreType.DMA((len(inputs),)),
+            pltpu.SemaphoreType.DMA((term_width // head_width + 1,)),
+        ],
+        fetched=range(len(inputs)),
+        written=(0,),
+        mebibytes=60,
     )
     got = exchange(terms, "my")
     spread, gain_sums = run(
@@ -370,41 +401,49 @@
     out_terms, acts = run(
         attend_kernel,
         (
-            full, gain_sums, tokens, ln_row, query_row, key_row,
-            w_qkv, w_hidden, w_attn_out, w_mlp_out, cotangent,
+            full, gain_sums, tokens, ln_gain, query_gain, key_gain,
+            *weights, cotangent,
         ),
         (shape(row_count, 2 * local_width + LANES), shape(row_count, act_width)),
+        mebibytes=16,
     )
     peer_acts = lax.ppermute(acts, "dp", [(source, source ^ 1) for source in range(n_dp)])
     out_got = exchange(out_terms, "mx")
-    chips = n_dp // 2
     block_rows = (3 * local_width + local_width * hidden_width // head_width + head_width + hidden_width) // n_dp
+    block = shape(block_rows, local_width)
     place = lax.axis_index("dp").reshape(1)
-    sums = run(
+    here, far, relayed, direct = run(
         lambda *refs: weight_kernel(head_width, hidden_width, n_dp, *refs),
         (place, acts, peer_acts),
-        tuple(shape(block_rows, local_width, dtype=BF16 if step else F32) for step in range(chips)),
+        (shape(block_rows, local_width, dtype=F32),) + (block,) * 3,
         scratch=(
             pltpu.VMEM((local_width, 2 * row_count), BF16),
             pltpu.VMEM((head_width, 2 * row_count), BF16),
             pltpu.VMEM((hidden_width, 2 * row_count), BF16),
         ),
         scalar=True,
-    )
-    parts = [sums[0]]
-    for step in range(1, chips):
-        pairs = [(s, 2 * ((s // 2 + step) % chips) + s % 2) for s in range(n_dp)]
-        parts.append(lax.ppermute(sums[step], "dp", pairs))
+        mebibytes=60,
+    )
+
+    def pass_on(values, step):
+        ways = [(s, (s + 2 * step * (1 - 2 * (s % 2))) % n_dp) for s in range(n_dp)]
+        return lax.ppermute(values, "dp", ways)
+
+    passing = pass_on(far, 1)
+    got_direct = pass_on(direct, -1)
+    passing, out_got = lax.optimization_barrier((passing, out_got))
+    joined = (relayed.astype(F32) + passing.astype(F32)).astype(BF16)
+    got_relayed = pass_on(joined, 1)
     place = jnp.stack([lax.axis_index("mx"), jnp.int32(width)])
     mixed, grad_tokens = run(
         token_kernel,
-        (place, out_got, full, tokens, ln_row, cotangent),
+        (place, out_got, full, tokens, ln_gain, cotangent),
         (shape(out_rows, local_width), shape(out_rows, local_width)),
         scalar=True,
     )
     grads = run(
         sum_kernel,
-        tuple(parts),
+        (here, got_relayed, got_direct),
         (
             shape(3, 1, local_width // n_dp, head_width, dtype=F32),
             shape(1, local_width // n_dp, hidden_width, dtype=F32),

time: 170 us -> 150 us (0.88)
  waiting for transfers between devices: 29.8 us -> 20.5 us
  Pallas kernels: 22.3 us -> 15.2 us
  local copies, waits for them, and re-layouts: 3.79 us -> 0.81 us
  starting transfers between devices: 47.6 us -> 45.2 us
    ppermute x3, waiting for transfers between devices: 17.7 us -> 10.5 us  [pass_on(): return lax.ppermute(values, 'dp', ways)]
    pallas_call x6, Pallas kernels: 22.3 us -> 15.2 us  [run(): pl.pallas_call(kernel, in_specs=in_specs, out_specs=out_specs, out_shape=...]
    all_to_all x1, waiting for transfers between devices: 9.1 us -> 7.07 us  [exchange(): return lax.all_to_all(values, axis, 0, 0, tiled=True)]
    unnamed x10 -> x24, local copies, waits for them, and re-layouts: 2.54 us -> 0.81 us
  transfers between devices with their start and end apart: 5 -> 5, of which waited for: 4 -> 4; matrix products, arithmetic and copies ran while one was open for 0% -> 1% of each run, Pallas kernels for 1% -> 1%
where the time goes in v4:
time: 150 us; the launch traced here: 149 us
  blocking collectives  65.2 us (43%)
  starting transfers between devices  45.2 us (30%)
  waiting for transfers between devices  20.5 us (14%)
  Pallas kernels  15.2 us (10%)
    all_to_all x2, blocking collectives, exchange(): return lax.all_to_all(values, axis, 0, 0, tiled=True)  65.2 us
    ppermute x3, starting transfers between devices, pass_on(): return lax.ppermute(values, 'dp', ways)  27 us
    pallas_call x6, Pallas kernels, run(): pl.pallas_call(kernel, in_specs=in_specs, out_specs=out_specs, out_shape=...  15.2 us
    ppermute x1, starting transfers between devices, per_device(): lax.ppermute(acts, 'dp', [(source, source ^ 1) for source in range(n_dp)])  10.9 us
    ppermute x3, waiting for transfers between devices, pass_on(): return lax.ppermute(values, 'dp', ways)  10.5 us
    all_to_all x1, starting transfers between devices, exchange(): return lax.all_to_all(values, axis, 0, 0, tiled=True)  7.28 us
    all_to_all x1, waiting for transfers between devices, exchange(): return lax.all_to_all(values, axis, 0, 0, tiled=True)  7.07 us
  transfers between devices with their start and end apart: 5, of which 4 were waited for; matrix products, arithmetic and copies ran while one was open for 1% of the time, Pallas kernels for 1%

profile of v4, /device:TPU:1, one launch (start us, length us, event | category | flops | bytes accessed | tf_op | source)
XLA Modules:
  0.0 149.0 jit_solution(3728068265650261421)
XLA Ops:
  0.6 3.8 %shard_map.136 = bf16[128,5120]{1,0:T(8,128)(2,1)} custom-call(bf16[128,384]{1,0:T(8,128)(2,1)} %tokens.3, f32[384]{0:T(512)} %ln_gain.3, bf16[3,384,384]{2,1,0:T(8,128)(2,1)} %w_qkv.1, bf16[384,1536]{1,0:T(8,128)(2,1)} %w_hidden.1, bf16[128,384]{1,0:T(8,128)(2,1)} %cotangent.3, bf16[384,384]{1,0:T(8,128)(2,1)} %w_attn.1, bf16[1536,384]{1,0:T(8,128)(2,1)} %w_mlp.1), custom_call_target="tpu_custom_call" | custom-call | tf_op jit(solution)/shard_map/pallas_call | solution.py:59
  4.4 36.8 %all_to_all.34 = bf16[16,8,5120]{2,1,0:T(8,128)(2,1)S(1)} all-to-all(bf16[16,8,5120]{2,1,0:T(8,128)(2,1)} %bitcast.13), channel_id=1, replica_groups=mesh['dp'=8,'mx'=8,'my'=16] {'my'}, dimensions={0} | all-to-all | bytes 2621440 | tf_op jit(solution)/shard_map/all_to_all | solution.py:357
  41.3 0.5 shard_map.137
  41.8 0.0 copy-start.1
  41.8 0.0 copy-start.8
  41.8 0.0 copy-start.9
  41.8 0.0 copy-start.10
  41.9 28.4 %all_to_all.35 = bf16[16,8,4736]{2,1,0:T(8,128)(2,1)S(1)} all-to-all(bf16[16,8,4736]{2,1,0:T(8,128)(2,1)S(1)} %bitcast.11), channel_id=1, replica_groups=mesh['dp'=8,'mx'=8,'my'=16] {'my'}, dimensions={0} | all-to-all | bytes 2424832 | tf_op jit(solution)/shard_map/all_to_all | solution.py:357
  70.3 0.0 copy-done.2
  70.3 0.0 copy-done.4
  70.3 0.0 copy-done.6
  70.3 0.0 copy-done.7
  70.3 0.0 copy-done
  70.3 0.0 copy-done.1
  70.3 3.7 %shard_map.138 = (bf16[128,896]{1,0:T(8,128)(2,1)}, bf16[128,5376]{1,0:T(8,128)(2,1)S(1)}) custom-call(bf16[128,4736]{1,0:T(8,128)(2,1)S(1)} %bitcast.8, f32[8,384]{1,0:T(8,128)S(1)} %get-tuple-element.23.gain_sums, bf16[128,384]{1,0:T(8,128)(2,1)S(1)} %copy-done.6, f32[384]{0:T(512)S(1)} %copy-done.8, f32[128]{0:T(128)S(1)} %copy-done.9, ...), custom_call_target="tpu_custom_call" | custom-call | tf_op jit(solution)/shard_map/pallas_call | solution.py:59
  74.1 10.9 %collective-permute-start = (bf16[128,5376]{1,0:T(8,128)(2,1)S(1)}, bf16[128,5376]{1,0:T(8,128)(2,1)}, u32[]{:S(2)}, u32[]{:S(2)}) collective-permute-start(bf16[128,5376]{1,0:T(8,128)(2,1)S(1)} %get-tuple-element.24.refs_1_), channel_id=1, source_target_pairs={{0,128},{128,0},{256,384},{384,256},{512,640},{640,512},{768,896},... | collective-permute-start | bytes 4128776 | tf_op jit(solution)/shard_map/ppermute | solution.py:410
  85.0 2.9 %collective-permute-done.refs_2_ = bf16[128,5376]{1,0:T(8,128)(2,1)} collective-permute-done((bf16[128,5376]{1,0:T(8,128)(2,1)S(1)}, bf16[128,5376]{1,0:T(8,128)(2,1)}, u32[]{:S(2)}, u32[]{:S(2)}) %collective-permute-start) | collective-permute-done | bytes 1376288 | tf_op jit(solution)/shard_map/ppermute | solution.py:410
  87.8 0.0 copy-done.3
  87.8 3.9 %shard_map.139 = (f32[576,384]{1,0:T(8,128)}, bf16[576,384]{1,0:T(8,128)(2,1)}, bf16[576,384]{1,0:T(8,128)(2,1)}, bf16[576,384]{1,0:T(8,128)(2,1)}) custom-call(s32[1]{0:T(128)} %bitcast.1.refs_0_, bf16[128,5376]{1,0:T(8,128)(2,1)} %copy-done.3, bf16[128,5376]{1,0:T(8,128)(2,1)} %collective-permute-done.refs_2_), custom_call_target="tpu_custom_call" | custom-call | tf_op jit(solution)/shard_map/pallas_call | solution.py:59
  91.7 22.0 %collective-permute-start.1 = (bf16[576,384]{1,0:T(8,128)(2,1)}, bf16[576,384]{1,0:T(8,128)(2,1)S(1)}, u32[]{:S(2)}, u32[]{:S(2)}) collective-permute-start(bf16[576,384]{1,0:T(8,128)(2,1)} %get-tuple-element.25), channel_id=1, source_target_pairs={{0,256},{128,896},{256,512},{384,128},{512,768},{640,384},{768,0},... | collective-permute-start | bytes 1327112 | tf_op jit(solution)/shard_map/ppermute | solution.py:430
  113.7 7.3 %all-to-all-start.2 = ((bf16[8,16,896]{2,1,0:T(8,128)(2,1)}), bf16[8,16,896]{2,1,0:T(8,128)(2,1)S(1)}, u32[]{:S(2)}, u32[]{:S(2)}) async-start(bf16[8,16,896]{2,1,0:T(8,128)(2,1)} %bitcast.6), calls=%async_computation.2 | async-start | bytes 458752 | tf_op jit(solution)/shard_map/all_to_all | solution.py:357
  121.0 1.9 %collective-permute-start.3 = (bf16[576,384]{1,0:T(8,128)(2,1)}, bf16[576,384]{1,0:T(8,128)(2,1)S(1)}, u32[]{:S(2)}, u32[]{:S(2)}) collective-permute-start(bf16[576,384]{1,0:T(8,128)(2,1)} %get-tuple-element.33), channel_id=1, source_target_pairs={{0,768},{128,384},{256,0},{384,640},{512,256},{640,896},{768,512},... | collective-permute-start | bytes 1327112 | tf_op jit(solution)/shard_map/ppermute | solution.py:430
  122.9 7.1 %all-to-all-done.2 = bf16[8,16,896]{2,1,0:T(8,128)(2,1)S(1)} async-done(((bf16[8,16,896]{2,1,0:T(8,128)(2,1)}), bf16[8,16,896]{2,1,0:T(8,128)(2,1)S(1)}, u32[]{:S(2)}, u32[]{:S(2)}) %all-to-all-start.2) | async-done | bytes 229408 | tf_op jit(solution)/shard_map/all_to_all | solution.py:357
  130.0 0.0 collective-permute-done.1
  130.0 0.8 copy-done.11
  130.8 1.3 add_convert_fusion
  132.1 3.1 %collective-permute-start.2 = (bf16[576,384]{1,0:T(8,128)(2,1)S(1)}, bf16[576,384]{1,0:T(8,128)(2,1)}, u32[]{:S(2)}, u32[]{:S(2)}) collective-permute-start(bf16[576,384]{1,0:T(8,128)(2,1)S(1)} %add_convert_fusion), channel_id=1, source_target_pairs={{0,256},{128,896},{256,512},{384,128},{512,768},{640,384},{768,0},... | collective-permute-start | bytes 1327112 | tf_op jit(solution)/shard_map/ppermute | solution.py:430
  135.2 0.1 pad_add_fusion.place
  135.3 1.2 shard_map.140
  136.5 0.7 collective-permute-done.3.direct
  137.2 9.9 %collective-permute-done.2.relayed = bf16[576,384]{1,0:T(8,128)(2,1)} collective-permute-done((bf16[576,384]{1,0:T(8,128)(2,1)S(1)}, bf16[576,384]{1,0:T(8,128)(2,1)}, u32[]{:S(2)}, u32[]{:S(2)}) %collective-permute-start.2) | collective-permute-done | bytes 442400 | tf_op jit(solution)/shard_map/ppermute | solution.py:430
  147.1 2.0 %shard_map.141 = (f32[3,1,48,384]{3,2,1,0:T(8,128)}, f32[1,48,1536]{2,1,0:T(8,128)}, f32[1,48,384]{2,1,0:T(8,128)}, f32[1,192,384]{2,1,0:T(8,128)}) custom-call(f32[576,384]{1,0:T(8,128)S(1)} %copy-done.5, bf16[576,384]{1,0:T(8,128)(2,1)} %collective-permute-done.2.relayed, bf16[576,384]{1,0:T(8,128)(2,1)S(1)} %collective-permute-done.3.direct), custom_call_target="tpu_custom_call" | custom-call | tf_op jit(solution)/shard_map/pallas_call | solution.py:59
  (12 shorter events, 0.0 us)
Async XLA Ops:
  41.2 29.0 %copy-start.2 = (bf16[3,384,384]{2,1,0:T(8,128)(2,1)S(1)}, bf16[3,384,384]{2,1,0:T(8,128)(2,1)}, u32[]{:S(2)}) copy-start(bf16[3,384,384]{2,1,0:T(8,128)(2,1)} %w_qkv.1) | copy-start | bytes 2654212
  41.3 29.0 %copy-start.4 = (bf16[384,384]{1,0:T(8,128)(2,1)S(1)}, bf16[384,384]{1,0:T(8,128)(2,1)}, u32[]{:S(2)}) copy-start(bf16[384,384]{1,0:T(8,128)(2,1)} %w_attn.1) | copy-start | bytes 884740
  41.3 29.0 %copy-start.6 = (bf16[128,384]{1,0:T(8,128)(2,1)S(1)}, bf16[128,384]{1,0:T(8,128)(2,1)}, u32[]{:S(2)}) copy-start(bf16[128,384]{1,0:T(8,128)(2,1)} %tokens.3) | copy-start | bytes 294916
  41.3 29.0 %copy-start.7 = (bf16[128,384]{1,0:T(8,128)(2,1)S(1)}, bf16[128,384]{1,0:T(8,128)(2,1)}, u32[]{:S(2)}) copy-start(bf16[128,384]{1,0:T(8,128)(2,1)} %cotangent.3) | copy-start | bytes 294916
  41.8 28.5 %copy-start = (bf16[384,1536]{1,0:T(8,128)(2,1)S(1)}, bf16[384,1536]{1,0:T(8,128)(2,1)}, u32[]{:S(2)}) copy-start(bf16[384,1536]{1,0:T(8,128)(2,1)} %w_hidden.1) | copy-start | bytes 3538948
  41.8 28.5 %copy-start.1 = (bf16[1536,384]{1,0:T(8,128)(2,1)S(1)}, bf16[1536,384]{1,0:T(8,128)(2,1)}, u32[]{:S(2)}) copy-start(bf16[1536,384]{1,0:T(8,128)(2,1)} %w_mlp.1) | copy-start | bytes 3538948
  41.8 28.5 %copy-start.8 = (f32[384]{0:T(512)S(1)}, f32[384]{0:T(512)}, u32[]{:S(2)}) copy-start(f32[384]{0:T(512)} %ln_gain.3) | copy-start | bytes 4612
  41.8 28.5 %copy-start.9 = (f32[128]{0:T(128)S(1)}, f32[128]{0:T(128)}, u32[]{:S(2)}) copy-start(f32[128]{0:T(128)} %query_gain.1) | copy-start | bytes 1540
  41.8 28.5 %copy-start.10 = (f32[128]{0:T(128)S(1)}, f32[128]{0:T(128)}, u32[]{:S(2)}) copy-start(f32[128]{0:T(128)} %key_gain.1) | copy-start | bytes 1540
  74.1 13.8 %copy-start.3 = (bf16[128,5376]{1,0:T(8,128)(2,1)}, bf16[128,5376]{1,0:T(8,128)(2,1)S(1)}, u32[]{:S(2)}) copy-start(bf16[128,5376]{1,0:T(8,128)(2,1)S(1)} %get-tuple-element.24.refs_1_) | copy-start | bytes 4128772
  74.1 13.8 %collective-permute-start = (bf16[128,5376]{1,0:T(8,128)(2,1)S(1)}, bf16[128,5376]{1,0:T(8,128)(2,1)}, u32[]{:S(2)}, u32[]{:S(2)}) collective-permute-start(bf16[128,5376]{1,0:T(8,128)(2,1)S(1)} %get-tuple-element.24.refs_1_), channel_id=1, source_target_pairs={{0,128},{128,0},{256,384},{384,256},{512,640},{640,512},{768,896},... | collective-permute-start | bytes 4128776 | tf_op jit(solution)/shard_map/ppermute | solution.py:410
  91.7 38.3 %collective-permute-start.1 = (bf16[576,384]{1,0:T(8,128)(2,1)}, bf16[576,384]{1,0:T(8,128)(2,1)S(1)}, u32[]{:S(2)}, u32[]{:S(2)}) collective-permute-start(bf16[576,384]{1,0:T(8,128)(2,1)} %get-tuple-element.25), channel_id=1, source_target_pairs={{0,256},{128,896},{256,512},{384,128},{512,768},{640,384},{768,0},... | collective-permute-start | bytes 1327112 | tf_op jit(solution)/shard_map/ppermute | solution.py:430
  113.7 16.3 %all-to-all-start.2 = ((bf16[8,16,896]{2,1,0:T(8,128)(2,1)}), bf16[8,16,896]{2,1,0:T(8,128)(2,1)S(1)}, u32[]{:S(2)}, u32[]{:S(2)}) async-start(bf16[8,16,896]{2,1,0:T(8,128)(2,1)} %bitcast.6), calls=%async_computation.2 | async-start | bytes 458752 | tf_op jit(solution)/shard_map/all_to_all | solution.py:357
  121.0 16.2 %collective-permute-start.3 = (bf16[576,384]{1,0:T(8,128)(2,1)}, bf16[576,384]{1,0:T(8,128)(2,1)S(1)}, u32[]{:S(2)}, u32[]{:S(2)}) collective-permute-start(bf16[576,384]{1,0:T(8,128)(2,1)} %get-tuple-element.33), channel_id=1, source_target_pairs={{0,768},{128,384},{256,0},{384,640},{512,256},{640,896},{768,512},... | collective-permute-start | bytes 1327112 | tf_op jit(solution)/shard_map/ppermute | solution.py:430
  130.0 0.8 copy-start.11
  130.8 16.3 %copy-start.5 = (f32[576,384]{1,0:T(8,128)S(1)}, f32[576,384]{1,0:T(8,128)}, u32[]{:S(2)}) copy-start(f32[576,384]{1,0:T(8,128)} %get-tuple-element.30.here) | copy-start | bytes 2654212
  132.1 15.0 %collective-permute-start.2 = (bf16[576,384]{1,0:T(8,128)(2,1)S(1)}, bf16[576,384]{1,0:T(8,128)(2,1)}, u32[]{:S(2)}, u32[]{:S(2)}) collective-permute-start(bf16[576,384]{1,0:T(8,128)(2,1)S(1)} %add_convert_fusion), channel_id=1, source_target_pairs={{0,256},{128,896},{256,512},{384,128},{512,768},{640,384},{768,0},... | collective-permute-start | bytes 1327112 | tf_op jit(solution)/shard_map/ppermute | solution.py:430

commit v5 on v4

--- a/solution.py
+++ b/solution.py
@@ -268,28 +268,47 @@
 
 
 def weight_kernel(
-    head_width, hidden_width, n_dp, place, own, peer, here, far, relayed, direct, norm_t, mix_t, act_t,
+    head_width, hidden_width, n_dp, place, own, peer, here_far, far_far, relayed_far, direct_far,
+    acts, norm_t, mix_t, act_t, here, far, relayed, direct, arrived, left_for,
 ):
-    local_width = norm_t.shape[0]
+    row_count, local_width = own.shape[0], norm_t.shape[0]
     hidden_at = 2 * local_width
     heads_at = hidden_at + 2 * hidden_width
     core, chip, chips = place[0] % 2, place[0] // 2, n_dp // 2
     toward = 1 - 2 * core
-    outs = (here, far, relayed, direct)
-    owners = [2 * ((chip + chips + step) % chips) + core for step in (0, 2, toward, -toward)]
+    outs = (far, relayed, direct, here)
+    outs_far = (far_far, relayed_far, direct_far, here_far)
+    owners = [2 * ((chip + chips + step) % chips) + core for step in (2, toward, -toward, 0)]
+    spans = (
+        (0, local_width),
+        (heads_at + head_width, 3 * head_width),
+        (hidden_at + hidden_width, hidden_width),
+        (hidden_at, hidden_width),
+        (local_width, local_width),
+        (heads_at, head_width),
+    )
+    loads = []
+    for index, (start, length) in enumerate(spans):
+        columns = pl.ds(start, length)
+        for side, source in enumerate((own, peer)):
+            target = acts.at[pl.ds(side * row_count, row_count), columns]
+            load = pltpu.make_async_copy(source.at[:, columns], target, arrived.at[2 * index + side])
+            load.start()
+            loads.append(load)
+
+    def ready(index):
+        loads[2 * index].wait()
+        loads[2 * index + 1].wait()
 
     def both(start, length):
-        return jnp.concatenate([own[:, start : start + length], peer[:, start : start + length]], axis=0)
-
-    norm_t[...] = both(0, local_width).T
-    mix_t[...] = both(heads_at, head_width).T
-    act_t[...] = both(hidden_at, hidden_width).T
+        return acts[:, start : start + length]
+
     def rows(ref, length):
         return jnp.concatenate(
             [ref[pl.ds(pl.multiple_of(owner * length, 16), length), :] for owner in owners], axis=0
         )
 
-    row = 0
+    row, sent, sends = 0, 0, []
 
     def emit(left, right):
         nonlocal row
@@ -299,14 +318,36 @@
             out[row : row + length, :] = product[step * length : (step + 1) * length].astype(out.dtype)
         row += length
 
+    def send():
+        nonlocal sent
+        part = pl.ds(sent, row - sent)
+        for out, out_far in zip(outs, outs_far):
+            copy = pltpu.make_async_copy(out.at[part, :], out_far.at[part, :], left_for.at[len(sends)])
+            copy.start()
+            sends.append(copy)
+        sent = row
+
+    ready(0)
+    norm_t[...] = both(0, local_width).T
     norm_rows = rows(norm_t, local_width // n_dp)
+    ready(1)
     for part in range(3):
         emit(norm_rows, both(heads_at + (1 + part) * head_width, head_width))
+    send()
+    ready(2)
     for block in range(hidden_width // head_width):
         emit(norm_rows, both(hidden_at + hidden_width + block * head_width, head_width))
+    send()
+    for index in (3, 4, 5):
+        ready(index)
+    mix_t[...] = both(heads_at, head_width).T
+    act_t[...] = both(hidden_at, hidden_width).T
     cotangent = both(local_width, local_width)
     emit(rows(mix_t, head_width // n_dp), cotangent)
     emit(rows(act_t, hidden_width // n_dp), cotangent)
+    send()
+    for copy in sends:
+        copy.wait()
 
 
 def token_kernel(place, got, full, tokens, ln_gain, cotangent, mixed, grad_tokens):
@@ -333,24 +374,39 @@
     grad_tokens[...] = (back + grad).astype(BF16)
 
 
-def sum_kernel(here, relayed, direct, qkv, hidden, attn, mlp):
-    def total(start, length):
-        value = here[start : start + length, :]
+def sum_kernel(
+    here, relayed, direct, qkv_far, hidden_far, attn_far, mlp_far, qkv, hidden, attn, mlp, left_for
+):
+    length, head_width = qkv.shape[2], qkv.shape[3]
+    blocks = hidden.shape[2] // head_width
+    cuts = (0, 3 * length, (3 + blocks) * length, here.shape[0])
+
+    def total(start, count):
+        value = here[start : start + count, :]
         for part in (relayed, direct):
-            value = value + part[start : start + length, :].astype(F32)
+            value = value + part[start : start + count, :].astype(F32)
         return value
 
-    row = 0
-    length, head_width = qkv.shape[2], qkv.shape[3]
+    sends = []
+
+    def send(source, target):
+        copy = pltpu.make_async_copy(source, target, left_for.at[len(sends)])
+        copy.start()
+        sends.append(copy)
+
     for part in range(3):
-        qkv[part, 0] = total(row, length)
-        row += length
-    for block in range(hidden.shape[2] // head_width):
-        hidden[0, :, block * head_width : (block + 1) * head_width] = total(row, length)
-        row += length
-    attn[0] = total(row, attn.shape[1])
-    row += attn.shape[1]
-    mlp[0] = total(row, mlp.shape[1])
+        qkv[part, 0] = total(part * length, length)
+    send(qkv, qkv_far)
+    for block in range(blocks):
+        columns = slice(block * head_width, (block + 1) * head_width)
+        hidden[0, :, columns] = total(cuts[1] + block * length, length)
+    send(hidden, hidden_far)
+    attn[0] = total(cuts[2], attn.shape[1])
+    send(attn, attn_far)
+    mlp[0] = total(cuts[2] + attn.shape[1], mlp.shape[1])
+    send(mlp, mlp_far)
+    for copy in sends:
+        copy.wait()
 
 
 def exchange(values, axis):
@@ -412,16 +468,23 @@
     block_rows = (3 * local_width + local_width * hidden_width // head_width + head_width + hidden_width) // n_dp
     block = shape(block_rows, local_width)
     place = lax.axis_index("dp").reshape(1)
+    weight_outs = (shape(block_rows, local_width, dtype=F32),) + (block,) * 3
     here, far, relayed, direct = run(
         lambda *refs: weight_kernel(head_width, hidden_width, n_dp, *refs),
         (place, acts, peer_acts),
-        (shape(block_rows, local_width, dtype=F32),) + (block,) * 3,
-        scratch=(
+        weight_outs,
+        scratch=[
+            pltpu.VMEM((2 * row_count, act_width), BF16),
             pltpu.VMEM((local_width, 2 * row_count), BF16),
             pltpu.VMEM((head_width, 2 * row_count), BF16),
             pltpu.VMEM((hidden_width, 2 * row_count), BF16),
-        ),
+            *(pltpu.VMEM(out.shape, out.dtype) for out in weight_outs),
+            pltpu.SemaphoreType.DMA((12,)),
+            pltpu.SemaphoreType.DMA((12,)),
+        ],
         scalar=True,
+        fetched=(1, 2),
+        written=(0, 1, 2, 3),
         mebibytes=60,
     )
 
@@ -431,8 +494,8 @@
 
     passing = pass_on(far, 1)
     got_direct = pass_on(direct, -1)
-    passing, out_got = lax.optimization_barrier((passing, out_got))
     joined = (relayed.astype(F32) + passing.astype(F32)).astype(BF16)
+    joined, out_got = lax.optimization_barrier((joined, out_got))
     got_relayed = pass_on(joined, 1)
     place = jnp.stack([lax.axis_index("mx"), jnp.int32(width)])
     mixed, grad_tokens = run(
@@ -441,15 +504,18 @@
         (shape(out_rows, local_width), shape(out_rows, local_width)),
         scalar=True,
     )
+    grad_shapes = (
+        shape(3, 1, local_width // n_dp, head_width, dtype=F32),
+        shape(1, local_width // n_dp, hidden_width, dtype=F32),
+        shape(1, head_width // n_dp, local_width, dtype=F32),
+        shape(1, hidden_width // n_dp, local_width, dtype=F32),
+    )
     grads = run(
         sum_kernel,
         (here, got_relayed, got_direct),
-        (
-            shape(3, 1, local_width // n_dp, head_width, dtype=F32),
-            shape(1, local_width // n_dp, hidden_width, dtype=F32),
-            shape(1, head_width // n_dp, local_width, dtype=F32),
-            shape(1, hidden_width // n_dp, local_width, dtype=F32),
-        ),
+        grad_shapes,
+        scratch=[pltpu.VMEM(grad.shape, grad.dtype) for grad in grad_shapes] + [pltpu.SemaphoreType.DMA((4,))],
+        written=(0, 1, 2, 3),
     )
     return (mixed, grad_tokens, *grads)
 

time: 150 us -> 148 us (0.987)
  the two profiles are of different devices: /device:TPU:1 before, /device:TPU:32 now
where the time goes in v5:
time: 148 us
  blocking collectives  79.5 us (54%)
  starting transfers between devices  29.2 us (20%)
  waiting for transfers between devices  21 us (14%)
  Pallas kernels  14.9 us (10%)
    all_to_all x2, blocking collectives, exchange(): return lax.all_to_all(values, axis, 0, 0, tiled=True)  79.5 us
    ppermute x3, starting transfers between devices, pass_on(): return lax.ppermute(values, 'dp', ways)  19.6 us
    ppermute x3, waiting for transfers between devices, pass_on(): return lax.ppermute(values, 'dp', ways)  17.8 us
    pallas_call x6, Pallas kernels, run(): pl.pallas_call(kernel, in_specs=in_specs, out_specs=out_specs, out_shape=...  14.9 us
    all_to_all x1, starting transfers between devices, exchange(): return lax.all_to_all(values, axis, 0, 0, tiled=True)  7.67 us
    ppermute x1, waiting for transfers between devices, per_device(): lax.ppermute(acts, 'dp', [(source, source ^ 1) for source in range(n_dp)])  3.22 us
  transfers between devices with their start and end apart: 5, of which 4 were waited for; matrix products, arithmetic and copies ran while one was open for 1% of the time, Pallas kernels for 1%

profile of v5, /device:TPU:32, one launch (start us, length us, event | category | flops | bytes accessed | tf_op | source)
XLA Modules:
  0.0 147.5 jit_solution(4035813407206825012)
XLA Ops:
  0.6 3.8 %shard_map.136 = bf16[128,5120]{1,0:T(8,128)(2,1)} custom-call(bf16[128,384]{1,0:T(8,128)(2,1)} %tokens.3, f32[384]{0:T(512)} %ln_gain.3, bf16[3,384,384]{2,1,0:T(8,128)(2,1)} %w_qkv.1, bf16[384,1536]{1,0:T(8,128)(2,1)} %w_hidden.1, bf16[128,384]{1,0:T(8,128)(2,1)} %cotangent.3, bf16[384,384]{1,0:T(8,128)(2,1)} %w_attn.1, bf16[1536,384]{1,0:T(8,128)(2,1)} %w_mlp.1), custom_call_target="tpu_custom_call" | custom-call | tf_op jit(solution)/shard_map/pallas_call | solution.py:59
  4.4 44.2 %all_to_all.34 = bf16[16,8,5120]{2,1,0:T(8,128)(2,1)S(1)} all-to-all(bf16[16,8,5120]{2,1,0:T(8,128)(2,1)} %bitcast.13), channel_id=1, replica_groups=mesh['dp'=8,'mx'=8,'my'=16] {'my'}, dimensions={0} | all-to-all | bytes 2621440 | tf_op jit(solution)/shard_map/all_to_all | solution.py:413
  48.6 0.5 shard_map.137
  49.2 0.0 copy-start.1
  49.2 0.0 copy-start.8
  49.2 0.0 copy-start.9
  49.2 0.0 copy-start.10
  49.2 35.3 %all_to_all.35 = bf16[16,8,4736]{2,1,0:T(8,128)(2,1)S(1)} all-to-all(bf16[16,8,4736]{2,1,0:T(8,128)(2,1)S(1)} %bitcast.11), channel_id=1, replica_groups=mesh['dp'=8,'mx'=8,'my'=16] {'my'}, dimensions={0} | all-to-all | bytes 2424832 | tf_op jit(solution)/shard_map/all_to_all | solution.py:413
  84.6 0.0 copy-done.2
  84.6 0.0 copy-done.4
  84.6 0.0 copy-done.6
  84.6 0.0 copy-done.7
  84.6 0.0 copy-done
  84.6 0.0 copy-done.1
  84.6 0.0 copy-done.8
  84.6 3.7 %shard_map.138 = (bf16[128,896]{1,0:T(8,128)(2,1)}, bf16[128,5376]{1,0:T(8,128)(2,1)S(1)}) custom-call(bf16[128,4736]{1,0:T(8,128)(2,1)S(1)} %bitcast.8, f32[8,384]{1,0:T(8,128)S(1)} %get-tuple-element.23.gain_sums, bf16[128,384]{1,0:T(8,128)(2,1)S(1)} %copy-done.6, f32[384]{0:T(512)S(1)} %copy-done.8, f32[128]{0:T(128)S(1)} %copy-done.9, ...), custom_call_target="tpu_custom_call" | custom-call | tf_op jit(solution)/shard_map/pallas_call | solution.py:59
  88.4 1.9 %collective-permute-start = (bf16[128,5376]{1,0:T(8,128)(2,1)S(1)}, bf16[128,5376]{1,0:T(8,128)(2,1)}, u32[]{:S(2)}, u32[]{:S(2)}) collective-permute-start(bf16[128,5376]{1,0:T(8,128)(2,1)S(1)} %get-tuple-element.24.refs_1_), channel_id=1, source_target_pairs={{0,128},{128,0},{256,384},{384,256},{512,640},{640,512},{768,896},... | collective-permute-start | bytes 4128776 | tf_op jit(solution)/shard_map/ppermute | solution.py:466
  90.3 3.2 %collective-permute-done.refs_2_ = bf16[128,5376]{1,0:T(8,128)(2,1)} collective-permute-done((bf16[128,5376]{1,0:T(8,128)(2,1)S(1)}, bf16[128,5376]{1,0:T(8,128)(2,1)}, u32[]{:S(2)}, u32[]{:S(2)}) %collective-permute-start) | collective-permute-done | bytes 1376288 | tf_op jit(solution)/shard_map/ppermute | solution.py:466
  93.5 3.5 %shard_map.139 = (f32[576,384]{1,0:T(8,128)}, bf16[576,384]{1,0:T(8,128)(2,1)}, bf16[576,384]{1,0:T(8,128)(2,1)}, bf16[576,384]{1,0:T(8,128)(2,1)}) custom-call(s32[1]{0:T(128)} %bitcast.1.refs_0_, bf16[128,5376]{1,0:T(8,128)(2,1)} %copy-done.3, bf16[128,5376]{1,0:T(8,128)(2,1)} %collective-permute-done.refs_2_), custom_call_target="tpu_custom_call" | custom-call | tf_op jit(solution)/shard_map/pallas_call | solution.py:59
  97.1 7.9 %collective-permute-start.1 = (bf16[576,384]{1,0:T(8,128)(2,1)}, bf16[576,384]{1,0:T(8,128)(2,1)S(1)}, u32[]{:S(2)}, u32[]{:S(2)}) collective-permute-start(bf16[576,384]{1,0:T(8,128)(2,1)} %get-tuple-element.26), channel_id=1, source_target_pairs={{0,256},{128,896},{256,512},{384,128},{512,768},{640,384},{768,0},... | collective-permute-start | bytes 1327112 | tf_op jit(solution)/shard_map/ppermute | solution.py:493
  105.0 7.7 %all-to-all-start.2 = ((bf16[8,16,896]{2,1,0:T(8,128)(2,1)}), bf16[8,16,896]{2,1,0:T(8,128)(2,1)S(1)}, u32[]{:S(2)}, u32[]{:S(2)}) async-start(bf16[8,16,896]{2,1,0:T(8,128)(2,1)} %bitcast.6), calls=%async_computation.2 | async-start | bytes 458752 | tf_op jit(solution)/shard_map/all_to_all | solution.py:413
  112.7 9.5 %collective-permute-start.3 = (bf16[576,384]{1,0:T(8,128)(2,1)}, bf16[576,384]{1,0:T(8,128)(2,1)S(1)}, u32[]{:S(2)}, u32[]{:S(2)}) collective-permute-start(bf16[576,384]{1,0:T(8,128)(2,1)} %get-tuple-element.33), channel_id=1, source_target_pairs={{0,768},{128,384},{256,0},{384,640},{512,256},{640,896},{768,512},... | collective-permute-start | bytes 1327112 | tf_op jit(solution)/shard_map/ppermute | solution.py:493
  122.2 1.6 %collective-permute-done.1 = bf16[576,384]{1,0:T(8,128)(2,1)S(1)} collective-permute-done((bf16[576,384]{1,0:T(8,128)(2,1)}, bf16[576,384]{1,0:T(8,128)(2,1)S(1)}, u32[]{:S(2)}, u32[]{:S(2)}) %collective-permute-start.1) | collective-permute-done | bytes 442400 | tf_op jit(solution)/shard_map/ppermute | solution.py:493
  123.7 0.8 copy-done.11
  124.5 1.3 add_convert_fusion
  125.8 0.0 all-to-all-done.2
  125.8 2.2 %collective-permute-start.2 = (bf16[576,384]{1,0:T(8,128)(2,1)S(1)}, bf16[576,384]{1,0:T(8,128)(2,1)}, u32[]{:S(2)}, u32[]{:S(2)}) collective-permute-start(bf16[576,384]{1,0:T(8,128)(2,1)S(1)} %add_convert_fusion), channel_id=1, source_target_pairs={{0,256},{128,896},{256,512},{384,128},{512,768},{640,384},{768,0},... | collective-permute-start | bytes 1327112 | tf_op jit(solution)/shard_map/ppermute | solution.py:493
  128.0 0.1 pad_add_fusion.place
  128.1 1.2 shard_map.140
  129.4 5.0 %collective-permute-done.3.direct = bf16[576,384]{1,0:T(8,128)(2,1)S(1)} collective-permute-done((bf16[576,384]{1,0:T(8,128)(2,1)}, bf16[576,384]{1,0:T(8,128)(2,1)S(1)}, u32[]{:S(2)}, u32[]{:S(2)}) %collective-permute-start.3) | collective-permute-done | bytes 442400 | tf_op jit(solution)/shard_map/ppermute | solution.py:493
  134.4 11.2 %collective-permute-done.2.relayed = bf16[576,384]{1,0:T(8,128)(2,1)} collective-permute-done((bf16[576,384]{1,0:T(8,128)(2,1)S(1)}, bf16[576,384]{1,0:T(8,128)(2,1)}, u32[]{:S(2)}, u32[]{:S(2)}) %collective-permute-start.2) | collective-permute-done | bytes 442400 | tf_op jit(solution)/shard_map/ppermute | solution.py:493
  145.5 2.0 %shard_map.141 = (f32[3,1,48,384]{3,2,1,0:T(8,128)}, f32[1,48,1536]{2,1,0:T(8,128)}, f32[1,48,384]{2,1,0:T(8,128)}, f32[1,192,384]{2,1,0:T(8,128)}) custom-call(f32[576,384]{1,0:T(8,128)S(1)} %copy-done.5, bf16[576,384]{1,0:T(8,128)(2,1)} %collective-permute-done.2.relayed, bf16[576,384]{1,0:T(8,128)(2,1)S(1)} %collective-permute-done.3.direct), custom_call_target="tpu_custom_call" | custom-call | tf_op jit(solution)/shard_map/pallas_call | solution.py:59
  (12 shorter events, 0.0 us)
Async XLA Ops:
  48.6 35.9 %copy-start.2 = (bf16[3,384,384]{2,1,0:T(8,128)(2,1)S(1)}, bf16[3,384,384]{2,1,0:T(8,128)(2,1)}, u32[]{:S(2)}) copy-start(bf16[3,384,384]{2,1,0:T(8,128)(2,1)} %w_qkv.1) | copy-start | bytes 2654212
  48.6 35.9 %copy-start.4 = (bf16[384,384]{1,0:T(8,128)(2,1)S(1)}, bf16[384,384]{1,0:T(8,128)(2,1)}, u32[]{:S(2)}) copy-start(bf16[384,384]{1,0:T(8,128)(2,1)} %w_attn.1) | copy-start | bytes 884740
  48.6 35.9 %copy-start.6 = (bf16[128,384]{1,0:T(8,128)(2,1)S(1)}, bf16[128,384]{1,0:T(8,128)(2,1)}, u32[]{:S(2)}) copy-start(bf16[128,384]{1,0:T(8,128)(2,1)} %tokens.3) | copy-start | bytes 294916
  48.6 35.9 %copy-start.7 = (bf16[128,384]{1,0:T(8,128)(2,1)S(1)}, bf16[128,384]{1,0:T(8,128)(2,1)}, u32[]{:S(2)}) copy-start(bf16[128,384]{1,0:T(8,128)(2,1)} %cotangent.3) | copy-start | bytes 294916
  49.2 35.4 %copy-start = (bf16[384,1536]{1,0:T(8,128)(2,1)S(1)}, bf16[384,1536]{1,0:T(8,128)(2,1)}, u32[]{:S(2)}) copy-start(bf16[384,1536]{1,0:T(8,128)(2,1)} %w_hidden.1) | copy-start | bytes 3538948
  49.2 35.4 %copy-start.1 = (bf16[1536,384]{1,0:T(8,128)(2,1)S(1)}, bf16[1536,384]{1,0:T(8,128)(2,1)}, u32[]{:S(2)}) copy-start(bf16[1536,384]{1,0:T(8,128)(2,1)} %w_mlp.1) | copy-start | bytes 3538948
  49.2 35.4 %copy-start.8 = (f32[384]{0:T(512)S(1)}, f32[384]{0:T(512)}, u32[]{:S(2)}) copy-start(f32[384]{0:T(512)} %ln_gain.3) | copy-start | bytes 4612
  49.2 35.4 %copy-start.9 = (f32[128]{0:T(128)S(1)}, f32[128]{0:T(128)}, u32[]{:S(2)}) copy-start(f32[128]{0:T(128)} %query_gain.1) | copy-start | bytes 1540
  49.2 35.4 %copy-start.10 = (f32[128]{0:T(128)S(1)}, f32[128]{0:T(128)}, u32[]{:S(2)}) copy-start(f32[128]{0:T(128)} %key_gain.1) | copy-start | bytes 1540
  88.4 5.1 %copy-start.3 = (bf16[128,5376]{1,0:T(8,128)(2,1)}, bf16[128,5376]{1,0:T(8,128)(2,1)S(1)}, u32[]{:S(2)}) copy-start(bf16[128,5376]{1,0:T(8,128)(2,1)S(1)} %get-tuple-element.24.refs_1_) | copy-start | bytes 4128772
  88.4 5.1 %collective-permute-start = (bf16[128,5376]{1,0:T(8,128)(2,1)S(1)}, bf16[128,5376]{1,0:T(8,128)(2,1)}, u32[]{:S(2)}, u32[]{:S(2)}) collective-permute-start(bf16[128,5376]{1,0:T(8,128)(2,1)S(1)} %get-tuple-element.24.refs_1_), channel_id=1, source_target_pairs={{0,128},{128,0},{256,384},{384,256},{512,640},{640,512},{768,896},... | collective-permute-start | bytes 4128776 | tf_op jit(solution)/shard_map/ppermute | solution.py:466
  97.1 26.7 %collective-permute-start.1 = (bf16[576,384]{1,0:T(8,128)(2,1)}, bf16[576,384]{1,0:T(8,128)(2,1)S(1)}, u32[]{:S(2)}, u32[]{:S(2)}) collective-permute-start(bf16[576,384]{1,0:T(8,128)(2,1)} %get-tuple-element.26), channel_id=1, source_target_pairs={{0,256},{128,896},{256,512},{384,128},{512,768},{640,384},{768,0},... | collective-permute-start | bytes 1327112 | tf_op jit(solution)/shard_map/ppermute | solution.py:493
  105.0 20.9 %all-to-all-start.2 = ((bf16[8,16,896]{2,1,0:T(8,128)(2,1)}), bf16[8,16,896]{2,1,0:T(8,128)(2,1)S(1)}, u32[]{:S(2)}, u32[]{:S(2)}) async-start(bf16[8,16,896]{2,1,0:T(8,128)(2,1)} %bitcast.6), calls=%async_computation.2 | async-start | bytes 458752 | tf_op jit(solution)/shard_map/all_to_all | solution.py:413
  112.7 21.7 %collective-permute-start.3 = (bf16[576,384]{1,0:T(8,128)(2,1)}, bf16[576,384]{1,0:T(8,128)(2,1)S(1)}, u32[]{:S(2)}, u32[]{:S(2)}) collective-permute-start(bf16[576,384]{1,0:T(8,128)(2,1)} %get-tuple-element.33), channel_id=1, source_target_pairs={{0,768},{128,384},{256,0},{384,640},{512,256},{640,896},{768,512},... | collective-permute-start | bytes 1327112 | tf_op jit(solution)/shard_map/ppermute | solution.py:493
  123.7 0.8 copy-start.11
  124.5 21.0 %copy-start.5 = (f32[576,384]{1,0:T(8,128)S(1)}, f32[576,384]{1,0:T(8,128)}, u32[]{:S(2)}) copy-start(f32[576,384]{1,0:T(8,128)} %get-tuple-element.31.here) | copy-start | bytes 2654212
  125.8 19.7 %collective-permute-start.2 = (bf16[576,384]{1,0:T(8,128)(2,1)S(1)}, bf16[576,384]{1,0:T(8,128)(2,1)}, u32[]{:S(2)}, u32[]{:S(2)}) collective-permute-start(bf16[576,384]{1,0:T(8,128)(2,1)S(1)} %add_convert_fusion), channel_id=1, source_target_pairs={{0,256},{128,896},{256,512},{384,128},{512,768},{640,384},{768,0},... | collective-permute-start | bytes 1327112 | tf_op jit(solution)/shard_map/ppermute | solution.py:493

commit v6 on v5

--- a/solution.py
+++ b/solution.py
@@ -119,9 +119,15 @@
     loads[6].wait()
     for block in range(blocks):
         emit(dot_last(back, w_mlp[block * head_width : (block + 1) * head_width, :]))
-    spread = jnp.broadcast_to(gain_sums[None], (rows // share, share, head_width))
+    stats = pieces(mean, 3) + pieces(squares, 3)
+    lane = lax.broadcasted_iota(jnp.int32, (rows, head_width), 1)
+    token = lax.broadcasted_iota(jnp.int32, (rows, head_width), 0) % share
+    block = jnp.zeros((rows, head_width), F32)
+    for index, value in enumerate(stats):
+        block = jnp.where(lane == token * len(stats) + index, value, block)
+    row = jnp.sum(block.reshape(rows // share, share, head_width), axis=1, keepdims=True)
+    spread = jnp.where(share_id[None] == share - 1, row, gain_sums[None])
     emit(spread.reshape(rows, head_width))
-    emit(to_lanes(pieces(mean, 3) + pieces(squares, 3)))
     for copy, _ in sends:
         copy.wait()
 
@@ -130,21 +136,27 @@
     rows, columns = got.shape
     share = sums_out.shape[0]
     parts = rows // share
-    hidden_width = (columns - 5 * head_width - LANES) // 2
+    hidden_width = (columns - 5 * head_width) // 2
     blocks = hidden_width // head_width
     width = parts * local_width
 
     def take(start, length):
         return got[:, start : start + length].astype(F32).reshape(parts, share, length)
 
-    stats_at = columns - LANES
-    stats = take(stats_at, LANES)
-    local_mean = from_lanes(stats, 0, 3)
+    gain_parts = take(columns - head_width, head_width)
+    stats = jnp.broadcast_to(gain_parts[:, share - 1 : share, :], gain_parts.shape)
+    lane = lax.broadcasted_iota(jnp.int32, stats.shape, 2)
+    first = lax.broadcasted_iota(jnp.int32, stats.shape, 1) * 6
+
+    def stat(offset):
+        keep = (lane >= first + offset) & (lane < first + offset + 3)
+        return jnp.sum(jnp.where(keep, stats, 0.0), axis=2, keepdims=True)
+
+    local_mean = stat(0)
     mean = jnp.sum(local_mean, axis=0, keepdims=True) / parts
     shift = local_mean - mean
-    square_sum = jnp.sum(from_lanes(stats, 3, 3) + local_width * shift * shift, axis=0)
+    square_sum = jnp.sum(stat(3) + local_width * shift * shift, axis=0)
     inverse = lax.rsqrt(square_sum / width + EPSILON)
-    gain_parts = take(stats_at - head_width, head_width)
     gain_sums = jnp.sum(gain_parts, axis=0)
     sums_out[...] = gain_sums
 
@@ -187,13 +199,10 @@
 
 
 def attend_kernel(
-    full, gain_sums, tokens, ln_gain, query_gain, key_gain, w_qkv, w_hidden, w_attn, w_mlp,
-    cotangent, terms, acts,
+    head_width, hidden_width, full, gain_sums, tokens, ln_gain, query_gain, key_gain, cotangent, acts
 ):
     head_size = query_gain.shape[0]
     query_row, key_row = query_gain[...][None], key_gain[...][None]
-    head_width = w_qkv.shape[2]
-    hidden_width = w_hidden.shape[1]
     local_width = tokens.shape[1]
     stats = full[:, 4 * head_width + 2 * hidden_width :].astype(F32)
     mean, inverse = from_lanes(stats, 0, 3), from_lanes(stats, 3, 3)
@@ -256,15 +265,50 @@
         plain_sum = plain_sum + jnp.sum(plain, axis=1, keepdims=True)
         hat_sum = hat_sum + jnp.sum(with_hat, axis=1, keepdims=True)
 
-    mixed = dot_plain(acts[:, acts_heads : acts_heads + head_width], w_attn[...])
-    mixed = mixed + dot_plain(full[:, hidden_at : hidden_at + hidden_width], w_mlp[...])
+    acts[:, acts_heads + 4 * head_width :] = to_lanes(pieces(plain_sum, 2) + pieces(hat_sum, 2)).astype(BF16)
+
+
+def terms_kernel(
+    acts_far, w_mlp_far, w_hidden_far, w_attn_far, w_qkv_far, terms,
+    acts, w_mlp, w_hidden, w_attn, w_qkv, arrived,
+):
+    head_width = w_qkv.shape[2]
+    hidden_width, local_width = w_mlp.shape
+    hidden_at = 2 * local_width
+    heads_at = hidden_at + 2 * hidden_width
+    loads = []
+
+    def load(source, target):
+        copy = pltpu.make_async_copy(source, target, arrived.at[len(loads)])
+        copy.start()
+        loads.append(copy)
+
+    def load_acts(start, length):
+        load(acts_far.at[:, pl.ds(start, length)], acts.at[:, pl.ds(start, length)])
+
+    load_acts(hidden_at, hidden_width)
+    load(w_mlp_far, w_mlp)
+    load_acts(hidden_at + hidden_width, hidden_width)
+    load(w_hidden_far, w_hidden)
+    load_acts(heads_at, 4 * head_width + LANES)
+    load(w_attn_far, w_attn)
+    load(w_qkv_far, w_qkv)
+
+    loads[0].wait()
+    loads[1].wait()
+    mixed = dot_plain(acts[:, hidden_at : hidden_at + hidden_width], w_mlp[...])
+    loads[2].wait()
+    loads[3].wait()
+    grad_normed = dot_last(acts[:, hidden_at + hidden_width : heads_at], w_hidden[...])
+    for copy in loads[4:]:
+        copy.wait()
+    mixed = mixed + dot_plain(acts[:, heads_at : heads_at + head_width], w_attn[...])
     terms[:, :local_width] = mixed.astype(BF16)
-    grad_normed = dot_last(full[:, hidden_at + hidden_width : hidden_at + 2 * hidden_width], w_hidden[...])
     for part in range(3):
-        start = acts_heads + (1 + part) * head_width
+        start = heads_at + (1 + part) * head_width
         grad_normed = grad_normed + dot_last(acts[:, start : start + head_width], w_qkv[part])
     terms[:, local_width : 2 * local_width] = grad_normed.astype(BF16)
-    terms[:, 2 * local_width :] = to_lanes(pieces(plain_sum, 2) + pieces(hat_sum, 2)).astype(BF16)
+    terms[:, 2 * local_width :] = acts[:, heads_at + 4 * head_width :]
 
 
 def weight_kernel(
@@ -422,12 +466,11 @@
     width = local_width * n_my
     share, out_rows = row_count // n_my, row_count // n_mx
 
-    weights = (w_qkv, w_hidden, w_attn_out, w_mlp_out)
 
     def shape(*dims, dtype=BF16):
         return jax.ShapeDtypeStruct(dims, dtype)
 
-    term_width = 5 * head_width + 2 * hidden_width + LANES
+    term_width = 5 * head_width + 2 * hidden_width
     inputs = (tokens, ln_gain, w_qkv, w_hidden, cotangent, w_attn_out, w_mlp_out)
     (terms,) = run(
         lambda *refs: project_kernel(share, *refs),
@@ -437,7 +480,7 @@
         + [
             pltpu.VMEM((row_count, term_width), BF16),
             pltpu.SemaphoreType.DMA((len(inputs),)),
-            pltpu.SemaphoreType.DMA((term_width // head_width + 1,)),
+            pltpu.SemaphoreType.DMA((term_width // head_width,)),
         ],
         fetched=range(len(inputs)),
         written=(0,),
@@ -453,17 +496,25 @@
         ),
     )
     full = exchange(spread, "my")
-    act_width = 2 * local_width + 2 * hidden_width + 4 * head_width
-    out_terms, acts = run(
-        attend_kernel,
-        (
-            full, gain_sums, tokens, ln_gain, query_gain, key_gain,
-            *weights, cotangent,
-        ),
-        (shape(row_count, 2 * local_width + LANES), shape(row_count, act_width)),
-        mebibytes=16,
+    act_width = 2 * local_width + 2 * hidden_width + 4 * head_width + LANES
+    (acts,) = run(
+        lambda *refs: attend_kernel(head_width, hidden_width, *refs),
+        (full, gain_sums, tokens, ln_gain, query_gain, key_gain, cotangent),
+        (shape(row_count, act_width),),
     )
     peer_acts = lax.ppermute(acts, "dp", [(source, source ^ 1) for source in range(n_dp)])
+    (out_terms,) = run(
+        terms_kernel,
+        (acts, w_mlp_out, w_hidden, w_attn_out, w_qkv),
+        (shape(row_count, 2 * local_width + LANES),),
+        scratch=[
+            pltpu.VMEM(array.shape, BF16) for array in (acts, w_mlp_out, w_hidden, w_attn_out, w_qkv)
+        ]
+        + [pltpu.SemaphoreType.DMA((7,))],
+        fetched=(0, 1, 2, 3, 4),
+        mebibytes=60,
+    )
+    peer_acts, out_terms = lax.optimization_barrier((peer_acts, out_terms))
     out_got = exchange(out_terms, "mx")
     block_rows = (3 * local_width + local_width * hidden_width // head_width + head_width + hidden_width) // n_dp
     block = shape(block_rows, local_width)

time: 148 us -> 148 us (level)
  the two profiles are of different devices: /device:TPU:32 before, /device:TPU:1 now
where the time goes in v6:
time: 148 us; the launch traced here: 146 us
  blocking collectives  65.3 us (44%)
  starting transfers between devices  45.9 us (31%)
  Pallas kernels  17.9 us (12%)
  waiting for transfers between devices  13.6 us (9%)
    all_to_all x2, blocking collectives, exchange(): return lax.all_to_all(values, axis, 0, 0, tiled=True)  65.3 us
    ppermute x3, starting transfers between devices, pass_on(): return lax.ppermute(values, 'dp', ways)  28.2 us
    pallas_call x7, Pallas kernels, run(): pl.pallas_call(kernel, in_specs=in_specs, out_specs=out_specs, out_shape=...  17.9 us
    ppermute x1, starting transfers between devices, per_device(): lax.ppermute(acts, 'dp', [(source, source ^ 1) for source in range(n_dp)])  10.4 us
    ppermute x3, waiting for transfers between devices, pass_on(): return lax.ppermute(values, 'dp', ways)  9.73 us
    all_to_all x1, starting transfers between devices, exchange(): return lax.all_to_all(values, axis, 0, 0, tiled=True)  7.28 us
    all_to_all x1, waiting for transfers between devices, exchange(): return lax.all_to_all(values, axis, 0, 0, tiled=True)  3.87 us
  transfers between devices with their start and end apart: 5, of which 4 were waited for; matrix products, arithmetic and copies ran while one was open for 1% of the time, Pallas kernels for 4%

profile of v6, /device:TPU:1, one launch (start us, length us, event | category | flops | bytes accessed | tf_op | source)
XLA Modules:
  0.0 145.7 jit_solution(11976329433293825763)
XLA Ops:
  0.6 3.9 %shard_map.136 = bf16[128,4992]{1,0:T(8,128)(2,1)} custom-call(bf16[128,384]{1,0:T(8,128)(2,1)} %tokens.1, f32[384]{0:T(512)} %ln_gain.1, bf16[3,384,384]{2,1,0:T(8,128)(2,1)} %w_qkv_far.1, bf16[384,1536]{1,0:T(8,128)(2,1)} %w_hidden_far.1, bf16[128,384]{1,0:T(8,128)(2,1)} %cotangent.1, bf16[384,384]{1,0:T(8,128)(2,1)} %w_attn_far.1, bf16[1536,384]{1,0:T(8,128)(2,1)} %w_mlp_far.1), custom_call_target="tpu_custom_call" | custom-call | tf_op jit(solution)/shard_map/pallas_call | solution.py:59
  4.6 36.3 %all_to_all.34 = bf16[16,8,4992]{2,1,0:T(8,128)(2,1)S(1)} all-to-all(bf16[16,8,4992]{2,1,0:T(8,128)(2,1)} %bitcast.13), channel_id=1, replica_groups=mesh['dp'=8,'mx'=8,'my'=16] {'my'}, dimensions={0} | all-to-all | bytes 2555904 | tf_op jit(solution)/shard_map/all_to_all | solution.py:457
  40.9 0.5 shard_map.137
  41.4 0.0 copy-start.2
  41.4 0.0 copy-start.4
  41.4 0.0 copy-start.5
  41.4 0.0 copy-start.6
  41.5 29.0 %all_to_all.35 = bf16[16,8,4736]{2,1,0:T(8,128)(2,1)S(1)} all-to-all(bf16[16,8,4736]{2,1,0:T(8,128)(2,1)S(1)} %bitcast.11), channel_id=1, replica_groups=mesh['dp'=8,'mx'=8,'my'=16] {'my'}, dimensions={0} | all-to-all | bytes 2424832 | tf_op jit(solution)/shard_map/all_to_all | solution.py:457
  70.4 0.0 copy-done.1
  70.4 0.0 copy-done.2
  70.4 0.0 copy-done.4
  70.4 0.0 copy-done.5
  70.5 0.0 copy-done.6
  70.5 2.5 %shard_map.138.acts_far.refs_1_ = bf16[128,5504]{1,0:T(8,128)(2,1)S(1)} custom-call(bf16[128,4736]{1,0:T(8,128)(2,1)S(1)} %bitcast.8, f32[8,384]{1,0:T(8,128)S(1)} %get-tuple-element.23.refs_1_, bf16[128,384]{1,0:T(8,128)(2,1)S(1)} %copy-done.1, f32[384]{0:T(512)S(1)} %copy-done.4, f32[128]{0:T(128)S(1)} %copy-done.5, f32[128]{0:T(128)S(1)} %copy-done.6, ...), custom_call_target="tpu_custom_call" | custom-call | tf_op jit(solution)/shard_map/pallas_call | solution.py:59
  72.9 10.4 %collective-permute-start = (bf16[128,5504]{1,0:T(8,128)(2,1)S(1)}, bf16[128,5504]{1,0:T(8,128)(2,1)}, u32[]{:S(2)}, u32[]{:S(2)}) collective-permute-start(bf16[128,5504]{1,0:T(8,128)(2,1)S(1)} %shard_map.138.acts_far.refs_1_), channel_id=1, source_target_pairs={{0,128},{128,0},{256,384},{384,256},{512,640},{640,512},{768,896},... | collective-permute-start | bytes 4227080 | tf_op jit(solution)/shard_map/ppermute | solution.py:505
  83.4 4.1 %shard_map.139 = bf16[128,896]{1,0:T(8,128)(2,1)} custom-call(bf16[128,5504]{1,0:T(8,128)(2,1)} %copy-done, bf16[1536,384]{1,0:T(8,128)(2,1)} %w_mlp_far.1, bf16[384,1536]{1,0:T(8,128)(2,1)} %w_hidden_far.1, bf16[384,384]{1,0:T(8,128)(2,1)} %w_attn_far.1, bf16[3,384,384]{2,1,0:T(8,128)(2,1)} %w_qkv_far.1), custom_call_target="tpu_custom_call" | custom-call | tf_op jit(solution)/shard_map/pallas_call | solution.py:59
  87.5 0.0 collective-permute-done.refs_2_
  87.6 3.6 %shard_map.140 = (f32[576,384]{1,0:T(8,128)}, bf16[576,384]{1,0:T(8,128)(2,1)}, bf16[576,384]{1,0:T(8,128)(2,1)}, bf16[576,384]{1,0:T(8,128)(2,1)}) custom-call(s32[1]{0:T(128)} %bitcast.1.refs_0_, bf16[128,5504]{1,0:T(8,128)(2,1)} %copy-done, bf16[128,5504]{1,0:T(8,128)(2,1)} %collective-permute-done.refs_2_), custom_call_target="tpu_custom_call" | custom-call | tf_op jit(solution)/shard_map/pallas_call | solution.py:59
  91.1 21.7 %collective-permute-start.1 = (bf16[576,384]{1,0:T(8,128)(2,1)}, bf16[576,384]{1,0:T(8,128)(2,1)S(1)}, u32[]{:S(2)}, u32[]{:S(2)}) collective-permute-start(bf16[576,384]{1,0:T(8,128)(2,1)} %get-tuple-element.26), channel_id=1, source_target_pairs={{0,256},{128,896},{256,512},{384,128},{512,768},{640,384},{768,0},... | collective-permute-start | bytes 1327112 | tf_op jit(solution)/shard_map/ppermute | solution.py:544
  112.9 7.3 %all-to-all-start.2 = ((bf16[8,16,896]{2,1,0:T(8,128)(2,1)}), bf16[8,16,896]{2,1,0:T(8,128)(2,1)S(1)}, u32[]{:S(2)}, u32[]{:S(2)}) async-start(bf16[8,16,896]{2,1,0:T(8,128)(2,1)} %bitcast.6), calls=%async_computation.2 | async-start | bytes 458752 | tf_op jit(solution)/shard_map/all_to_all | solution.py:457
  120.2 1.9 %collective-permute-start.3 = (bf16[576,384]{1,0:T(8,128)(2,1)}, bf16[576,384]{1,0:T(8,128)(2,1)S(1)}, u32[]{:S(2)}, u32[]{:S(2)}) collective-permute-start(bf16[576,384]{1,0:T(8,128)(2,1)} %get-tuple-element.33), channel_id=1, source_target_pairs={{0,768},{128,384},{256,0},{384,640},{512,256},{640,896},{768,512},... | collective-permute-start | bytes 1327112 | tf_op jit(solution)/shard_map/ppermute | solution.py:544
  122.1 1.1 collective-permute-done.1
  123.2 0.8 copy-done.7
  123.9 1.3 add_convert_fusion
  125.3 3.9 %all-to-all-done.2 = bf16[8,16,896]{2,1,0:T(8,128)(2,1)S(1)} async-done(((bf16[8,16,896]{2,1,0:T(8,128)(2,1)}), bf16[8,16,896]{2,1,0:T(8,128)(2,1)S(1)}, u32[]{:S(2)}, u32[]{:S(2)}) %all-to-all-start.2) | async-done | bytes 229408 | tf_op jit(solution)/shard_map/all_to_all | solution.py:457
  129.2 4.6 %collective-permute-start.2 = (bf16[576,384]{1,0:T(8,128)(2,1)S(1)}, bf16[576,384]{1,0:T(8,128)(2,1)}, u32[]{:S(2)}, u32[]{:S(2)}) collective-permute-start(bf16[576,384]{1,0:T(8,128)(2,1)S(1)} %add_convert_fusion), channel_id=1, source_target_pairs={{0,256},{128,896},{256,512},{384,128},{512,768},{640,384},{768,0},... | collective-permute-start | bytes 1327112 | tf_op jit(solution)/shard_map/ppermute | solution.py:544
  133.7 0.1 pad_add_fusion.place
  133.8 1.2 shard_map.141
  135.0 3.3 %collective-permute-done.3.direct = bf16[576,384]{1,0:T(8,128)(2,1)S(1)} collective-permute-done((bf16[576,384]{1,0:T(8,128)(2,1)}, bf16[576,384]{1,0:T(8,128)(2,1)S(1)}, u32[]{:S(2)}, u32[]{:S(2)}) %collective-permute-start.3) | collective-permute-done | bytes 442400 | tf_op jit(solution)/shard_map/ppermute | solution.py:544
  138.4 5.3 %collective-permute-done.2.relayed = bf16[576,384]{1,0:T(8,128)(2,1)} collective-permute-done((bf16[576,384]{1,0:T(8,128)(2,1)S(1)}, bf16[576,384]{1,0:T(8,128)(2,1)}, u32[]{:S(2)}, u32[]{:S(2)}) %collective-permute-start.2) | collective-permute-done | bytes 442400 | tf_op jit(solution)/shard_map/ppermute | solution.py:544
  143.7 0.0 copy-done.3
  143.7 2.0 %shard_map.142 = (f32[3,1,48,384]{3,2,1,0:T(8,128)}, f32[1,48,1536]{2,1,0:T(8,128)}, f32[1,48,384]{2,1,0:T(8,128)}, f32[1,192,384]{2,1,0:T(8,128)}) custom-call(f32[576,384]{1,0:T(8,128)S(1)} %copy-done.3, bf16[576,384]{1,0:T(8,128)(2,1)} %collective-permute-done.2.relayed, bf16[576,384]{1,0:T(8,128)(2,1)S(1)} %collective-permute-done.3.direct), custom_call_target="tpu_custom_call" | custom-call | tf_op jit(solution)/shard_map/pallas_call | solution.py:59
  (5 shorter events, 0.0 us)
Async XLA Ops:
  41.4 29.0 %copy-start.1 = (bf16[128,384]{1,0:T(8,128)(2,1)S(1)}, bf16[128,384]{1,0:T(8,128)(2,1)}, u32[]{:S(2)}) copy-start(bf16[128,384]{1,0:T(8,128)(2,1)} %tokens.1) | copy-start | bytes 294916
  41.4 29.0 %copy-start.2 = (bf16[128,384]{1,0:T(8,128)(2,1)S(1)}, bf16[128,384]{1,0:T(8,128)(2,1)}, u32[]{:S(2)}) copy-start(bf16[128,384]{1,0:T(8,128)(2,1)} %cotangent.1) | copy-start | bytes 294916
  41.4 29.0 %copy-start.4 = (f32[384]{0:T(512)S(1)}, f32[384]{0:T(512)}, u32[]{:S(2)}) copy-start(f32[384]{0:T(512)} %ln_gain.1) | copy-start | bytes 4612
  41.4 29.0 %copy-start.5 = (f32[128]{0:T(128)S(1)}, f32[128]{0:T(128)}, u32[]{:S(2)}) copy-start(f32[128]{0:T(128)} %refs_4_.3) | copy-start | bytes 1540
  41.4 29.0 %copy-start.6 = (f32[128]{0:T(128)S(1)}, f32[128]{0:T(128)}, u32[]{:S(2)}) copy-start(f32[128]{0:T(128)} %refs_5_.3) | copy-start | bytes 1540
  72.9 10.4 %copy-start = (bf16[128,5504]{1,0:T(8,128)(2,1)}, bf16[128,5504]{1,0:T(8,128)(2,1)S(1)}, u32[]{:S(2)}) copy-start(bf16[128,5504]{1,0:T(8,128)(2,1)S(1)} %shard_map.138.acts_far.refs_1_) | copy-start | bytes 4227076
  72.9 14.6 %collective-permute-start = (bf16[128,5504]{1,0:T(8,128)(2,1)S(1)}, bf16[128,5504]{1,0:T(8,128)(2,1)}, u32[]{:S(2)}, u32[]{:S(2)}) collective-permute-start(bf16[128,5504]{1,0:T(8,128)(2,1)S(1)} %shard_map.138.acts_far.refs_1_), channel_id=1, source_target_pairs={{0,128},{128,0},{256,384},{384,256},{512,640},{640,512},{768,896},... | collective-permute-start | bytes 4227080 | tf_op jit(solution)/shard_map/ppermute | solution.py:505
  91.1 32.0 %collective-permute-start.1 = (bf16[576,384]{1,0:T(8,128)(2,1)}, bf16[576,384]{1,0:T(8,128)(2,1)S(1)}, u32[]{:S(2)}, u32[]{:S(2)}) collective-permute-start(bf16[576,384]{1,0:T(8,128)(2,1)} %get-tuple-element.26), channel_id=1, source_target_pairs={{0,256},{128,896},{256,512},{384,128},{512,768},{640,384},{768,0},... | collective-permute-start | bytes 1327112 | tf_op jit(solution)/shard_map/ppermute | solution.py:544
  112.9 16.3 %all-to-all-start.2 = ((bf16[8,16,896]{2,1,0:T(8,128)(2,1)}), bf16[8,16,896]{2,1,0:T(8,128)(2,1)S(1)}, u32[]{:S(2)}, u32[]{:S(2)}) async-start(bf16[8,16,896]{2,1,0:T(8,128)(2,1)} %bitcast.6), calls=%async_computation.2 | async-start | bytes 458752 | tf_op jit(solution)/shard_map/all_to_all | solution.py:457
  120.2 18.2 %collective-permute-start.3 = (bf16[576,384]{1,0:T(8,128)(2,1)}, bf16[576,384]{1,0:T(8,128)(2,1)S(1)}, u32[]{:S(2)}, u32[]{:S(2)}) collective-permute-start(bf16[576,384]{1,0:T(8,128)(2,1)} %get-tuple-element.33), channel_id=1, source_target_pairs={{0,768},{128,384},{256,0},{384,640},{512,256},{640,896},{768,512},... | collective-permute-start | bytes 1327112 | tf_op jit(solution)/shard_map/ppermute | solution.py:544
  123.2 0.8 copy-start.7
  123.9 19.7 %copy-start.3 = (f32[576,384]{1,0:T(8,128)S(1)}, f32[576,384]{1,0:T(8,128)}, u32[]{:S(2)}) copy-start(f32[576,384]{1,0:T(8,128)} %get-tuple-element.31.here) | copy-start | bytes 2654212
  129.2 14.5 %collective-permute-start.2 = (bf16[576,384]{1,0:T(8,128)(2,1)S(1)}, bf16[576,384]{1,0:T(8,128)(2,1)}, u32[]{:S(2)}, u32[]{:S(2)}) collective-permute-start(bf16[576,384]{1,0:T(8,128)(2,1)S(1)} %add_convert_fusion), channel_id=1, source_target_pairs={{0,256},{128,896},{256,512},{384,128},{512,768},{640,384},{768,0},... | collective-permute-start | bytes 1327112 | tf_op jit(solution)/shard_map/ppermute | solution.py:544

commit v7 on v6

--- a/solution.py
+++ b/solution.py
@@ -45,6 +45,56 @@
     lane = lax.broadcasted_iota(jnp.int32, block.shape, block.ndim - 1)
     keep = (lane >= first) & (lane < first + count)
     return jnp.sum(jnp.where(keep, block, 0.0), axis=-1, keepdims=True)
+
+
+def pack_stats(mean, squares, share, width):
+    rows = mean.shape[0]
+    stats = pieces(mean, 3) + pieces(squares, 3)
+    lane = lax.broadcasted_iota(jnp.int32, (rows, width), 1)
+    token = lax.broadcasted_iota(jnp.int32, (rows, width), 0) % share
+    block = jnp.zeros((rows, width), F32)
+    for index, value in enumerate(stats):
+        block = jnp.where(lane == token * len(stats) + index, value, block)
+    return jnp.sum(block.reshape(rows // share, share, width), axis=1, keepdims=True)
+
+
+def unpack_stats(blocks, offset):
+    share = blocks.shape[1]
+    stats = jnp.broadcast_to(blocks[:, share - 1 : share, :], blocks.shape)
+    lane = lax.broadcasted_iota(jnp.int32, blocks.shape, 2)
+    first = lax.broadcasted_iota(jnp.int32, blocks.shape, 1) * 6 + offset
+    keep = (lane >= first) & (lane < first + 3)
+    return jnp.sum(jnp.where(keep, stats, 0.0), axis=2, keepdims=True)
+
+
+class Merge:
+    def __init__(self, got, share, parts, part_width, head_width):
+        self.got, self.share, self.parts, self.head_width = got, share, parts, head_width
+        rows, columns = got.shape
+        self.rows, self.kept = rows, rows // parts
+        self.gains = self.take(columns - head_width, head_width).reshape(rows // share, share, head_width)
+        local_mean = unpack_stats(self.gains, 0)
+        self.mean = self.add(local_mean.reshape(rows, 1)) / parts
+        everywhere = jnp.broadcast_to(self.mean[None], (parts, self.kept, 1))
+        self.shift = local_mean - everywhere.reshape(rows // share, share, 1)
+        squares = unpack_stats(self.gains, 3) + part_width * self.shift * self.shift
+        self.squares = self.add(squares.reshape(rows, 1))
+
+    def take(self, start, length):
+        return self.got[:, start : start + length].astype(F32)
+
+    def add(self, values):
+        return jnp.sum(values.reshape(self.parts, self.kept, values.shape[1]), axis=0)
+
+    def plain(self, block):
+        return self.add(self.take(block * self.head_width, self.head_width))
+
+    def projected(self, block):
+        change = self.shift * self.gains[:, block : block + 1, :]
+        return self.plain(block) + self.add(change.reshape(self.rows, self.head_width))
+
+    def gain_sums(self):
+        return self.add(self.gains.reshape(self.rows, self.head_width))
 
 
 def run(kernel, operands, out_shape, scratch=(), scalar=False, fetched=(), written=(), mebibytes=16):
@@ -119,68 +169,55 @@
     loads[6].wait()
     for block in range(blocks):
         emit(dot_last(back, w_mlp[block * head_width : (block + 1) * head_width, :]))
-    stats = pieces(mean, 3) + pieces(squares, 3)
-    lane = lax.broadcasted_iota(jnp.int32, (rows, head_width), 1)
-    token = lax.broadcasted_iota(jnp.int32, (rows, head_width), 0) % share
-    block = jnp.zeros((rows, head_width), F32)
-    for index, value in enumerate(stats):
-        block = jnp.where(lane == token * len(stats) + index, value, block)
-    row = jnp.sum(block.reshape(rows // share, share, head_width), axis=1, keepdims=True)
+    row = pack_stats(mean, squares, share, head_width)
     spread = jnp.where(share_id[None] == share - 1, row, gain_sums[None])
     emit(spread.reshape(rows, head_width))
     for copy, _ in sends:
         copy.wait()
 
 
-def share_kernel(head_width, local_width, got, out, sums_out):
+def merge_kernel(share, parts, part_width, head_width, got, out):
+    merge = Merge(got, share, parts, part_width, head_width)
+    last = got.shape[1] // head_width - 1
+    blocks = (last - 4) // 2
+    for block in range(last):
+        value = merge.projected(block) if block < 3 + blocks else merge.plain(block)
+        out[:, block * head_width : (block + 1) * head_width] = value.astype(BF16)
+    row = pack_stats(merge.mean, merge.squares, share, head_width)
+    sums = merge.gain_sums().reshape(merge.kept // share, share, head_width)
+    share_id = lax.broadcasted_iota(jnp.int32, sums.shape, 1)
+    sums = jnp.where(share_id == share - 1, row, sums)
+    out[:, last * head_width :] = sums.reshape(merge.kept, head_width).astype(BF16)
+
+
+def share_kernel(parts, part_width, head_width, got, out, sums_out):
     rows, columns = got.shape
-    share = sums_out.shape[0]
-    parts = rows // share
+    share = rows // parts
     hidden_width = (columns - 5 * head_width) // 2
     blocks = hidden_width // head_width
-    width = parts * local_width
-
-    def take(start, length):
-        return got[:, start : start + length].astype(F32).reshape(parts, share, length)
-
-    gain_parts = take(columns - head_width, head_width)
-    stats = jnp.broadcast_to(gain_parts[:, share - 1 : share, :], gain_parts.shape)
-    lane = lax.broadcasted_iota(jnp.int32, stats.shape, 2)
-    first = lax.broadcasted_iota(jnp.int32, stats.shape, 1) * 6
-
-    def stat(offset):
-        keep = (lane >= first + offset) & (lane < first + offset + 3)
-        return jnp.sum(jnp.where(keep, stats, 0.0), axis=2, keepdims=True)
-
-    local_mean = stat(0)
-    mean = jnp.sum(local_mean, axis=0, keepdims=True) / parts
-    shift = local_mean - mean
-    square_sum = jnp.sum(stat(3) + local_width * shift * shift, axis=0)
-    inverse = lax.rsqrt(square_sum / width + EPSILON)
-    gain_sums = jnp.sum(gain_parts, axis=0)
+    merge = Merge(got, share, parts, part_width, head_width)
+    inverse = lax.rsqrt(merge.squares / (parts * part_width) + EPSILON)
+    gain_sums = merge.gain_sums()
     sums_out[...] = gain_sums
 
     def spread(value):
         length = value.shape[1]
-        tiled = jnp.broadcast_to(value[None], (parts, share, length))
-        return tiled.reshape(rows, length).astype(BF16)
+        tiled = jnp.broadcast_to(value[None], (out.shape[0] // share, share, length))
+        return tiled.reshape(out.shape[0], length).astype(BF16)
 
     def projected(block):
-        total = jnp.sum(take(block * head_width, head_width), axis=0)
-        total = total + jnp.sum(shift * gain_parts[:, block : block + 1, :], axis=0)
-        return (inverse * total).astype(BF16).astype(F32)
-
-    back_at = (3 + blocks) * head_width
+        return (inverse * merge.projected(block)).astype(BF16).astype(F32)
+
+    back_at = 3 + blocks
     for block in range(3):
         out[:, block * head_width : (block + 1) * head_width] = spread(projected(block))
-    out[:, 3 * head_width : 4 * head_width] = spread(jnp.sum(take(back_at, head_width), axis=0))
+    out[:, 3 * head_width : 4 * head_width] = spread(merge.plain(back_at))
     plain_sum = jnp.zeros((share, 1), F32)
     hat_sum = jnp.zeros((share, 1), F32)
     inner_scale = 0.7978845608028654
     for block in range(blocks):
         pre = projected(3 + block)
-        grad_act = jnp.sum(take(back_at + (1 + block) * head_width, head_width), axis=0)
-        grad_act = grad_act.astype(BF16).astype(F32)
+        grad_act = merge.plain(back_at + 1 + block).astype(BF16).astype(F32)
         squared = pre * pre
         bent = jnp.tanh(inner_scale * (pre + 0.044715 * squared * pre))
         active = 0.5 * pre * (1.0 + bent)
@@ -194,7 +231,7 @@
         out[:, start : start + head_width] = spread(active)
         start += hidden_width
         out[:, start : start + head_width] = spread(grad_pre)
-    scalars = pieces(mean[0], 3) + pieces(inverse, 3) + pieces(plain_sum, 2) + pieces(hat_sum, 2)
+    scalars = pieces(merge.mean, 3) + pieces(inverse, 3) + pieces(plain_sum, 2) + pieces(hat_sum, 2)
     out[:, 4 * head_width + 2 * hidden_width :] = spread(to_lanes(scalars))
 
 
@@ -453,8 +490,8 @@
         copy.wait()
 
 
-def exchange(values, axis):
-    return lax.all_to_all(values, axis, 0, 0, tiled=True)
+def exchange(values, axis, groups=None):
+    return lax.all_to_all(values, axis, 0, 0, tiled=True, axis_index_groups=groups)
 
 
 def per_device(
@@ -465,6 +502,9 @@
     head_width, hidden_width = w_qkv.shape[2], w_hidden.shape[1]
     width = local_width * n_my
     share, out_rows = row_count // n_my, row_count // n_mx
+    near = 4 if n_my % 16 == 0 else 2
+    near_groups = [[first + step for step in range(near)] for first in range(0, n_my, near)]
+    far_groups = [list(range(first, n_my, near)) for first in range(near)]
 
 
     def shape(*dims, dtype=BF16):
@@ -486,16 +526,24 @@
         written=(0,),
         mebibytes=60,
     )
-    got = exchange(terms, "my")
+    got = exchange(terms, "my", near_groups)
+    (terms,) = run(
+        lambda *refs: merge_kernel(share, near, local_width, head_width, *refs),
+        (got,),
+        (shape(row_count // near, term_width),),
+    )
+    got = exchange(terms, "my", far_groups)
     spread, gain_sums = run(
-        lambda *refs: share_kernel(head_width, local_width, *refs),
+        lambda *refs: share_kernel(n_my // near, near * local_width, head_width, *refs),
         (got,),
         (
-            shape(row_count, 4 * head_width + 2 * hidden_width + LANES),
+            shape(row_count // near, 4 * head_width + 2 * hidden_width + LANES),
             shape(share, head_width, dtype=F32),
         ),
     )
-    full = exchange(spread, "my")
+    part = exchange(spread, "my", far_groups)
+    spread = jnp.broadcast_to(part[None], (near, *part.shape)).reshape(row_count, part.shape[1])
+    full = exchange(spread, "my", near_groups)
     act_width = 2 * local_width + 2 * hidden_width + 4 * head_width + LANES
     (acts,) = run(
         lambda *refs: attend_kernel(head_width, hidden_width, *refs),

time: 148 us -> 138 us (0.932)
  starting transfers between devices: 45.9 us -> 39.8 us
  blocking collectives: 65.3 us -> 61.1 us
    ppermute x3, starting transfers between devices: 28.2 us -> 23.4 us  [pass_on(): return lax.ppermute(values, 'dp', ways)]
    all_to_all x2 -> x4, blocking collectives: 65.3 us -> 61.1 us  [exchange(): lax.all_to_all(values, axis, 0, 0, tiled=True, axis_index_groups=groups)]
    pallas_call x7 -> x8, Pallas kernels: 17.9 us -> 18 us  [run(): pl.pallas_call(kernel, in_specs=in_specs, out_specs=out_specs, out_shape=...]
where the time goes in v7:
time: 138 us; the launch traced here: 136 us
  blocking collectives  61.1 us (44%)
  starting transfers between devices  39.8 us (29%)
  Pallas kernels  18 us (13%)
  waiting for transfers between devices  13.6 us (10%)
  other arithmetic  1.41 us (1%)
    all_to_all x4, blocking collectives, exchange(): lax.all_to_all(values, axis, 0, 0, tiled=True, axis_index_groups=groups)  61.1 us
    ppermute x3, starting transfers between devices, pass_on(): return lax.ppermute(values, 'dp', ways)  23.4 us
    pallas_call x8, Pallas kernels, run(): pl.pallas_call(kernel, in_specs=in_specs, out_specs=out_specs, out_shape=...  18 us
    ppermute x3, waiting for transfers between devices, pass_on(): return lax.ppermute(values, 'dp', ways)  9.72 us
    ppermute x1, starting transfers between devices, per_device(): lax.ppermute(acts, 'dp', [(source, source ^ 1) for source in range(n_dp)])  9.09 us
    all_to_all x1, starting transfers between devices, exchange(): lax.all_to_all(values, axis, 0, 0, tiled=True, axis_index_groups=groups)  7.29 us
    all_to_all x1, waiting for transfers between devices, exchange(): lax.all_to_all(values, axis, 0, 0, tiled=True, axis_index_groups=groups)  3.88 us
  transfers between devices with their start and end apart: 5, of which 4 were waited for; matrix products, arithmetic and copies ran while one was open for 1% of the time, Pallas kernels for 4%

profile of v7, /device:TPU:1, one launch (start us, length us, event | category | flops | bytes accessed | tf_op | source)
XLA Modules:
  0.0 135.6 jit_solution(17614978375033414759)
XLA Ops:
  0.6 3.9 %shard_map.136 = bf16[128,4992]{1,0:T(8,128)(2,1)} custom-call(bf16[128,384]{1,0:T(8,128)(2,1)} %tokens.1, f32[384]{0:T(512)} %ln_gain.1, bf16[3,384,384]{2,1,0:T(8,128)(2,1)} %w_qkv_far.1, bf16[384,1536]{1,0:T(8,128)(2,1)} %w_hidden_far.1, bf16[128,384]{1,0:T(8,128)(2,1)} %cotangent.1, bf16[384,384]{1,0:T(8,128)(2,1)} %w_attn_far.1, bf16[1536,384]{1,0:T(8,128)(2,1)} %w_mlp_far.1), custom_call_target="tpu_custom_call" | custom-call | tf_op jit(solution)/shard_map/pallas_call | solution.py:109
  4.6 16.1 %all_to_all.51 = bf16[4,32,4992]{2,1,0:T(8,128)(2,1)S(1)} all-to-all(bf16[4,32,4992]{2,1,0:T(8,128)(2,1)} %bitcast.18), channel_id=1, replica_groups={{0,1,2,3},{4,5,6,7},{8,9,10,11},{12,13,14,15},{16,17,18,19},{20,21,22,2..., dimensions={0} | all-to-all | bytes 2555904 | tf_op jit(solution)/shard_map/all_to_all | solution.py:494
  20.7 0.4 shard_map.137
  21.1 21.1 %all_to_all.52 = bf16[4,8,4992]{2,1,0:T(8,128)(2,1)S(1)} all-to-all(bf16[4,8,4992]{2,1,0:T(8,128)(2,1)S(1)} %bitcast.15), channel_id=1, replica_groups={{0,4,8,12},{1,5,9,13},{2,6,10,14},{3,7,11,15},{16,20,24,28},{17,21,25,2..., dimensions={0} | all-to-all | bytes 638976 | tf_op jit(solution)/shard_map/all_to_all | solution.py:494
  42.3 0.3 shard_map.138
  42.5 11.4 %all_to_all.53 = bf16[4,8,4736]{2,1,0:T(8,128)(2,1)S(1)} all-to-all(bf16[4,8,4736]{2,1,0:T(8,128)(2,1)S(1)} %bitcast.17), channel_id=1, replica_groups={{0,4,8,12},{1,5,9,13},{2,6,10,14},{3,7,11,15},{16,20,24,28},{17,21,25,2..., dimensions={0} | all-to-all | bytes 606208 | tf_op jit(solution)/shard_map/all_to_all | solution.py:494
  53.9 0.1 broadcast_in_dim.9
  54.0 0.0 copy-start.1
  54.0 0.0 copy-start.2
  54.0 0.0 copy-start.4
  54.0 0.0 copy-start.5
  54.0 0.0 copy-start.6
  54.0 12.5 %all_to_all.54 = bf16[4,32,4736]{2,1,0:T(8,128)(2,1)S(1)} all-to-all(bf16[4,32,4736]{2,1,0:T(8,128)(2,1)S(1)} %broadcast_in_dim.9), channel_id=1, replica_groups={{0,1,2,3},{4,5,6,7},{8,9,10,11},{12,13,14,15},{16,17,18,19},{20,21,22,2..., dimensions={0} | all-to-all | bytes 2424832 | tf_op jit(solution)/shard_map/all_to_all | solution.py:494
  66.5 0.0 copy-done.5
  66.6 2.4 %shard_map.139.acts_far.refs_1_ = bf16[128,5504]{1,0:T(8,128)(2,1)S(1)} custom-call(bf16[128,4736]{1,0:T(8,128)(2,1)S(1)} %bitcast.11, f32[8,384]{1,0:T(8,128)S(1)} %get-tuple-element.23.refs_1_, bf16[128,384]{1,0:T(8,128)(2,1)S(1)} %copy-done.1, f32[384]{0:T(512)S(1)} %copy-done.4, f32[128]{0:T(128)S(1)} %copy-done.5, f32[128]{0:T(128)S(1)} %copy-done.6, ...), custom_call_target="tpu_custom_call" | custom-call | tf_op jit(solution)/shard_map/pallas_call | solution.py:109
  69.0 9.1 %collective-permute-start = (bf16[128,5504]{1,0:T(8,128)(2,1)S(1)}, bf16[128,5504]{1,0:T(8,128)(2,1)}, u32[]{:S(2)}, u32[]{:S(2)}) collective-permute-start(bf16[128,5504]{1,0:T(8,128)(2,1)S(1)} %shard_map.139.acts_far.refs_1_), channel_id=1, source_target_pairs={{0,128},{128,0},{256,384},{384,256},{512,640},{640,512},{768,896},... | collective-permute-start | bytes 4227080 | tf_op jit(solution)/shard_map/ppermute | solution.py:553
  78.1 4.1 %shard_map.140 = bf16[128,896]{1,0:T(8,128)(2,1)} custom-call(bf16[128,5504]{1,0:T(8,128)(2,1)} %copy-done, bf16[1536,384]{1,0:T(8,128)(2,1)} %w_mlp_far.1, bf16[384,1536]{1,0:T(8,128)(2,1)} %w_hidden_far.1, bf16[384,384]{1,0:T(8,128)(2,1)} %w_attn_far.1, bf16[3,384,384]{2,1,0:T(8,128)(2,1)} %w_qkv_far.1), custom_call_target="tpu_custom_call" | custom-call | tf_op jit(solution)/shard_map/pallas_call | solution.py:109
  82.3 0.0 collective-permute-done.refs_2_
  82.3 3.6 %shard_map.141 = (f32[576,384]{1,0:T(8,128)}, bf16[576,384]{1,0:T(8,128)(2,1)}, bf16[576,384]{1,0:T(8,128)(2,1)}, bf16[576,384]{1,0:T(8,128)(2,1)}) custom-call(s32[1]{0:T(128)} %bitcast.1.refs_0_, bf16[128,5504]{1,0:T(8,128)(2,1)} %copy-done, bf16[128,5504]{1,0:T(8,128)(2,1)} %collective-permute-done.refs_2_), custom_call_target="tpu_custom_call" | custom-call | tf_op jit(solution)/shard_map/pallas_call | solution.py:109
  85.9 16.9 %collective-permute-start.1 = (bf16[576,384]{1,0:T(8,128)(2,1)}, bf16[576,384]{1,0:T(8,128)(2,1)S(1)}, u32[]{:S(2)}, u32[]{:S(2)}) collective-permute-start(bf16[576,384]{1,0:T(8,128)(2,1)} %get-tuple-element.26), channel_id=1, source_target_pairs={{0,256},{128,896},{256,512},{384,128},{512,768},{640,384},{768,0},... | collective-permute-start | bytes 1327112 | tf_op jit(solution)/shard_map/ppermute | solution.py:592
  102.8 7.3 %all-to-all-start.4 = ((bf16[8,16,896]{2,1,0:T(8,128)(2,1)}), bf16[8,16,896]{2,1,0:T(8,128)(2,1)S(1)}, u32[]{:S(2)}, u32[]{:S(2)}) async-start(bf16[8,16,896]{2,1,0:T(8,128)(2,1)} %bitcast.9), calls=%async_computation.4 | async-start | bytes 458752 | tf_op jit(solution)/shard_map/all_to_all | solution.py:494
  110.1 1.9 %collective-permute-start.3 = (bf16[576,384]{1,0:T(8,128)(2,1)}, bf16[576,384]{1,0:T(8,128)(2,1)S(1)}, u32[]{:S(2)}, u32[]{:S(2)}) collective-permute-start(bf16[576,384]{1,0:T(8,128)(2,1)} %get-tuple-element.33), channel_id=1, source_target_pairs={{0,768},{128,384},{256,0},{384,640},{512,256},{640,896},{768,512},... | collective-permute-start | bytes 1327112 | tf_op jit(solution)/shard_map/ppermute | solution.py:592
  112.0 1.1 collective-permute-done.1
  113.1 0.8 copy-done.7
  113.9 1.3 add_convert_fusion
  115.2 3.9 %all-to-all-done.4 = bf16[8,16,896]{2,1,0:T(8,128)(2,1)S(1)} async-done(((bf16[8,16,896]{2,1,0:T(8,128)(2,1)}), bf16[8,16,896]{2,1,0:T(8,128)(2,1)S(1)}, u32[]{:S(2)}, u32[]{:S(2)}) %all-to-all-start.4) | async-done | bytes 229408 | tf_op jit(solution)/shard_map/all_to_all | solution.py:494
  119.1 4.6 %collective-permute-start.2 = (bf16[576,384]{1,0:T(8,128)(2,1)S(1)}, bf16[576,384]{1,0:T(8,128)(2,1)}, u32[]{:S(2)}, u32[]{:S(2)}) collective-permute-start(bf16[576,384]{1,0:T(8,128)(2,1)S(1)} %add_convert_fusion), channel_id=1, source_target_pairs={{0,256},{128,896},{256,512},{384,128},{512,768},{640,384},{768,0},... | collective-permute-start | bytes 1327112 | tf_op jit(solution)/shard_map/ppermute | solution.py:592
  123.7 0.1 pad_add_fusion.place
  123.7 1.2 shard_map.142
  125.0 3.3 %collective-permute-done.3.direct = bf16[576,384]{1,0:T(8,128)(2,1)S(1)} collective-permute-done((bf16[576,384]{1,0:T(8,128)(2,1)}, bf16[576,384]{1,0:T(8,128)(2,1)S(1)}, u32[]{:S(2)}, u32[]{:S(2)}) %collective-permute-start.3) | collective-permute-done | bytes 442400 | tf_op jit(solution)/shard_map/ppermute | solution.py:592
  128.3 5.3 %collective-permute-done.2.relayed = bf16[576,384]{1,0:T(8,128)(2,1)} collective-permute-done((bf16[576,384]{1,0:T(8,128)(2,1)S(1)}, bf16[576,384]{1,0:T(8,128)(2,1)}, u32[]{:S(2)}, u32[]{:S(2)}) %collective-permute-start.2) | collective-permute-done | bytes 442400 | tf_op jit(solution)/shard_map/ppermute | solution.py:592
  133.6 2.0 %shard_map.143 = (f32[3,1,48,384]{3,2,1,0:T(8,128)}, f32[1,48,1536]{2,1,0:T(8,128)}, f32[1,48,384]{2,1,0:T(8,128)}, f32[1,192,384]{2,1,0:T(8,128)}) custom-call(f32[576,384]{1,0:T(8,128)S(1)} %copy-done.3, bf16[576,384]{1,0:T(8,128)(2,1)} %collective-permute-done.2.relayed, bf16[576,384]{1,0:T(8,128)(2,1)S(1)} %collective-permute-done.3.direct), custom_call_target="tpu_custom_call" | custom-call | tf_op jit(solution)/shard_map/pallas_call | solution.py:109
  (9 shorter events, 0.0 us)
Async XLA Ops:
  54.0 12.5 %copy-start.1 = (bf16[128,384]{1,0:T(8,128)(2,1)S(1)}, bf16[128,384]{1,0:T(8,128)(2,1)}, u32[]{:S(2)}) copy-start(bf16[128,384]{1,0:T(8,128)(2,1)} %tokens.1) | copy-start | bytes 294916
  54.0 12.5 %copy-start.2 = (bf16[128,384]{1,0:T(8,128)(2,1)S(1)}, bf16[128,384]{1,0:T(8,128)(2,1)}, u32[]{:S(2)}) copy-start(bf16[128,384]{1,0:T(8,128)(2,1)} %cotangent.1) | copy-start | bytes 294916
  54.0 12.5 %copy-start.4 = (f32[384]{0:T(512)S(1)}, f32[384]{0:T(512)}, u32[]{:S(2)}) copy-start(f32[384]{0:T(512)} %ln_gain.1) | copy-start | bytes 4612
  54.0 12.5 %copy-start.5 = (f32[128]{0:T(128)S(1)}, f32[128]{0:T(128)}, u32[]{:S(2)}) copy-start(f32[128]{0:T(128)} %refs_4_.3) | copy-start | bytes 1540
  54.0 12.5 %copy-start.6 = (f32[128]{0:T(128)S(1)}, f32[128]{0:T(128)}, u32[]{:S(2)}) copy-start(f32[128]{0:T(128)} %refs_5_.3) | copy-start | bytes 1540
  69.0 9.1 %copy-start = (bf16[128,5504]{1,0:T(8,128)(2,1)}, bf16[128,5504]{1,0:T(8,128)(2,1)S(1)}, u32[]{:S(2)}) copy-start(bf16[128,5504]{1,0:T(8,128)(2,1)S(1)} %shard_map.139.acts_far.refs_1_) | copy-start | bytes 4227076
  69.0 13.3 %collective-permute-start = (bf16[128,5504]{1,0:T(8,128)(2,1)S(1)}, bf16[128,5504]{1,0:T(8,128)(2,1)}, u32[]{:S(2)}, u32[]{:S(2)}) collective-permute-start(bf16[128,5504]{1,0:T(8,128)(2,1)S(1)} %shard_map.139.acts_far.refs_1_), channel_id=1, source_target_pairs={{0,128},{128,0},{256,384},{384,256},{512,640},{640,512},{768,896},... | collective-permute-start | bytes 4227080 | tf_op jit(solution)/shard_map/ppermute | solution.py:553
  85.9 27.2 %collective-permute-start.1 = (bf16[576,384]{1,0:T(8,128)(2,1)}, bf16[576,384]{1,0:T(8,128)(2,1)S(1)}, u32[]{:S(2)}, u32[]{:S(2)}) collective-permute-start(bf16[576,384]{1,0:T(8,128)(2,1)} %get-tuple-element.26), channel_id=1, source_target_pairs={{0,256},{128,896},{256,512},{384,128},{512,768},{640,384},{768,0},... | collective-permute-start | bytes 1327112 | tf_op jit(solution)/shard_map/ppermute | solution.py:592
  102.8 16.3 %all-to-all-start.4 = ((bf16[8,16,896]{2,1,0:T(8,128)(2,1)}), bf16[8,16,896]{2,1,0:T(8,128)(2,1)S(1)}, u32[]{:S(2)}, u32[]{:S(2)}) async-start(bf16[8,16,896]{2,1,0:T(8,128)(2,1)} %bitcast.9), calls=%async_computation.4 | async-start | bytes 458752 | tf_op jit(solution)/shard_map/all_to_all | solution.py:494
  110.1 18.2 %collective-permute-start.3 = (bf16[576,384]{1,0:T(8,128)(2,1)}, bf16[576,384]{1,0:T(8,128)(2,1)S(1)}, u32[]{:S(2)}, u32[]{:S(2)}) collective-permute-start(bf16[576,384]{1,0:T(8,128)(2,1)} %get-tuple-element.33), channel_id=1, source_target_pairs={{0,768},{128,384},{256,0},{384,640},{512,256},{640,896},{768,512},... | collective-permute-start | bytes 1327112 | tf_op jit(solution)/shard_map/ppermute | solution.py:592
  113.1 0.8 copy-start.7
  113.9 19.8 %copy-start.3 = (f32[576,384]{1,0:T(8,128)S(1)}, f32[576,384]{1,0:T(8,128)}, u32[]{:S(2)}) copy-start(f32[576,384]{1,0:T(8,128)} %get-tuple-element.31.here) | copy-start | bytes 2654212
  119.1 14.5 %collective-permute-start.2 = (bf16[576,384]{1,0:T(8,128)(2,1)S(1)}, bf16[576,384]{1,0:T(8,128)(2,1)}, u32[]{:S(2)}, u32[]{:S(2)}) collective-permute-start(bf16[576,384]{1,0:T(8,128)(2,1)S(1)} %add_convert_fusion), channel_id=1, source_target_pairs={{0,256},{128,896},{256,512},{384,128},{512,768},{640,384},{768,0},... | collective-permute-start | bytes 1327112 | tf_op jit(solution)/shard_map/ppermute | solution.py:592

commit v8 on v7

--- a/solution.py
+++ b/solution.py
@@ -47,37 +47,51 @@
     return jnp.sum(jnp.where(keep, block, 0.0), axis=-1, keepdims=True)
 
 
-def pack_stats(mean, squares, share, width):
-    rows = mean.shape[0]
-    stats = pieces(mean, 3) + pieces(squares, 3)
+def pack(values, share, width):
+    rows = values[0].shape[0]
     lane = lax.broadcasted_iota(jnp.int32, (rows, width), 1)
     token = lax.broadcasted_iota(jnp.int32, (rows, width), 0) % share
     block = jnp.zeros((rows, width), F32)
-    for index, value in enumerate(stats):
-        block = jnp.where(lane == token * len(stats) + index, value, block)
+    for index, value in enumerate(values):
+        block = jnp.where(lane == token * len(values) + index, value, block)
     return jnp.sum(block.reshape(rows // share, share, width), axis=1, keepdims=True)
 
 
-def unpack_stats(blocks, offset):
-    share = blocks.shape[1]
-    stats = jnp.broadcast_to(blocks[:, share - 1 : share, :], blocks.shape)
-    lane = lax.broadcasted_iota(jnp.int32, blocks.shape, 2)
-    first = lax.broadcasted_iota(jnp.int32, blocks.shape, 1) * 6 + offset
+def unpack(row, share, count, offset):
+    shape = (row.shape[0], share, row.shape[2])
+    lane = lax.broadcasted_iota(jnp.int32, shape, 2)
+    first = lax.broadcasted_iota(jnp.int32, shape, 1) * count + offset
     keep = (lane >= first) & (lane < first + 3)
-    return jnp.sum(jnp.where(keep, stats, 0.0), axis=2, keepdims=True)
+    return jnp.sum(jnp.where(keep, jnp.broadcast_to(row, shape), 0.0), axis=2, keepdims=True)
 
 
 class Merge:
-    def __init__(self, got, share, parts, part_width, head_width):
-        self.got, self.share, self.parts, self.head_width = got, share, parts, head_width
+    def __init__(self, got, share, parts, part_width, head_width, compact):
+        self.got, self.parts, self.head_width = got, parts, head_width
         rows, columns = got.shape
         self.rows, self.kept = rows, rows // parts
-        self.gains = self.take(columns - head_width, head_width).reshape(rows // share, share, head_width)
-        local_mean = unpack_stats(self.gains, 0)
+        lines = head_width // LANES
+        if compact:
+            share, start = self.kept, columns - LANES
+            block = self.take(start, LANES).reshape(parts, share, LANES)
+            blocks = (start // head_width - 4) // 2 + 3
+            self.gain_rows = [
+                jnp.concatenate([block[:, row : row + 1, :] for row in range(first, first + lines)], axis=2)
+                for first in range(0, blocks * lines, lines)
+            ]
+            last = blocks * lines
+            local_mean = unpack(block[:, last : last + 1, :], share, 3, 0)
+            local_squares = unpack(block[:, last + 1 : last + 2, :], share, 3, 0)
+        else:
+            start = columns - head_width
+            block = self.take(start, head_width).reshape(rows // share, share, head_width)
+            self.gain_rows = [block[:, row : row + 1, :] for row in range(share - 1)]
+            local_mean = unpack(block[:, share - 1 : share, :], share, 6, 0)
+            local_squares = unpack(block[:, share - 1 : share, :], share, 6, 3)
         self.mean = self.add(local_mean.reshape(rows, 1)) / parts
         everywhere = jnp.broadcast_to(self.mean[None], (parts, self.kept, 1))
         self.shift = local_mean - everywhere.reshape(rows // share, share, 1)
-        squares = unpack_stats(self.gains, 3) + part_width * self.shift * self.shift
+        squares = local_squares + part_width * self.shift * self.shift
         self.squares = self.add(squares.reshape(rows, 1))
 
     def take(self, start, length):
@@ -90,11 +104,11 @@
         return self.add(self.take(block * self.head_width, self.head_width))
 
     def projected(self, block):
-        change = self.shift * self.gains[:, block : block + 1, :]
+        change = self.shift * self.gain_rows[block]
         return self.plain(block) + self.add(change.reshape(self.rows, self.head_width))
 
-    def gain_sums(self):
-        return self.add(self.gains.reshape(self.rows, self.head_width))
+    def gain_sum(self, block):
+        return jnp.sum(self.gain_rows[block], axis=0)
 
 
 def run(kernel, operands, out_shape, scratch=(), scalar=False, fetched=(), written=(), mebibytes=16):
@@ -116,7 +130,7 @@
     )(*operands)
 
 
-def project_kernel(share, *refs):
+def project_kernel(kept, *refs):
     far, out_far, near, out, arrived, left_for = refs[:7], refs[7], refs[8:15], refs[15], refs[16], refs[17]
     tokens, ln_gain, w_qkv, w_hidden, cotangent, w_attn, w_mlp = near
     rows, width = tokens.shape
@@ -149,8 +163,9 @@
     row_id = lax.broadcasted_iota(jnp.int32, (16, width), 0)
     gain_rows = jnp.where(row_id == 0, high, jnp.where(row_id == 1, low, 0.0)).astype(BF16)
     left = jnp.concatenate([scaled, gain_rows], axis=0)
-    share_id = lax.broadcasted_iota(jnp.int32, (share, head_width), 0)
-    gain_sums = jnp.zeros((share, head_width), F32)
+    lines = head_width // LANES
+    line_id = lax.broadcasted_iota(jnp.int32, (kept, LANES), 0)
+    gain_sums = jnp.zeros((kept, LANES), F32)
     for block in range(3 + blocks):
         if block == 0 or block == 3:
             loads[2 + block // 3].wait()
@@ -161,7 +176,9 @@
         product = dot_plain(left, weight)
         emit(product[:rows])
         both = product[rows : rows + 1] + product[rows + 1 : rows + 2]
-        gain_sums = jnp.where(share_id == block, both, gain_sums)
+        for line in range(lines):
+            value = both[:, line * LANES : (line + 1) * LANES]
+            gain_sums = jnp.where(line_id == block * lines + line, value, gain_sums)
     loads[4].wait()
     loads[5].wait()
     back = cotangent[...]
@@ -169,23 +186,29 @@
     loads[6].wait()
     for block in range(blocks):
         emit(dot_last(back, w_mlp[block * head_width : (block + 1) * head_width, :]))
-    row = pack_stats(mean, squares, share, head_width)
-    spread = jnp.where(share_id[None] == share - 1, row, gain_sums[None])
-    emit(spread.reshape(rows, head_width))
+    last = (3 + blocks) * lines
+    spread = jnp.where(line_id[None] == last, pack(pieces(mean, 3), kept, LANES), gain_sums[None])
+    spread = jnp.where(line_id[None] == last + 1, pack(pieces(squares, 3), kept, LANES), spread)
+    emit(spread.reshape(rows, LANES))
     for copy, _ in sends:
         copy.wait()
 
 
 def merge_kernel(share, parts, part_width, head_width, got, out):
-    merge = Merge(got, share, parts, part_width, head_width)
-    last = got.shape[1] // head_width - 1
+    merge = Merge(got, share, parts, part_width, head_width, True)
+    last = (got.shape[1] - LANES) // head_width
     blocks = (last - 4) // 2
+    shape = (merge.kept // share, share, head_width)
+    share_id = lax.broadcasted_iota(jnp.int32, shape, 1)
+    sums = jnp.zeros(shape, F32)
     for block in range(last):
-        value = merge.projected(block) if block < 3 + blocks else merge.plain(block)
+        if block < 3 + blocks:
+            value = merge.projected(block)
+            sums = jnp.where(share_id == block, merge.gain_sum(block)[None], sums)
+        else:
+            value = merge.plain(block)
         out[:, block * head_width : (block + 1) * head_width] = value.astype(BF16)
-    row = pack_stats(merge.mean, merge.squares, share, head_width)
-    sums = merge.gain_sums().reshape(merge.kept // share, share, head_width)
-    share_id = lax.broadcasted_iota(jnp.int32, sums.shape, 1)
+    row = pack(pieces(merge.mean, 3) + pieces(merge.squares, 3), share, head_width)
     sums = jnp.where(share_id == share - 1, row, sums)
     out[:, last * head_width :] = sums.reshape(merge.kept, head_width).astype(BF16)
 
@@ -195,9 +218,12 @@
     share = rows // parts
     hidden_width = (columns - 5 * head_width) // 2
     blocks = hidden_width // head_width
-    merge = Merge(got, share, parts, part_width, head_width)
+    merge = Merge(got, share, parts, part_width, head_width, False)
     inverse = lax.rsqrt(merge.squares / (parts * part_width) + EPSILON)
-    gain_sums = merge.gain_sums()
+    share_id = lax.broadcasted_iota(jnp.int32, sums_out.shape, 0)
+    gain_sums = jnp.zeros(sums_out.shape, F32)
+    for block in range(3 + blocks):
+        gain_sums = jnp.where(share_id == block, merge.gain_sum(block), gain_sums)
     sums_out[...] = gain_sums
 
     def spread(value):
@@ -456,11 +482,19 @@
 
 
 def sum_kernel(
-    here, relayed, direct, qkv_far, hidden_far, attn_far, mlp_far, qkv, hidden, attn, mlp, left_for
+    here, relayed_far, direct, qkv_far, hidden_far, attn_far, mlp_far,
+    relayed, qkv, hidden, attn, mlp, arrived, left_for,
 ):
     length, head_width = qkv.shape[2], qkv.shape[3]
     blocks = hidden.shape[2] // head_width
     cuts = (0, 3 * length, (3 + blocks) * length, here.shape[0])
+    loads = []
+    for index, (start, end) in enumerate(zip(cuts, cuts[1:])):
+        part = pl.ds(start, end - start)
+        loads.append(
+            pltpu.make_async_copy(relayed_far.at[part, :], relayed.at[part, :], arrived.at[index])
+        )
+        loads[index].start()
 
     def total(start, count):
         value = here[start : start + count, :]
@@ -475,13 +509,16 @@
         copy.start()
         sends.append(copy)
 
+    loads[0].wait()
     for part in range(3):
         qkv[part, 0] = total(part * length, length)
     send(qkv, qkv_far)
+    loads[1].wait()
     for block in range(blocks):
         columns = slice(block * head_width, (block + 1) * head_width)
         hidden[0, :, columns] = total(cuts[1] + block * length, length)
     send(hidden, hidden_far)
+    loads[2].wait()
     attn[0] = total(cuts[2], attn.shape[1])
     send(attn, attn_far)
     mlp[0] = total(cuts[2] + attn.shape[1], mlp.shape[1])
@@ -510,17 +547,17 @@
     def shape(*dims, dtype=BF16):
         return jax.ShapeDtypeStruct(dims, dtype)
 
-    term_width = 5 * head_width + 2 * hidden_width
+    near_width = 4 * head_width + 2 * hidden_width + LANES
     inputs = (tokens, ln_gain, w_qkv, w_hidden, cotangent, w_attn_out, w_mlp_out)
     (terms,) = run(
-        lambda *refs: project_kernel(share, *refs),
+        lambda *refs: project_kernel(row_count // near, *refs),
         inputs,
-        (shape(row_count, term_width),),
+        (shape(row_count, near_width),),
         scratch=[pltpu.VMEM(array.shape, array.dtype) for array in inputs]
         + [
-            pltpu.VMEM((row_count, term_width), BF16),
+            pltpu.VMEM((row_count, near_width), BF16),
             pltpu.SemaphoreType.DMA((len(inputs),)),
-            pltpu.SemaphoreType.DMA((term_width // head_width,)),
+            pltpu.SemaphoreType.DMA((near_width // head_width + 1,)),
         ],
         fetched=range(len(inputs)),
         written=(0,),
@@ -530,7 +567,7 @@
     (terms,) = run(
         lambda *refs: merge_kernel(share, near, local_width, head_width, *refs),
         (got,),
-        (shape(row_count // near, term_width),),
+        (shape(row_count // near, 5 * head_width + 2 * hidden_width),),
     )
     got = exchange(terms, "my", far_groups)
     spread, gain_sums = run(
@@ -613,7 +650,10 @@
         sum_kernel,
         (here, got_relayed, got_direct),
         grad_shapes,
-        scratch=[pltpu.VMEM(grad.shape, grad.dtype) for grad in grad_shapes] + [pltpu.SemaphoreType.DMA((4,))],
+        scratch=[pltpu.VMEM(block.shape, BF16)]
+        + [pltpu.VMEM(grad.shape, grad.dtype) for grad in grad_shapes]
+        + [pltpu.SemaphoreType.DMA((3,)), pltpu.SemaphoreType.DMA((4,))],
+        fetched=(1,),
         written=(0, 1, 2, 3),
     )
     return (mixed, grad_tokens, *grads)

time: 138 us -> 136 us (0.986)
  no operation moved by 1% of the time
where the time goes in v8:
time: 136 us; the launch traced here: 135 us
  blocking collectives  60.6 us (45%)
  starting transfers between devices  39.6 us (29%)
  Pallas kernels  17.7 us (13%)
  waiting for transfers between devices  13.6 us (10%)
  other arithmetic  1.41 us (1%)
    all_to_all x4, blocking collectives, exchange(): lax.all_to_all(values, axis, 0, 0, tiled=True, axis_index_groups=groups)  60.6 us
    ppermute x3, starting transfers between devices, pass_on(): return lax.ppermute(values, 'dp', ways)  22.6 us
    pallas_call x8, Pallas kernels, run(): pl.pallas_call(kernel, in_specs=in_specs, out_specs=out_specs, out_shape=...  17.7 us
    ppermute x3, waiting for transfers between devices, pass_on(): return lax.ppermute(values, 'dp', ways)  9.64 us
    ppermute x1, starting transfers between devices, per_device(): lax.ppermute(acts, 'dp', [(source, source ^ 1) for source in range(n_dp)])  9.63 us
    all_to_all x1, starting transfers between devices, exchange(): lax.all_to_all(values, axis, 0, 0, tiled=True, axis_index_groups=groups)  7.38 us
    all_to_all x1, waiting for transfers between devices, exchange(): lax.all_to_all(values, axis, 0, 0, tiled=True, axis_index_groups=groups)  3.96 us
  transfers between devices with their start and end apart: 5, of which 4 were waited for; matrix products, arithmetic and copies ran while one was open for 1% of the time, Pallas kernels for 4%

profile of v8, /device:TPU:1, one launch (start us, length us, event | category | flops | bytes accessed | tf_op | source)
XLA Modules:
  0.0 134.6 jit_solution(3855911387183689705)
XLA Ops:
  0.6 3.7 %shard_map.136 = bf16[128,4736]{1,0:T(8,128)(2,1)} custom-call(bf16[128,384]{1,0:T(8,128)(2,1)} %tokens.1, f32[384]{0:T(512)} %ln_gain.1, bf16[3,384,384]{2,1,0:T(8,128)(2,1)} %w_qkv_far.1, bf16[384,1536]{1,0:T(8,128)(2,1)} %w_hidden_far.1, bf16[128,384]{1,0:T(8,128)(2,1)} %cotangent.1, bf16[384,384]{1,0:T(8,128)(2,1)} %w_attn_far.1, bf16[1536,384]{1,0:T(8,128)(2,1)} %w_mlp_far.1), custom_call_target="tpu_custom_call" | custom-call | tf_op jit(solution)/shard_map/pallas_call | solution.py:123
  4.4 16.0 %all_to_all.51 = bf16[4,32,4736]{2,1,0:T(8,128)(2,1)S(1)} all-to-all(bf16[4,32,4736]{2,1,0:T(8,128)(2,1)} %bitcast.18), channel_id=1, replica_groups={{0,1,2,3},{4,5,6,7},{8,9,10,11},{12,13,14,15},{16,17,18,19},{20,21,22,2..., dimensions={0} | all-to-all | bytes 2424832 | tf_op jit(solution)/shard_map/all_to_all | solution.py:531
  20.3 0.4 shard_map.137
  20.7 20.6 %all_to_all.52 = bf16[4,8,4992]{2,1,0:T(8,128)(2,1)S(1)} all-to-all(bf16[4,8,4992]{2,1,0:T(8,128)(2,1)S(1)} %bitcast.15), channel_id=1, replica_groups={{0,4,8,12},{1,5,9,13},{2,6,10,14},{3,7,11,15},{16,20,24,28},{17,21,25,2..., dimensions={0} | all-to-all | bytes 638976 | tf_op jit(solution)/shard_map/all_to_all | solution.py:531
  41.4 0.3 shard_map.138
  41.7 11.5 %all_to_all.53 = bf16[4,8,4736]{2,1,0:T(8,128)(2,1)S(1)} all-to-all(bf16[4,8,4736]{2,1,0:T(8,128)(2,1)S(1)} %bitcast.17), channel_id=1, replica_groups={{0,4,8,12},{1,5,9,13},{2,6,10,14},{3,7,11,15},{16,20,24,28},{17,21,25,2..., dimensions={0} | all-to-all | bytes 606208 | tf_op jit(solution)/shard_map/all_to_all | solution.py:531
  53.1 0.1 broadcast_in_dim.9
  53.2 0.0 copy-start.1
  53.2 0.0 copy-start.2
  53.2 0.0 copy-start.4
  53.3 0.0 copy-start.5
  53.3 0.0 copy-start.6
  53.3 12.5 %all_to_all.54 = bf16[4,32,4736]{2,1,0:T(8,128)(2,1)S(1)} all-to-all(bf16[4,32,4736]{2,1,0:T(8,128)(2,1)S(1)} %broadcast_in_dim.9), channel_id=1, replica_groups={{0,1,2,3},{4,5,6,7},{8,9,10,11},{12,13,14,15},{16,17,18,19},{20,21,22,2..., dimensions={0} | all-to-all | bytes 2424832 | tf_op jit(solution)/shard_map/all_to_all | solution.py:531
  65.8 0.0 copy-done.5
  65.8 2.4 %shard_map.139.acts_far.refs_1_ = bf16[128,5504]{1,0:T(8,128)(2,1)S(1)} custom-call(bf16[128,4736]{1,0:T(8,128)(2,1)S(1)} %bitcast.11, f32[8,384]{1,0:T(8,128)S(1)} %get-tuple-element.23.refs_1_, bf16[128,384]{1,0:T(8,128)(2,1)S(1)} %copy-done.1, f32[384]{0:T(512)S(1)} %copy-done.4, f32[128]{0:T(128)S(1)} %copy-done.5, f32[128]{0:T(128)S(1)} %copy-done.6, ...), custom_call_target="tpu_custom_call" | custom-call | tf_op jit(solution)/shard_map/pallas_call | solution.py:123
  68.2 9.6 %collective-permute-start = (bf16[128,5504]{1,0:T(8,128)(2,1)S(1)}, bf16[128,5504]{1,0:T(8,128)(2,1)}, u32[]{:S(2)}, u32[]{:S(2)}) collective-permute-start(bf16[128,5504]{1,0:T(8,128)(2,1)S(1)} %shard_map.139.acts_far.refs_1_), channel_id=1, source_target_pairs={{0,128},{128,0},{256,384},{384,256},{512,640},{640,512},{768,896},... | collective-permute-start | bytes 4227080 | tf_op jit(solution)/shard_map/ppermute | solution.py:590
  77.9 4.1 %shard_map.140 = bf16[128,896]{1,0:T(8,128)(2,1)} custom-call(bf16[128,5504]{1,0:T(8,128)(2,1)} %copy-done, bf16[1536,384]{1,0:T(8,128)(2,1)} %w_mlp_far.1, bf16[384,1536]{1,0:T(8,128)(2,1)} %w_hidden_far.1, bf16[384,384]{1,0:T(8,128)(2,1)} %w_attn_far.1, bf16[3,384,384]{2,1,0:T(8,128)(2,1)} %w_qkv_far.1), custom_call_target="tpu_custom_call" | custom-call | tf_op jit(solution)/shard_map/pallas_call | solution.py:123
  82.1 0.0 collective-permute-done.refs_2_
  82.1 3.6 %shard_map.141 = (f32[576,384]{1,0:T(8,128)}, bf16[576,384]{1,0:T(8,128)(2,1)}, bf16[576,384]{1,0:T(8,128)(2,1)}, bf16[576,384]{1,0:T(8,128)(2,1)}) custom-call(s32[1]{0:T(128)} %bitcast.1.refs_0_, bf16[128,5504]{1,0:T(8,128)(2,1)} %copy-done, bf16[128,5504]{1,0:T(8,128)(2,1)} %collective-permute-done.refs_2_), custom_call_target="tpu_custom_call" | custom-call | tf_op jit(solution)/shard_map/pallas_call | solution.py:123
  85.6 16.1 %collective-permute-start.1 = (bf16[576,384]{1,0:T(8,128)(2,1)}, bf16[576,384]{1,0:T(8,128)(2,1)S(1)}, u32[]{:S(2)}, u32[]{:S(2)}) collective-permute-start(bf16[576,384]{1,0:T(8,128)(2,1)} %get-tuple-element.26), channel_id=1, source_target_pairs={{0,256},{128,896},{256,512},{384,128},{512,768},{640,384},{768,0},... | collective-permute-start | bytes 1327112 | tf_op jit(solution)/shard_map/ppermute | solution.py:629
  101.8 7.4 %all-to-all-start.4 = ((bf16[8,16,896]{2,1,0:T(8,128)(2,1)}), bf16[8,16,896]{2,1,0:T(8,128)(2,1)S(1)}, u32[]{:S(2)}, u32[]{:S(2)}) async-start(bf16[8,16,896]{2,1,0:T(8,128)(2,1)} %bitcast.9), calls=%async_computation.4 | async-start | bytes 458752 | tf_op jit(solution)/shard_map/all_to_all | solution.py:531
  109.2 1.9 %collective-permute-start.3 = (bf16[576,384]{1,0:T(8,128)(2,1)}, bf16[576,384]{1,0:T(8,128)(2,1)S(1)}, u32[]{:S(2)}, u32[]{:S(2)}) collective-permute-start(bf16[576,384]{1,0:T(8,128)(2,1)} %get-tuple-element.33), channel_id=1, source_target_pairs={{0,768},{128,384},{256,0},{384,640},{512,256},{640,896},{768,512},... | collective-permute-start | bytes 1327112 | tf_op jit(solution)/shard_map/ppermute | solution.py:629
  111.1 1.0 collective-permute-done.1
  112.1 0.8 copy-done.7
  112.8 1.3 add_convert_fusion
  114.2 4.0 %all-to-all-done.4 = bf16[8,16,896]{2,1,0:T(8,128)(2,1)S(1)} async-done(((bf16[8,16,896]{2,1,0:T(8,128)(2,1)}), bf16[8,16,896]{2,1,0:T(8,128)(2,1)S(1)}, u32[]{:S(2)}, u32[]{:S(2)}) %all-to-all-start.4) | async-done | bytes 229408 | tf_op jit(solution)/shard_map/all_to_all | solution.py:531
  118.1 4.6 %collective-permute-start.2 = (bf16[576,384]{1,0:T(8,128)(2,1)S(1)}, bf16[576,384]{1,0:T(8,128)(2,1)}, u32[]{:S(2)}, u32[]{:S(2)}) collective-permute-start(bf16[576,384]{1,0:T(8,128)(2,1)S(1)} %add_convert_fusion), channel_id=1, source_target_pairs={{0,256},{128,896},{256,512},{384,128},{512,768},{640,384},{768,0},... | collective-permute-start | bytes 1327112 | tf_op jit(solution)/shard_map/ppermute | solution.py:629
  122.7 0.1 pad_add_fusion.place
  122.8 1.2 shard_map.142
  124.0 2.3 %collective-permute-done.3.direct = bf16[576,384]{1,0:T(8,128)(2,1)S(1)} collective-permute-done((bf16[576,384]{1,0:T(8,128)(2,1)}, bf16[576,384]{1,0:T(8,128)(2,1)S(1)}, u32[]{:S(2)}, u32[]{:S(2)}) %collective-permute-start.3) | collective-permute-done | bytes 442400 | tf_op jit(solution)/shard_map/ppermute | solution.py:629
  126.3 6.4 %collective-permute-done.2.relayed_far = bf16[576,384]{1,0:T(8,128)(2,1)} collective-permute-done((bf16[576,384]{1,0:T(8,128)(2,1)S(1)}, bf16[576,384]{1,0:T(8,128)(2,1)}, u32[]{:S(2)}, u32[]{:S(2)}) %collective-permute-start.2) | collective-permute-done | bytes 442400 | tf_op jit(solution)/shard_map/ppermute | solution.py:629
  132.7 1.9 %shard_map.143 = (f32[3,1,48,384]{3,2,1,0:T(8,128)}, f32[1,48,1536]{2,1,0:T(8,128)}, f32[1,48,384]{2,1,0:T(8,128)}, f32[1,192,384]{2,1,0:T(8,128)}) custom-call(f32[576,384]{1,0:T(8,128)S(1)} %copy-done.3, bf16[576,384]{1,0:T(8,128)(2,1)} %collective-permute-done.2.relayed_far, bf16[576,384]{1,0:T(8,128)(2,1)S(1)} %collective-permute-done.3.direct), custom_call_target="tpu_custom_call" | custom-call | tf_op jit(solution)/shard_map/pallas_call | solution.py:123
  (9 shorter events, 0.0 us)
Async XLA Ops:
  53.2 12.5 %copy-start.1 = (bf16[128,384]{1,0:T(8,128)(2,1)S(1)}, bf16[128,384]{1,0:T(8,128)(2,1)}, u32[]{:S(2)}) copy-start(bf16[128,384]{1,0:T(8,128)(2,1)} %tokens.1) | copy-start | bytes 294916
  53.2 12.5 %copy-start.2 = (bf16[128,384]{1,0:T(8,128)(2,1)S(1)}, bf16[128,384]{1,0:T(8,128)(2,1)}, u32[]{:S(2)}) copy-start(bf16[128,384]{1,0:T(8,128)(2,1)} %cotangent.1) | copy-start | bytes 294916
  53.2 12.5 %copy-start.4 = (f32[384]{0:T(512)S(1)}, f32[384]{0:T(512)}, u32[]{:S(2)}) copy-start(f32[384]{0:T(512)} %ln_gain.1) | copy-start | bytes 4612
  53.3 12.5 %copy-start.5 = (f32[128]{0:T(128)S(1)}, f32[128]{0:T(128)}, u32[]{:S(2)}) copy-start(f32[128]{0:T(128)} %refs_4_.3) | copy-start | bytes 1540
  53.3 12.5 %copy-start.6 = (f32[128]{0:T(128)S(1)}, f32[128]{0:T(128)}, u32[]{:S(2)}) copy-start(f32[128]{0:T(128)} %refs_5_.3) | copy-start | bytes 1540
  68.2 9.7 %copy-start = (bf16[128,5504]{1,0:T(8,128)(2,1)}, bf16[128,5504]{1,0:T(8,128)(2,1)S(1)}, u32[]{:S(2)}) copy-start(bf16[128,5504]{1,0:T(8,128)(2,1)S(1)} %shard_map.139.acts_far.refs_1_) | copy-start | bytes 4227076
  68.2 13.8 %collective-permute-start = (bf16[128,5504]{1,0:T(8,128)(2,1)S(1)}, bf16[128,5504]{1,0:T(8,128)(2,1)}, u32[]{:S(2)}, u32[]{:S(2)}) collective-permute-start(bf16[128,5504]{1,0:T(8,128)(2,1)S(1)} %shard_map.139.acts_far.refs_1_), channel_id=1, source_target_pairs={{0,128},{128,0},{256,384},{384,256},{512,640},{640,512},{768,896},... | collective-permute-start | bytes 4227080 | tf_op jit(solution)/shard_map/ppermute | solution.py:590
  85.6 26.4 %collective-permute-start.1 = (bf16[576,384]{1,0:T(8,128)(2,1)}, bf16[576,384]{1,0:T(8,128)(2,1)S(1)}, u32[]{:S(2)}, u32[]{:S(2)}) collective-permute-start(bf16[576,384]{1,0:T(8,128)(2,1)} %get-tuple-element.26), channel_id=1, source_target_pairs={{0,256},{128,896},{256,512},{384,128},{512,768},{640,384},{768,0},... | collective-permute-start | bytes 1327112 | tf_op jit(solution)/shard_map/ppermute | solution.py:629
  101.8 16.4 %all-to-all-start.4 = ((bf16[8,16,896]{2,1,0:T(8,128)(2,1)}), bf16[8,16,896]{2,1,0:T(8,128)(2,1)S(1)}, u32[]{:S(2)}, u32[]{:S(2)}) async-start(bf16[8,16,896]{2,1,0:T(8,128)(2,1)} %bitcast.9), calls=%async_computation.4 | async-start | bytes 458752 | tf_op jit(solution)/shard_map/all_to_all | solution.py:531
  109.2 17.1 %collective-permute-start.3 = (bf16[576,384]{1,0:T(8,128)(2,1)}, bf16[576,384]{1,0:T(8,128)(2,1)S(1)}, u32[]{:S(2)}, u32[]{:S(2)}) collective-permute-start(bf16[576,384]{1,0:T(8,128)(2,1)} %get-tuple-element.33), channel_id=1, source_target_pairs={{0,768},{128,384},{256,0},{384,640},{512,256},{640,896},{768,512},... | collective-permute-start | bytes 1327112 | tf_op jit(solution)/shard_map/ppermute | solution.py:629
  112.1 0.8 copy-start.7
  112.8 19.8 %copy-start.3 = (f32[576,384]{1,0:T(8,128)S(1)}, f32[576,384]{1,0:T(8,128)}, u32[]{:S(2)}) copy-start(f32[576,384]{1,0:T(8,128)} %get-tuple-element.31.here) | copy-start | bytes 2654212
  118.1 14.5 %collective-permute-start.2 = (bf16[576,384]{1,0:T(8,128)(2,1)S(1)}, bf16[576,384]{1,0:T(8,128)(2,1)}, u32[]{:S(2)}, u32[]{:S(2)}) collective-permute-start(bf16[576,384]{1,0:T(8,128)(2,1)S(1)} %add_convert_fusion), channel_id=1, source_target_pairs={{0,256},{128,896},{256,512},{384,128},{512,768},{640,384},{768,0},... | collective-permute-start | bytes 1327112 | tf_op jit(solution)/shard_map/ppermute | solution.py:629

commit v9 on v8

--- a/solution.py
+++ b/solution.py
@@ -290,44 +290,52 @@
         centred = centred - hat * jnp.mean(grad * hat, axis=1, keepdims=True)
         return (root * centred).astype(BF16)
 
-    for head in range(head_width // head_size):
-        low, high = head * head_size, (head + 1) * head_size
-        query = full[:, low:high].astype(F32)
-        key = full[:, head_width + low : head_width + high].astype(F32)
-        value_low = full[:, 2 * head_width + low : 2 * head_width + high]
-        grad_mix = full[:, 3 * head_width + low : 3 * head_width + high]
-        query_hat, query_root = normalise(query)
-        key_hat, key_root = normalise(key)
-        query_norm = (query_hat * query_row).astype(BF16)
-        key_norm = (key_hat * key_row).astype(BF16)
-        scores = dot_last(query_norm, key_norm) * scale
-        weights = jnp.exp(scores - jnp.max(scores, axis=1, keepdims=True))
-        probs = weights / jnp.sum(weights, axis=1, keepdims=True)
-        probs_low = probs.astype(BF16)
-        acts[:, acts_heads + low : acts_heads + high] = dot_plain(probs_low, value_low).astype(BF16)
-        grad_probs = dot_last(grad_mix, value_low)
-        grad_value = dot_first(probs_low, grad_mix).astype(BF16)
-        grad_scores = probs * (grad_probs - jnp.sum(grad_probs * probs, axis=1, keepdims=True))
-        grad_scores = grad_scores.astype(BF16)
-        grad_query = back(
-            dot_plain(grad_scores, key_norm) * scale, query_hat, query_root, query_row
-        )
-        grad_key = back(
-            dot_first(grad_scores, query_norm) * scale, key_hat, key_root, key_row
-        )
-        plain = jnp.zeros_like(query)
-        with_hat = jnp.zeros_like(query)
-        for part, (grad, pre) in enumerate(
-            ((grad_query, query), (grad_key, key), (grad_value, value_low.astype(F32)))
+    heads = [
+        (head * head_size, (head + 1) * head_size) for head in range(head_width // head_size)
+    ]
+
+    def of(part):
+        return [full[:, part * head_width + low : part * head_width + high] for low, high in heads]
+
+    queries, keys = [x.astype(F32) for x in of(0)], [x.astype(F32) for x in of(1)]
+    values, grad_mixes = of(2), of(3)
+    query_hats, query_roots = zip(*map(normalise, queries))
+    key_hats, key_roots = zip(*map(normalise, keys))
+    query_norms = [(hat * query_row).astype(BF16) for hat in query_hats]
+    key_norms = [(hat * key_row).astype(BF16) for hat in key_hats]
+    scores = [dot_last(query, key) * scale for query, key in zip(query_norms, key_norms)]
+    grad_probs = [dot_last(grad, value) for grad, value in zip(grad_mixes, values)]
+    raised = [jnp.exp(score - jnp.max(score, axis=1, keepdims=True)) for score in scores]
+    probs = [value / jnp.sum(value, axis=1, keepdims=True) for value in raised]
+    probs_low = [prob.astype(BF16) for prob in probs]
+    mixes = [dot_plain(prob, value).astype(BF16) for prob, value in zip(probs_low, values)]
+    grad_values = [dot_first(prob, grad).astype(BF16) for prob, grad in zip(probs_low, grad_mixes)]
+    grad_scores = [
+        (prob * (grad - jnp.sum(grad * prob, axis=1, keepdims=True))).astype(BF16)
+        for prob, grad in zip(probs, grad_probs)
+    ]
+    grad_queries = [
+        back(dot_plain(grad, key) * scale, hat, root, query_row)
+        for grad, key, hat, root in zip(grad_scores, key_norms, query_hats, query_roots)
+    ]
+    grad_keys = [
+        back(dot_first(grad, query) * scale, hat, root, key_row)
+        for grad, query, hat, root in zip(grad_scores, query_norms, key_hats, key_roots)
+    ]
+    plain = jnp.zeros_like(queries[0])
+    with_hat = jnp.zeros_like(queries[0])
+    for index, (low, high) in enumerate(heads):
+        acts[:, acts_heads + low : acts_heads + high] = mixes[index]
+        for part, (grads, pres) in enumerate(
+            ((grad_queries, queries), (grad_keys, keys), (grad_values, values))
         ):
             start = acts_heads + (1 + part) * head_width
-            acts[:, start + low : start + high] = grad
-            grad = grad.astype(F32)
+            acts[:, start + low : start + high] = grads[index]
+            grad = grads[index].astype(F32)
             plain = plain + grad * gain_sums[part : part + 1, low:high]
-            with_hat = with_hat + grad * pre
-        plain_sum = plain_sum + jnp.sum(plain, axis=1, keepdims=True)
-        hat_sum = hat_sum + jnp.sum(with_hat, axis=1, keepdims=True)
-
+            with_hat = with_hat + grad * pres[index].astype(F32)
+    plain_sum = plain_sum + jnp.sum(plain, axis=1, keepdims=True)
+    hat_sum = hat_sum + jnp.sum(with_hat, axis=1, keepdims=True)
     acts[:, acts_heads + 4 * head_width :] = to_lanes(pieces(plain_sum, 2) + pieces(hat_sum, 2)).astype(BF16)
 
 
@@ -349,27 +357,30 @@
     def load_acts(start, length):
         load(acts_far.at[:, pl.ds(start, length)], acts.at[:, pl.ds(start, length)])
 
+    load_acts(heads_at, 4 * head_width + LANES)
+    load(w_attn_far, w_attn)
+    load(w_qkv_far, w_qkv)
     load_acts(hidden_at, hidden_width)
     load(w_mlp_far, w_mlp)
     load_acts(hidden_at + hidden_width, hidden_width)
     load(w_hidden_far, w_hidden)
-    load_acts(heads_at, 4 * head_width + LANES)
-    load(w_attn_far, w_attn)
-    load(w_qkv_far, w_qkv)
-
-    loads[0].wait()
-    loads[1].wait()
-    mixed = dot_plain(acts[:, hidden_at : hidden_at + hidden_width], w_mlp[...])
-    loads[2].wait()
-    loads[3].wait()
-    grad_normed = dot_last(acts[:, hidden_at + hidden_width : heads_at], w_hidden[...])
-    for copy in loads[4:]:
-        copy.wait()
-    mixed = mixed + dot_plain(acts[:, heads_at : heads_at + head_width], w_attn[...])
-    terms[:, :local_width] = mixed.astype(BF16)
+
+    def ready(*which):
+        for index in which:
+            loads[index].wait()
+
+    ready(0, 1)
+    mixed = dot_plain(acts[:, heads_at : heads_at + head_width], w_attn[...])
+    ready(2)
+    grad_normed = jnp.zeros(mixed.shape, F32)
     for part in range(3):
         start = heads_at + (1 + part) * head_width
         grad_normed = grad_normed + dot_last(acts[:, start : start + head_width], w_qkv[part])
+    ready(3, 4)
+    mixed = mixed + dot_plain(acts[:, hidden_at : hidden_at + hidden_width], w_mlp[...])
+    terms[:, :local_width] = mixed.astype(BF16)
+    ready(5, 6)
+    grad_normed = grad_normed + dot_last(acts[:, hidden_at + hidden_width : heads_at], w_hidden[...])
     terms[:, local_width : 2 * local_width] = grad_normed.astype(BF16)
     terms[:, 2 * local_width :] = acts[:, heads_at + 4 * head_width :]
 

time: 136 us -> 135 us (level)
  Pallas kernels: 17.7 us -> 16.3 us
    pallas_call x8, Pallas kernels: 17.7 us -> 16.3 us  [run(): pl.pallas_call(kernel, in_specs=in_specs, out_specs=out_specs, out_shape=...]
where the time goes in v9:
time: 135 us; the launch traced here: 133 us
  blocking collectives  60.6 us (45%)
  starting transfers between devices  39.6 us (29%)
  Pallas kernels  16.3 us (12%)
  waiting for transfers between devices  13.6 us (10%)
  other arithmetic  1.41 us (1%)
    all_to_all x4, blocking collectives, exchange(): lax.all_to_all(values, axis, 0, 0, tiled=True, axis_index_groups=groups)  60.6 us
    ppermute x3, starting transfers between devices, pass_on(): return lax.ppermute(values, 'dp', ways)  22.6 us
    pallas_call x8, Pallas kernels, run(): pl.pallas_call(kernel, in_specs=in_specs, out_specs=out_specs, out_shape=...  16.3 us
    ppermute x1, starting transfers between devices, per_device(): lax.ppermute(acts, 'dp', [(source, source ^ 1) for source in range(n_dp)])  9.64 us
    ppermute x3, waiting for transfers between devices, pass_on(): return lax.ppermute(values, 'dp', ways)  9.64 us
    all_to_all x1, starting transfers between devices, exchange(): lax.all_to_all(values, axis, 0, 0, tiled=True, axis_index_groups=groups)  7.38 us
    all_to_all x1, waiting for transfers between devices, exchange(): lax.all_to_all(values, axis, 0, 0, tiled=True, axis_index_groups=groups)  3.97 us
  transfers between devices with their start and end apart: 5, of which 4 were waited for; matrix products, arithmetic and copies ran while one was open for 1% of the time, Pallas kernels for 4%

profile of v9, /device:TPU:1, one launch (start us, length us, event | category | flops | bytes accessed | tf_op | source)
XLA Modules:
  0.0 133.1 jit_solution(3992115223832126237)
XLA Ops:
  0.6 3.7 %shard_map.136 = bf16[128,4736]{1,0:T(8,128)(2,1)} custom-call(bf16[128,384]{1,0:T(8,128)(2,1)} %tokens.1, f32[384]{0:T(512)} %ln_gain.1, bf16[3,384,384]{2,1,0:T(8,128)(2,1)} %w_qkv_far.1, bf16[384,1536]{1,0:T(8,128)(2,1)} %w_hidden_far.1, bf16[128,384]{1,0:T(8,128)(2,1)} %cotangent.1, bf16[384,384]{1,0:T(8,128)(2,1)} %w_attn_far.1, bf16[1536,384]{1,0:T(8,128)(2,1)} %w_mlp_far.1), custom_call_target="tpu_custom_call" | custom-call | tf_op jit(solution)/shard_map/pallas_call | solution.py:123
  4.4 16.0 %all_to_all.51 = bf16[4,32,4736]{2,1,0:T(8,128)(2,1)S(1)} all-to-all(bf16[4,32,4736]{2,1,0:T(8,128)(2,1)} %bitcast.18), channel_id=1, replica_groups={{0,1,2,3},{4,5,6,7},{8,9,10,11},{12,13,14,15},{16,17,18,19},{20,21,22,2..., dimensions={0} | all-to-all | bytes 2424832 | tf_op jit(solution)/shard_map/all_to_all | solution.py:542
  20.3 0.4 shard_map.137
  20.7 20.6 %all_to_all.52 = bf16[4,8,4992]{2,1,0:T(8,128)(2,1)S(1)} all-to-all(bf16[4,8,4992]{2,1,0:T(8,128)(2,1)S(1)} %bitcast.15), channel_id=1, replica_groups={{0,4,8,12},{1,5,9,13},{2,6,10,14},{3,7,11,15},{16,20,24,28},{17,21,25,2..., dimensions={0} | all-to-all | bytes 638976 | tf_op jit(solution)/shard_map/all_to_all | solution.py:542
  41.4 0.3 shard_map.138
  41.7 11.5 %all_to_all.53 = bf16[4,8,4736]{2,1,0:T(8,128)(2,1)S(1)} all-to-all(bf16[4,8,4736]{2,1,0:T(8,128)(2,1)S(1)} %bitcast.17), channel_id=1, replica_groups={{0,4,8,12},{1,5,9,13},{2,6,10,14},{3,7,11,15},{16,20,24,28},{17,21,25,2..., dimensions={0} | all-to-all | bytes 606208 | tf_op jit(solution)/shard_map/all_to_all | solution.py:542
  53.1 0.1 broadcast_in_dim.9
  53.2 0.0 copy-start.1
  53.2 0.0 copy-start.2
  53.2 0.0 copy-start.4
  53.3 0.0 copy-start.5
  53.3 0.0 copy-start.6
  53.3 12.5 %all_to_all.54 = bf16[4,32,4736]{2,1,0:T(8,128)(2,1)S(1)} all-to-all(bf16[4,32,4736]{2,1,0:T(8,128)(2,1)S(1)} %broadcast_in_dim.9), channel_id=1, replica_groups={{0,1,2,3},{4,5,6,7},{8,9,10,11},{12,13,14,15},{16,17,18,19},{20,21,22,2..., dimensions={0} | all-to-all | bytes 2424832 | tf_op jit(solution)/shard_map/all_to_all | solution.py:542
  65.8 0.0 copy-done.2
  65.8 1.4 %shard_map.139.acts_far.refs_1_ = bf16[128,5504]{1,0:T(8,128)(2,1)S(1)} custom-call(bf16[128,4736]{1,0:T(8,128)(2,1)S(1)} %bitcast.11, f32[8,384]{1,0:T(8,128)S(1)} %get-tuple-element.23.refs_1_, bf16[128,384]{1,0:T(8,128)(2,1)S(1)} %copy-done.1, f32[384]{0:T(512)S(1)} %copy-done.4, f32[128]{0:T(128)S(1)} %copy-done.5, f32[128]{0:T(128)S(1)} %copy-done.6, ...), custom_call_target="tpu_custom_call" | custom-call | tf_op jit(solution)/shard_map/pallas_call | solution.py:123
  67.2 9.6 %collective-permute-start = (bf16[128,5504]{1,0:T(8,128)(2,1)S(1)}, bf16[128,5504]{1,0:T(8,128)(2,1)}, u32[]{:S(2)}, u32[]{:S(2)}) collective-permute-start(bf16[128,5504]{1,0:T(8,128)(2,1)S(1)} %shard_map.139.acts_far.refs_1_), channel_id=1, source_target_pairs={{0,128},{128,0},{256,384},{384,256},{512,640},{640,512},{768,896},... | collective-permute-start | bytes 4227080 | tf_op jit(solution)/shard_map/ppermute | solution.py:601
  76.9 3.7 %shard_map.140 = bf16[128,896]{1,0:T(8,128)(2,1)} custom-call(bf16[128,5504]{1,0:T(8,128)(2,1)} %copy-done, bf16[1536,384]{1,0:T(8,128)(2,1)} %w_mlp_far.1, bf16[384,1536]{1,0:T(8,128)(2,1)} %w_hidden_far.1, bf16[384,384]{1,0:T(8,128)(2,1)} %w_attn_far.1, bf16[3,384,384]{2,1,0:T(8,128)(2,1)} %w_qkv_far.1), custom_call_target="tpu_custom_call" | custom-call | tf_op jit(solution)/shard_map/pallas_call | solution.py:123
  80.6 0.0 collective-permute-done.refs_2_
  80.6 3.6 %shard_map.141 = (f32[576,384]{1,0:T(8,128)}, bf16[576,384]{1,0:T(8,128)(2,1)}, bf16[576,384]{1,0:T(8,128)(2,1)}, bf16[576,384]{1,0:T(8,128)(2,1)}) custom-call(s32[1]{0:T(128)} %bitcast.1.refs_0_, bf16[128,5504]{1,0:T(8,128)(2,1)} %copy-done, bf16[128,5504]{1,0:T(8,128)(2,1)} %collective-permute-done.refs_2_), custom_call_target="tpu_custom_call" | custom-call | tf_op jit(solution)/shard_map/pallas_call | solution.py:123
  84.2 16.1 %collective-permute-start.1 = (bf16[576,384]{1,0:T(8,128)(2,1)}, bf16[576,384]{1,0:T(8,128)(2,1)S(1)}, u32[]{:S(2)}, u32[]{:S(2)}) collective-permute-start(bf16[576,384]{1,0:T(8,128)(2,1)} %get-tuple-element.26), channel_id=1, source_target_pairs={{0,256},{128,896},{256,512},{384,128},{512,768},{640,384},{768,0},... | collective-permute-start | bytes 1327112 | tf_op jit(solution)/shard_map/ppermute | solution.py:640
  100.3 7.4 %all-to-all-start.4 = ((bf16[8,16,896]{2,1,0:T(8,128)(2,1)}), bf16[8,16,896]{2,1,0:T(8,128)(2,1)S(1)}, u32[]{:S(2)}, u32[]{:S(2)}) async-start(bf16[8,16,896]{2,1,0:T(8,128)(2,1)} %bitcast.9), calls=%async_computation.4 | async-start | bytes 458752 | tf_op jit(solution)/shard_map/all_to_all | solution.py:542
  107.7 1.9 %collective-permute-start.3 = (bf16[576,384]{1,0:T(8,128)(2,1)}, bf16[576,384]{1,0:T(8,128)(2,1)S(1)}, u32[]{:S(2)}, u32[]{:S(2)}) collective-permute-start(bf16[576,384]{1,0:T(8,128)(2,1)} %get-tuple-element.33), channel_id=1, source_target_pairs={{0,768},{128,384},{256,0},{384,640},{512,256},{640,896},{768,512},... | collective-permute-start | bytes 1327112 | tf_op jit(solution)/shard_map/ppermute | solution.py:640
  109.6 1.0 collective-permute-done.1
  110.6 0.8 copy-done.7
  111.4 1.3 %add_convert_fusion = bf16[576,384]{1,0:T(8,128)(2,1)S(1)} fusion(bf16[576,384]{1,0:T(8,128)(2,1)} %copy-done.7, bf16[576,384]{1,0:T(8,128)(2,1)} %get-tuple-element.25), kind=kLoop, calls=%fused_computation | loop fusion | flops 884736 | bytes 1327104 | tf_op jit(solution)/shard_map/convert_element_type | solution.py:644
  112.7 4.0 %all-to-all-done.4 = bf16[8,16,896]{2,1,0:T(8,128)(2,1)S(1)} async-done(((bf16[8,16,896]{2,1,0:T(8,128)(2,1)}), bf16[8,16,896]{2,1,0:T(8,128)(2,1)S(1)}, u32[]{:S(2)}, u32[]{:S(2)}) %all-to-all-start.4) | async-done | bytes 229408 | tf_op jit(solution)/shard_map/all_to_all | solution.py:542
  116.7 4.6 %collective-permute-start.2 = (bf16[576,384]{1,0:T(8,128)(2,1)S(1)}, bf16[576,384]{1,0:T(8,128)(2,1)}, u32[]{:S(2)}, u32[]{:S(2)}) collective-permute-start(bf16[576,384]{1,0:T(8,128)(2,1)S(1)} %add_convert_fusion), channel_id=1, source_target_pairs={{0,256},{128,896},{256,512},{384,128},{512,768},{640,384},{768,0},... | collective-permute-start | bytes 1327112 | tf_op jit(solution)/shard_map/ppermute | solution.py:640
  121.3 0.1 pad_add_fusion.place
  121.3 1.2 shard_map.142
  122.6 2.2 %collective-permute-done.3.direct = bf16[576,384]{1,0:T(8,128)(2,1)S(1)} collective-permute-done((bf16[576,384]{1,0:T(8,128)(2,1)}, bf16[576,384]{1,0:T(8,128)(2,1)S(1)}, u32[]{:S(2)}, u32[]{:S(2)}) %collective-permute-start.3) | collective-permute-done | bytes 442400 | tf_op jit(solution)/shard_map/ppermute | solution.py:640
  124.8 6.4 %collective-permute-done.2.relayed_far = bf16[576,384]{1,0:T(8,128)(2,1)} collective-permute-done((bf16[576,384]{1,0:T(8,128)(2,1)S(1)}, bf16[576,384]{1,0:T(8,128)(2,1)}, u32[]{:S(2)}, u32[]{:S(2)}) %collective-permute-start.2) | collective-permute-done | bytes 442400 | tf_op jit(solution)/shard_map/ppermute | solution.py:640
  131.2 1.9 %shard_map.143 = (f32[3,1,48,384]{3,2,1,0:T(8,128)}, f32[1,48,1536]{2,1,0:T(8,128)}, f32[1,48,384]{2,1,0:T(8,128)}, f32[1,192,384]{2,1,0:T(8,128)}) custom-call(f32[576,384]{1,0:T(8,128)S(1)} %copy-done.3, bf16[576,384]{1,0:T(8,128)(2,1)} %collective-permute-done.2.relayed_far, bf16[576,384]{1,0:T(8,128)(2,1)S(1)} %collective-permute-done.3.direct), custom_call_target="tpu_custom_call" | custom-call | tf_op jit(solution)/shard_map/pallas_call | solution.py:123
  (9 shorter events, 0.0 us)
Async XLA Ops:
  53.2 12.5 %copy-start.1 = (bf16[128,384]{1,0:T(8,128)(2,1)S(1)}, bf16[128,384]{1,0:T(8,128)(2,1)}, u32[]{:S(2)}) copy-start(bf16[128,384]{1,0:T(8,128)(2,1)} %tokens.1) | copy-start | bytes 294916
  53.2 12.5 %copy-start.2 = (bf16[128,384]{1,0:T(8,128)(2,1)S(1)}, bf16[128,384]{1,0:T(8,128)(2,1)}, u32[]{:S(2)}) copy-start(bf16[128,384]{1,0:T(8,128)(2,1)} %cotangent.1) | copy-start | bytes 294916
  53.2 12.5 %copy-start.4 = (f32[384]{0:T(512)S(1)}, f32[384]{0:T(512)}, u32[]{:S(2)}) copy-start(f32[384]{0:T(512)} %ln_gain.1) | copy-start | bytes 4612
  53.3 12.5 %copy-start.5 = (f32[128]{0:T(128)S(1)}, f32[128]{0:T(128)}, u32[]{:S(2)}) copy-start(f32[128]{0:T(128)} %refs_4_.3) | copy-start | bytes 1540
  53.3 12.5 %copy-start.6 = (f32[128]{0:T(128)S(1)}, f32[128]{0:T(128)}, u32[]{:S(2)}) copy-start(f32[128]{0:T(128)} %refs_5_.3) | copy-start | bytes 1540
  67.2 9.7 %copy-start = (bf16[128,5504]{1,0:T(8,128)(2,1)}, bf16[128,5504]{1,0:T(8,128)(2,1)S(1)}, u32[]{:S(2)}) copy-start(bf16[128,5504]{1,0:T(8,128)(2,1)S(1)} %shard_map.139.acts_far.refs_1_) | copy-start | bytes 4227076
  67.2 13.4 %collective-permute-start = (bf16[128,5504]{1,0:T(8,128)(2,1)S(1)}, bf16[128,5504]{1,0:T(8,128)(2,1)}, u32[]{:S(2)}, u32[]{:S(2)}) collective-permute-start(bf16[128,5504]{1,0:T(8,128)(2,1)S(1)} %shard_map.139.acts_far.refs_1_), channel_id=1, source_target_pairs={{0,128},{128,0},{256,384},{384,256},{512,640},{640,512},{768,896},... | collective-permute-start | bytes 4227080 | tf_op jit(solution)/shard_map/ppermute | solution.py:601
  84.2 26.4 %collective-permute-start.1 = (bf16[576,384]{1,0:T(8,128)(2,1)}, bf16[576,384]{1,0:T(8,128)(2,1)S(1)}, u32[]{:S(2)}, u32[]{:S(2)}) collective-permute-start(bf16[576,384]{1,0:T(8,128)(2,1)} %get-tuple-element.26), channel_id=1, source_target_pairs={{0,256},{128,896},{256,512},{384,128},{512,768},{640,384},{768,0},... | collective-permute-start | bytes 1327112 | tf_op jit(solution)/shard_map/ppermute | solution.py:640
  100.3 16.4 %all-to-all-start.4 = ((bf16[8,16,896]{2,1,0:T(8,128)(2,1)}), bf16[8,16,896]{2,1,0:T(8,128)(2,1)S(1)}, u32[]{:S(2)}, u32[]{:S(2)}) async-start(bf16[8,16,896]{2,1,0:T(8,128)(2,1)} %bitcast.9), calls=%async_computation.4 | async-start | bytes 458752 | tf_op jit(solution)/shard_map/all_to_all | solution.py:542
  107.7 17.1 %collective-permute-start.3 = (bf16[576,384]{1,0:T(8,128)(2,1)}, bf16[576,384]{1,0:T(8,128)(2,1)S(1)}, u32[]{:S(2)}, u32[]{:S(2)}) collective-permute-start(bf16[576,384]{1,0:T(8,128)(2,1)} %get-tuple-element.33), channel_id=1, source_target_pairs={{0,768},{128,384},{256,0},{384,640},{512,256},{640,896},{768,512},... | collective-permute-start | bytes 1327112 | tf_op jit(solution)/shard_map/ppermute | solution.py:640
  110.6 0.8 copy-start.7
  111.4 19.8 %copy-start.3 = (f32[576,384]{1,0:T(8,128)S(1)}, f32[576,384]{1,0:T(8,128)}, u32[]{:S(2)}) copy-start(f32[576,384]{1,0:T(8,128)} %get-tuple-element.31.here) | copy-start | bytes 2654212
  116.7 14.5 %collective-permute-start.2 = (bf16[576,384]{1,0:T(8,128)(2,1)S(1)}, bf16[576,384]{1,0:T(8,128)(2,1)}, u32[]{:S(2)}, u32[]{:S(2)}) collective-permute-start(bf16[576,384]{1,0:T(8,128)(2,1)S(1)} %add_convert_fusion), channel_id=1, source_target_pairs={{0,256},{128,896},{256,512},{384,128},{512,768},{640,384},{768,0},... | collective-permute-start | bytes 1327112 | tf_op jit(solution)/shard_map/ppermute | solution.py:640
